TPU v7x, 256 devices: a whole 4x4x8 slice. The times are simulated.
256 devices in a mesh: seq: 32 (over z_hi, x, core), fsdp: 8 (over z_lo, y).
Axes of the slice: x: 4, y: 4, z: 8 (z_hi: 4, z_lo: 2; z = z_hi * 2 + z_lo), core: 2. Of those that a mesh axis runs over, the one named last changes fastest.
Arguments:
- prompt: bfloat16 [8, 256, 4096], P('fsdp'), may hold values from -6 to 6
- lengths: int32 [8], P('fsdp'), may hold values from 1 to 256, 1152 in all
- timesteps: int32 [8], P('fsdp'), may hold values from 0 to 999
- ref_errors: float32 [8, 2], P('fsdp'), may hold values from 4.2 to 4.45
- gain_ffn: float32 [4096], replicated, may hold values from 0.5 to 1.5
- w_in_gate: bfloat16 [4096, 8192], P('fsdp', 'seq'), may hold values from -0.09375 to 0.09375
- w_in_up: bfloat16 [4096, 8192], P('fsdp', 'seq'), may hold values from -0.09375 to 0.09375
- w_in_down: bfloat16 [8192, 4096], P('seq', 'fsdp'), may hold values from -0.0625 to 0.0625
- gain_final: float32 [4096], replicated, may hold values from 0.5 to 1.5
- w_context: bfloat16 [4096, 4096], P('fsdp', 'seq'), may hold values from -0.09375 to 0.09375
- image_q: bfloat16 [8, 2, 2048, 2048], P('fsdp', None, 'seq'), may hold values from -128 to 128
- image_k: bfloat16 [8, 2, 2048, 2048], P('fsdp', None, 'seq'), may hold values from -4 to 4
- image_v: bfloat16 [8, 2, 2048, 2048], P('fsdp', None, 'seq'), may hold values from -6 to 6
- w_out: bfloat16 [2048, 1280], P('fsdp'), may hold values from -0.125 to 0.125
- target: bfloat16 [8, 2, 2048, 1280], P('fsdp', None, 'seq'), may hold values from -12 to 12
Outputs:
- pair_loss: float32 [8], P('fsdp')
- grad_q: bfloat16 [8, 2, 2048, 2048], P('fsdp', None, None, 'seq')
- grad_k: bfloat16 [8, 2, 2048, 2048], P('fsdp', None, None, 'seq')
- grad_v: bfloat16 [8, 2, 2048, 2048], P('fsdp', None, None, 'seq')
All inputs are finite; a program needn't handle non-finite values. No bound on the sum of `lengths` on one device may be relied on, other than what follows from the above.
Results may differ from a plain program's by a relative error of at most 0.029.
Values may be sent and summed in bfloat16 or wider, within the bound.
A program may use at most 128 MiB of HBM per device.

v0:
```python
import math

import jax
import jax.numpy as jnp
from jax import lax
from jax.sharding import PartitionSpec as P

PROMPT = 256
HEAD = 64
CH = 1280


dpo_beta = 20.0
norm_eps = 1e-06


def rms_gain(values, gain):
    mean_sq = jnp.mean(values * values, axis=-1, keepdims=True)
    return values * lax.rsqrt(mean_sq + norm_eps) * gain


def noise_level(step_index):
    fraction = (step_index.astype(jnp.float32) + 1.0) / 1000.0
    return 3.0 * fraction / (1.0 + 2.0 * fraction)


def softmax_rows(queries, key_rows, key_mask):
    scores = jnp.einsum("qh,kh->qk", queries, key_rows, preferred_element_type=jnp.float32) * (
        1.0 / math.sqrt(HEAD)
    )
    scores = jnp.where(key_mask[None, :], scores, -jnp.inf)
    top_score = jnp.max(scores, axis=-1, keepdims=True)
    weights = jnp.exp(scores - top_score)
    return (weights / jnp.sum(weights, axis=-1, keepdims=True)).astype(jnp.bfloat16)


def stream_forward(queries, key_rows, value_rows, key_mask):
    seq_len = queries.shape[0]
    block_rows = min(512, seq_len)
    query_blocks = queries.reshape(seq_len // block_rows, block_rows, HEAD)

    def one_block(query_block):
        probs_bf = softmax_rows(query_block, key_rows, key_mask)
        return jnp.dot(probs_bf, value_rows, preferred_element_type=jnp.float32).astype(
            jnp.bfloat16
        )

    return lax.map(one_block, query_blocks).reshape(seq_len, HEAD)


def stream_backward(queries, key_rows, value_rows, key_mask, attended, grad_out):
    seq_len = queries.shape[0]
    block_rows = min(512, seq_len)
    block_count = seq_len // block_rows

    def one_block(carried, pieces):
        key_acc, value_acc = carried
        query_block, out_block, grad_block = pieces
        probs_bf = softmax_rows(query_block, key_rows, key_mask)
        grad_prob = jnp.einsum(
            "qh,kh->qk", grad_block, value_rows, preferred_element_type=jnp.float32
        )
        row_delta = jnp.sum(
            grad_block.astype(jnp.float32) * out_block.astype(jnp.float32), axis=-1, keepdims=True
        )
        grad_score = (
            probs_bf.astype(jnp.float32) * (grad_prob - row_delta) * (1.0 / math.sqrt(HEAD))
        ).astype(jnp.bfloat16)
        grad_query = jnp.dot(grad_score, key_rows, preferred_element_type=jnp.float32).astype(
            jnp.bfloat16
        )
        key_acc = key_acc + jnp.einsum(
            "qk,qh->kh", grad_score[:, :seq_len], query_block, preferred_element_type=jnp.float32
        )
        value_acc = value_acc + jnp.einsum(
            "qk,qh->kh", probs_bf[:, :seq_len], grad_block, preferred_element_type=jnp.float32
        )
        return ((key_acc, value_acc), grad_query)

    zeros_acc = jnp.zeros((seq_len, HEAD), jnp.float32)
    shaped = (
        queries.reshape(block_count, block_rows, HEAD),
        attended.reshape(block_count, block_rows, HEAD),
        grad_out.reshape(block_count, block_rows, HEAD),
    )
    (key_acc, value_acc), grad_query = lax.scan(one_block, (zeros_acc, zeros_acc), shaped)
    return (
        grad_query.reshape(seq_len, HEAD),
        key_acc.astype(jnp.bfloat16),
        value_acc.astype(jnp.bfloat16),
    )


def on_device(
    prompt,
    lengths,
    timesteps,
    ref_errors,
    gain_ffn,
    w_in_gate,
    w_in_up,
    w_in_down,
    gain_final,
    w_context,
    image_q,
    image_k,
    image_v,
    w_out,
    target,
):
    gate_full, up_full, down_full, context_full, out_full = (
        lax.all_gather(w_in_gate, "fsdp", axis=0, tiled=True),
        lax.all_gather(w_in_up, "fsdp", axis=0, tiled=True),
        lax.all_gather(w_in_down, "fsdp", axis=1, tiled=True),
        lax.all_gather(w_context, "fsdp", axis=0, tiled=True),
        lax.all_gather(w_out, "fsdp", axis=0, tiled=True),
    )
    prompt_f32 = prompt[0].astype(jnp.float32)
    normed = rms_gain(prompt_f32, gain_ffn).astype(jnp.bfloat16)
    gate_act = jnp.dot(normed, gate_full, preferred_element_type=jnp.float32)
    up_act = jnp.dot(normed, up_full, preferred_element_type=jnp.float32)
    hidden = (jax.nn.gelu(gate_act, approximate=True) * up_act).astype(jnp.bfloat16)
    partial_value = jnp.dot(hidden, down_full, preferred_element_type=jnp.float32)
    summed = lax.psum(partial_value.astype(jnp.bfloat16), "seq").astype(jnp.float32)
    encoded = rms_gain(prompt_f32 + summed, gain_final).astype(jnp.bfloat16)
    context = jnp.dot(encoded, context_full, preferred_element_type=jnp.float32).astype(
        jnp.bfloat16
    )
    text_keys = context[:, :HEAD]
    text_values = context[:, HEAD:]
    q_heads, k_heads, v_heads = (
        lax.all_to_all(image_q, "seq", split_axis=3, concat_axis=2, tiled=True),
        lax.all_to_all(image_k, "seq", split_axis=3, concat_axis=2, tiled=True),
        lax.all_to_all(image_v, "seq", split_axis=3, concat_axis=2, tiled=True),
    )
    seq_len = q_heads.shape[2]
    key_mask = jnp.arange(seq_len + PROMPT) < seq_len + lengths[0]
    key_sets = []
    value_sets = []
    head_outs = []
    for stream in range(2):
        key_rows = jnp.concatenate([k_heads[0, stream], text_keys], axis=0)
        value_rows = jnp.concatenate([v_heads[0, stream], text_values], axis=0)
        key_sets.append(key_rows)
        value_sets.append(value_rows)
        head_outs.append(stream_forward(q_heads[0, stream], key_rows, value_rows, key_mask))
    attended = jnp.stack(head_outs)[None]
    tok_out = lax.all_to_all(attended, "seq", split_axis=2, concat_axis=3, tiled=True)
    predicted = jnp.einsum("sti,ic->stc", tok_out[0], out_full, preferred_element_type=jnp.float32)
    residual = predicted - target[0].astype(jnp.float32)
    partial_err = jnp.sum(residual * residual, axis=(1, 2))
    error_sums = lax.psum(partial_err, "seq")
    mean_errors = error_sums / (seq_len * CH)
    error_gap = mean_errors[0] - ref_errors[0, 0] - (mean_errors[1] - ref_errors[0, 1])
    sigma_t = noise_level(timesteps[0])
    logit_value = dpo_beta * sigma_t * error_gap
    pair_loss = jax.nn.softplus(logit_value)[None]
    coefficient = sigma_t * jax.nn.sigmoid(logit_value)
    stream_signs = jnp.stack([coefficient, -coefficient])
    grad_pred = (stream_signs[:, None, None] * residual).astype(jnp.bfloat16)
    grad_tok = jnp.einsum(
        "stc,ic->sti", grad_pred, out_full, preferred_element_type=jnp.float32
    ).astype(jnp.bfloat16)
    grad_heads = lax.all_to_all(grad_tok[None], "seq", split_axis=3, concat_axis=2, tiled=True)
    query_grads = []
    key_grads = []
    value_grads = []
    for stream in range(2):
        grad_query, grad_key, grad_value = stream_backward(
            q_heads[0, stream],
            key_sets[stream],
            value_sets[stream],
            key_mask,
            head_outs[stream],
            grad_heads[0, stream],
        )
        query_grads.append(grad_query)
        key_grads.append(grad_key)
        value_grads.append(grad_value)
    return (
        pair_loss,
        jnp.stack(query_grads)[None],
        jnp.stack(key_grads)[None],
        jnp.stack(value_grads)[None],
    )


def solution(mesh):
    return jax.shard_map(
        on_device,
        mesh=mesh,
        in_specs=(
            P("fsdp", None, None),
            P("fsdp"),
            P("fsdp"),
            P("fsdp", None),
            P(),
            P("fsdp", "seq"),
            P("fsdp", "seq"),
            P("seq", "fsdp"),
            P(),
            P("fsdp", "seq"),
            P("fsdp", None, "seq", None),
            P("fsdp", None, "seq", None),
            P("fsdp", None, "seq", None),
            P("fsdp", None),
            P("fsdp", None, "seq", None),
        ),
        out_specs=(
            P("fsdp"),
            P("fsdp", None, None, "seq"),
            P("fsdp", None, None, "seq"),
            P("fsdp", None, None, "seq"),
        ),
        check_vma=False,
    )
```

profile of v0, /device:TPU:33, one launch (start us, length us, event | category | flops | bytes accessed | tf_op | source)
XLA Modules:
  0.0 884.0 jit_solution(1464084878823795982)
XLA Ops:
  11.7 38.5 %all-gather.6.cloned.1.call-done = bf16[4096,256]{1,0:T(8,128)(2,1)} async-done(((bf16[512,256]{1,0:T(8,128)(2,1)}), bf16[4096,256]{1,0:T(8,128)(2,1)}) %all-gather.6.cloned.1.call-update) | async-done | bytes 2097168 | tf_op jit(solution)/shard_map/all_gather | solution.py:112
  50.2 3.0 fusion.103
  53.2 42.2 %all-gather.10.cloned.1.call-done = bf16[256,4096]{1,0:T(8,128)(2,1)} async-done(((bf16[256,512]{1,0:T(8,128)(2,1)}), bf16[256,4096]{1,0:T(8,128)(2,1)}) %all-gather.10.cloned.1.call-update) | async-done | bytes 2097168 | tf_op jit(solution)/shard_map/all_gather | solution.py:114
  95.4 45.2 %all-gather.8.cloned.1.call-done = bf16[4096,256]{1,0:T(8,128)(2,1)} async-done(((bf16[512,256]{1,0:T(8,128)(2,1)}), bf16[4096,256]{1,0:T(8,128)(2,1)}) %all-gather.8.cloned.1.call-update) | async-done | bytes 2097168 | tf_op jit(solution)/shard_map/all_gather | solution.py:113
  140.6 6.0 convolution_convert_fusion.2
  148.6 3.8 reshape.73
  152.4 15.4 %all-to-all-start.2 = ((bf16[32,2,4096]{2,1,0:T(2,128)(2,1)}), bf16[32,2,4096]{2,1,0:T(2,128)(2,1)S(1)}, u32[]{:S(2)}, u32[]{:S(2)}) async-start(bf16[32,2,4096]{2,1,0:T(2,128)(2,1)} %reshape.73), calls=%async_computation.2 | async-start | bytes 1048576 | tf_op jit(solution)/shard_map/all_to_all | solution.py:134
  170.4 3.8 reshape.71
  174.2 13.0 %all-to-all-done.2 = bf16[32,2,4096]{2,1,0:T(2,128)(2,1)S(1)} async-done(((bf16[32,2,4096]{2,1,0:T(2,128)(2,1)}), bf16[32,2,4096]{2,1,0:T(2,128)(2,1)S(1)}, u32[]{:S(2)}, u32[]{:S(2)}) %all-to-all-start.2) | async-done | bytes 524320 | tf_op jit(solution)/shard_map/all_to_all | solution.py:134
  187.2 4.8 all-to-all-start.1
  192.0 3.6 copy.69
  195.6 3.8 reshape.69
  199.4 11.8 %all-to-all-done.1 = bf16[32,2,4096]{2,1,0:T(2,128)(2,1)S(1)} async-done(((bf16[32,2,4096]{2,1,0:T(2,128)(2,1)}), bf16[32,2,4096]{2,1,0:T(2,128)(2,1)S(1)}, u32[]{:S(2)}, u32[]{:S(2)}) %all-to-all-start.1) | async-done | bytes 524320 | tf_op jit(solution)/shard_map/all_to_all | solution.py:133
  211.9 4.5 all-to-all-start
  219.4 3.7 copy.75
  223.0 3.7 reshape.72
  226.7 3.7 copy.72
  236.9 2.9 copy.109
  243.2 219.1 %all-reduce.2.cloned.1.call-done = bf16[256,4096]{1,0:T(8,128)(2,1)} async-done(((bf16[256,4096]{1,0:T(8,128)(2,1)}), bf16[256,4096]{1,0:T(8,128)(2,1)}) %all-reduce.2.cloned.1.call-update) | async-done | bytes 2097168 | tf_op jit(solution)/shard_map/psum | solution.py:124
  464.6 34.1 %all-gather.12.cloned.1.call-done = bf16[4096,128]{1,0:T(8,128)(2,1)} async-done(((bf16[512,128]{1,0:T(8,128)(2,1)}), bf16[4096,128]{1,0:T(8,128)(2,1)}) %all-gather.12.cloned.1.call-update) | async-done | bytes 1048592 | tf_op jit(solution)/shard_map/all_gather | solution.py:115
  498.8 3.0 fusion.91
  502.0 2.8 pad_maximum_fusion.1
  504.9 19.6 %while.52 = (s32[]{:T(128)}, bf16[4,512,64]{1,2,0:T(8,128)(2,1)S(1)}, bf16[4,512,64]{2,1,0:T(8,128)(2,1)}, bf16[2304,64]{1,0:T(8,128)(2,1)S(1)}, bf16[2304,64]{1,0:T(8,128)(2,1)}, /*index=5*/s32[]{:T(128)}, s32[]{:T(128)}) while((s32[]{:T(128)}, bf16[4,512,64]{1,2,0:T(8,128)(2,1)S(1)}, bf16[4,512,64]{2,1,0:T(8,128)(2,1)}, ...), condition=%wide.region_6.7_spmd.clone, body=%wide.region_3.6_spmd.clone.sunk | while | flops 311461120 | bytes 14957653 | solution.py:48
  525.1 11.8 %while.53 = (s32[]{:T(128)}, bf16[4,512,64]{1,2,0:T(8,128)(2,1)S(1)}, bf16[4,512,64]{2,1,0:T(8,128)(2,1)S(1)}, bf16[2304,64]{1,0:T(8,128)(2,1)S(1)}, bf16[2304,64]{1,0:T(8,128)(2,1)S(1)}, /*index=5*/s32[]{:T(128)}, s32[]{:T(128)}) while((s32[]{:T(128)}, bf16[4,512,64]{1,2,0:T(8,128)(2,1)S(1)}, ...), condition=%wide.region_10.11_spmd.clone, body=%wide.region_7.10_spmd.clone.sunk | while | flops 311461120 | bytes 15547737 | solution.py:48
  538.3 3.6 copy.83
  541.9 3.9 reshape.75
  545.8 15.5 %all-to-all-start.3 = ((bf16[32,2,4096]{2,1,0:T(2,128)(2,1)}), bf16[32,2,4096]{2,1,0:T(2,128)(2,1)}, u32[]{:S(2)}, u32[]{:S(2)}) async-start(bf16[32,2,4096]{2,1,0:T(2,128)(2,1)} %reshape.75), calls=%async_computation.3 | async-start | bytes 1048576 | tf_op jit(solution)/shard_map/all_to_all | solution.py:148
  562.6 21.0 %all-to-all-done.3 = bf16[32,2,4096]{2,1,0:T(2,128)(2,1)} async-done(((bf16[32,2,4096]{2,1,0:T(2,128)(2,1)}), bf16[32,2,4096]{2,1,0:T(2,128)(2,1)}, u32[]{:S(2)}, u32[]{:S(2)}) %all-to-all-start.3) | async-done | bytes 524320 | tf_op jit(solution)/shard_map/all_to_all | solution.py:148
  583.6 3.7 reshape.76
  587.3 2.9 copy.107
  592.3 3.5 multiply_reduce_fusion.1
  595.8 69.1 %psum.15 = f32[2]{0:T(128)S(1)} all-reduce(f32[2]{0:T(128)S(1)} %get-tuple-element.468), channel_id=1, replica_groups=mesh['seq'=32,'fsdp'=8] {'seq'}, use_global_device_ids=true, to_apply=%region_12.13 | all-reduce | flops 2 | bytes 16 | tf_op jit(solution)/shard_map/psum | solution.py:152
  668.2 4.3 fusion.83
  674.8 8.9 %all-to-all-start.4 = ((bf16[32,2,4096]{2,1,0:T(2,128)(2,1)}), bf16[32,2,4096]{2,1,0:T(2,128)(2,1)S(1)}, u32[]{:S(2)}, u32[]{:S(2)}) async-start(bf16[32,2,4096]{2,1,0:T(2,128)(2,1)} %reshape.77), calls=%async_computation.4 | async-start | bytes 1048576 | tf_op jit(solution)/shard_map/all_to_all | solution.py:164
  683.8 18.1 %all-to-all-done.4 = bf16[32,2,4096]{2,1,0:T(2,128)(2,1)S(1)} async-done(((bf16[32,2,4096]{2,1,0:T(2,128)(2,1)}), bf16[32,2,4096]{2,1,0:T(2,128)(2,1)S(1)}, u32[]{:S(2)}, u32[]{:S(2)}) %all-to-all-start.4) | async-done | bytes 524320 | tf_op jit(solution)/shard_map/all_to_all | solution.py:164
  706.6 78.6 %while.54 = (s32[]{:T(128)}, f32[2048,64]{0,1:T(8,128)}, f32[2048,64]{0,1:T(8,128)}, bf16[4,512,64]{1,2,0:T(8,128)(2,1)}, bf16[4,512,64]{2,1,0:T(8,128)(2,1)}, /...) while((s32[]{:T(128)}, f32[2048,64]{0,1:T(8,128)}, ...), condition=%wide.region_17.18_spmd.clone, body=%wide.region_13.17_spmd.clone.sunk | while | flops 737444608 | bytes 32068744 | solution.py:86
  714.3 3.5 fusion.192
  717.7 2.9 convolution_add_fusion.8
  720.6 3.1 fusion.193
  733.7 3.5 fusion.192
  737.1 3.0 convolution_add_fusion.8
  740.2 3.1 fusion.193
  743.3 2.4 convolution_add_fusion.9
  753.4 3.5 fusion.192
  756.9 3.0 convolution_add_fusion.8
  759.9 3.1 fusion.193
  763.0 2.4 convolution_add_fusion.9
  773.2 3.5 fusion.192
  776.6 3.0 convolution_add_fusion.8
  779.6 3.1 fusion.193
  782.8 2.4 convolution_add_fusion.9
  789.7 77.7 %while.55 = (s32[]{:T(128)}, f32[2048,64]{0,1:T(8,128)}, f32[2048,64]{0,1:T(8,128)}, bf16[4,512,64]{1,2,0:T(8,128)(2,1)}, bf16[4,512,64]{2,1,0:T(8,128)(2,1)}, /...) while((s32[]{:T(128)}, f32[2048,64]{0,1:T(8,128)}, ...), condition=%wide.region_22.23_spmd.clone, body=%wide.region_18.22_spmd.clone.sunk | while | flops 737444608 | bytes 37147868 | solution.py:86
  797.6 3.2 fusion.206
  800.8 3.0 convolution_add_fusion.10
  803.8 3.1 fusion.207
  816.9 3.2 fusion.206
  820.1 3.1 convolution_add_fusion.10
  823.2 3.1 fusion.207
  836.3 3.2 fusion.206
  839.5 3.1 convolution_add_fusion.10
  842.6 3.1 fusion.207
  855.7 3.2 fusion.206
  858.9 3.1 convolution_add_fusion.10
  862.0 3.1 fusion.207
  (211 shorter events, 153.3 us)
Async XLA Ops:
  7.2 43.0 %all-gather.6.cloned.1.call-start = ((), (), s32[]{:S(2)}) async-start(), calls=%async_computation.5 | async-start | bytes 2359296 | tf_op jit(solution)/shard_map/all_gather | solution.py:112
  7.9 87.5 %all-gather.10.cloned.1.call-start = ((), (), s32[]{:S(2)}) async-start(), calls=%async_computation.7 | async-start | bytes 2359296 | tf_op jit(solution)/shard_map/all_gather | solution.py:114
  8.6 131.9 %all-gather.8.cloned.1.call-start = ((), (), s32[]{:S(2)}) async-start(), calls=%async_computation.6 | async-start | bytes 2359296 | tf_op jit(solution)/shard_map/all_gather | solution.py:113
  9.4 131.2 %copy-start.2 = (bf16[1,256,4096]{2,1,0:T(8,128)(2,1)S(1)}, bf16[1,256,4096]{2,1,0:T(8,128)(2,1)}, u32[]{:S(2)}) copy-start(bf16[1,256,4096]{2,1,0:T(8,128)(2,1)} %param.23) | copy-start | bytes 6291460
  9.4 131.2 %copy-start.14 = (f32[4096]{0:T(1024)S(1)}, f32[4096]{0:T(1024)}, u32[]{:S(2)}) copy-start(f32[4096]{0:T(1024)} %param.27) | copy-start | bytes 49156
  9.4 452.8 %all-reduce.2.cloned.1.call-start = ((), (), s32[]{:S(2)}) async-start(), calls=%async_computation.8 | async-start | bytes 4194304 | tf_op jit(solution)/shard_map/psum | solution.py:124
  53.2 93.4 %copy-start.8 = (bf16[1,2,64,2048]{3,2,1,0:T(8,128)(2,1)S(1)}, bf16[1,2,64,2048]{3,2,1,0:T(8,128)(2,1)}, u32[]{:S(2)}) copy-start(bf16[1,2,64,2048]{3,2,1,0:T(8,128)(2,1)} %param.35) | copy-start | bytes 1572868
  146.6 21.8 %copy-start.9 = (bf16[1,2,64,2048]{3,2,1,0:T(8,128)(2,1)S(1)}, bf16[1,2,64,2048]{3,2,1,0:T(8,128)(2,1)}, u32[]{:S(2)}) copy-start(bf16[1,2,64,2048]{3,2,1,0:T(8,128)(2,1)} %param.34) | copy-start | bytes 1572868
  152.4 34.8 %all-to-all-start.2 = ((bf16[32,2,4096]{2,1,0:T(2,128)(2,1)}), bf16[32,2,4096]{2,1,0:T(2,128)(2,1)S(1)}, u32[]{:S(2)}, u32[]{:S(2)}) async-start(bf16[32,2,4096]{2,1,0:T(2,128)(2,1)} %reshape.73), calls=%async_computation.2 | async-start | bytes 1048576 | tf_op jit(solution)/shard_map/all_to_all | solution.py:134
  167.8 331.0 %all-gather.12.cloned.1.call-start = ((), (), s32[]{:S(2)}) async-start(), calls=%async_computation.9 | async-start | bytes 1179648 | tf_op jit(solution)/shard_map/all_gather | solution.py:115
  187.2 24.0 %all-to-all-start.1 = ((bf16[32,2,4096]{2,1,0:T(2,128)(2,1)}), bf16[32,2,4096]{2,1,0:T(2,128)(2,1)S(1)}, u32[]{:S(2)}, u32[]{:S(2)}) async-start(bf16[32,2,4096]{2,1,0:T(2,128)(2,1)} %reshape.71), calls=%async_computation.1 | async-start | bytes 1048576 | tf_op jit(solution)/shard_map/all_to_all | solution.py:133
  211.1 0.8 copy-start.6
  211.9 23.3 %all-to-all-start = ((bf16[32,2,4096]{2,1,0:T(2,128)(2,1)}), bf16[32,2,4096]{2,1,0:T(2,128)(2,1)S(1)}, u32[]{:S(2)}, u32[]{:S(2)}) async-start(bf16[32,2,4096]{2,1,0:T(2,128)(2,1)} %reshape.69), calls=%async_computation | async-start | bytes 1048576 | tf_op jit(solution)/shard_map/all_to_all | solution.py:132
  216.4 375.9 %all-gather.14.cloned.1.call-start = ((), (), s32[]{:S(2)}) async-start(), calls=%async_computation.10 | async-start | bytes 5898240 | tf_op jit(solution)/shard_map/all_gather | solution.py:116
  239.8 259.0 %copy-start.15 = (f32[4096]{0:T(1024)S(1)}, f32[4096]{0:T(1024)}, u32[]{:S(2)}) copy-start(f32[4096]{0:T(1024)} %param.31) | copy-start | bytes 49156
  524.4 0.7 copy-start.4
  537.0 53.2 %copy-start = (bf16[2304,64]{1,0:T(8,128)(2,1)}, bf16[2304,64]{1,0:T(8,128)(2,1)S(1)}, u32[]{:S(2)}) copy-start(bf16[2304,64]{1,0:T(8,128)(2,1)S(1)} %get-tuple-element.807) | copy-start | bytes 884740
  537.0 53.2 %copy-start.3 = (bf16[4,512,64]{2,1,0:T(8,128)(2,1)}, bf16[4,512,64]{2,1,0:T(8,128)(2,1)S(1)}, u32[]{:S(2)}) copy-start(bf16[4,512,64]{2,1,0:T(8,128)(2,1)S(1)} %get-tuple-element.808) | copy-start | bytes 786436
  537.0 53.2 %copy-start.5 = (bf16[4,512,64]{1,2,0:T(8,128)(2,1)}, bf16[4,512,64]{1,2,0:T(8,128)(2,1)S(1)}, u32[]{:S(2)}) copy-start(bf16[4,512,64]{1,2,0:T(8,128)(2,1)S(1)} %get-tuple-element.734) | copy-start | bytes 786436
  537.0 25.0 %copy-start.13 = (f32[1,2]{1,0:T(1,128)S(1)}, f32[1,2]{1,0:T(1,128)}, u32[]{:S(2)}) copy-start(f32[1,2]{1,0:T(1,128)} %param.26) | copy-start | bytes 28
  541.9 50.4 %copy-start.12 = (bf16[1,2,64,1280]{3,2,1,0:T(8,128)(2,1)S(1)}, bf16[1,2,64,1280]{3,2,1,0:T(8,128)(2,1)}, u32[]{:S(2)}) copy-start(bf16[1,2,64,1280]{3,2,1,0:T(8,128)(2,1)} %param.37) | copy-start | bytes 983044
  545.8 37.8 %all-to-all-start.3 = ((bf16[32,2,4096]{2,1,0:T(2,128)(2,1)}), bf16[32,2,4096]{2,1,0:T(2,128)(2,1)}, u32[]{:S(2)}, u32[]{:S(2)}) async-start(bf16[32,2,4096]{2,1,0:T(2,128)(2,1)} %reshape.75), calls=%async_computation.3 | async-start | bytes 1048576 | tf_op jit(solution)/shard_map/all_to_all | solution.py:148
  674.8 27.2 %all-to-all-start.4 = ((bf16[32,2,4096]{2,1,0:T(2,128)(2,1)}), bf16[32,2,4096]{2,1,0:T(2,128)(2,1)S(1)}, u32[]{:S(2)}, u32[]{:S(2)}) async-start(bf16[32,2,4096]{2,1,0:T(2,128)(2,1)} %reshape.77), calls=%async_computation.4 | async-start | bytes 1048576 | tf_op jit(solution)/shard_map/all_to_all | solution.py:164
  792.5 5.1 copy-start.1
  800.8 6.1 copy-start.10
  808.4 0.8 copy-start.11
  811.8 5.1 copy-start.1
  820.1 6.2 copy-start.10
  827.8 0.8 copy-start.11
  831.2 5.1 copy-start.1
  839.5 6.2 copy-start.10
  847.2 0.8 copy-start.11
  850.6 5.1 copy-start.1
  858.9 6.2 copy-start.10
  866.6 0.8 copy-start.11
  867.4 6.0 copy-start.7
Sparse Core Ops, SparseCore 0:
  9.8 40.3 all-gather.5
  52.0 43.3 all-gather.9
  97.2 43.3 all-gather.7
  146.7 315.4 all-reduce.1
  464.0 34.6 all-gather.11
  500.5 79.8 all-gather.13
where the time goes:
time: 896 us; the launch traced here: 884 us
  waiting for transfers between devices  446 us (50%)
  matrix products  150 us (17%)
  local copies, waits for them, and re-layouts  104 us (12%)
  blocking collectives  69.1 us (8%)
  starting transfers between devices  49.4 us (6%)
  other arithmetic  44.3 us (5%)
  between operations  19.9 us (2%)
    psum x1, waiting for transfers between devices, on_device(): lax.psum(partial_value.astype(jnp.bfloat16), 'seq').astype(jnp.float32)  219 us
    psum x1, blocking collectives, on_device(): error_sums = lax.psum(partial_err, 'seq')  69.1 us
    all_gather x1, waiting for transfers between devices, on_device(): lax.all_gather(w_in_up, 'fsdp', axis=0, tiled=True)  45.2 us
    all_gather x1, waiting for transfers between devices, on_device(): lax.all_gather(w_in_down, 'fsdp', axis=1, tiled=True)  42.2 us
    unnamed x43, local copies, waits for them, and re-layouts  41.1 us
    all_gather x1, waiting for transfers between devices, on_device(): lax.all_gather(w_in_gate, 'fsdp', axis=0, tiled=True)  38.5 us
    all_gather x1, waiting for transfers between devices, on_device(): lax.all_gather(w_context, 'fsdp', axis=0, tiled=True)  34.1 us
    dot_general x8, matrix products, one_block(): jnp.einsum('qh,kh->qk', grad_block, value_rows, preferred_element_type=jn...  26.7 us
  transfers between devices with their start and end apart: 11, of which 10 were waited for; matrix products, arithmetic and copies ran while one was open for 12% of the time, Pallas kernels for 0%

commit v1 on v0

v1 whole, which is shorter than its diff:
```python
import functools
import math

import jax
import jax.numpy as jnp
from jax import lax
from jax.experimental import pallas as pl
from jax.experimental.pallas import tpu as pltpu
from jax.sharding import PartitionSpec as P

PROMPT = 256
HEAD = 64
CH = 1280
SEQ = 2048
LANES = 128
ROWS = 256

dpo_beta = 20.0
norm_eps = 1e-06

NT = (((1,), (1,)), ((), ()))
NN = (((1,), (0,)), ((), ()))


def dot(a, b, dims=NN):
    return lax.dot_general(a, b, dims, preferred_element_type=jnp.float32)


def rms_gain(values, gain):
    mean_sq = jnp.mean(values * values, axis=-1, keepdims=True)
    return values * lax.rsqrt(mean_sq + norm_eps) * gain


def noise_level(step_index):
    fraction = (step_index.astype(jnp.float32) + 1.0) / 1000.0
    return 3.0 * fraction / (1.0 + 2.0 * fraction)


def head_lanes(j):
    lane = lax.broadcasted_iota(jnp.int32, (1, LANES), 1)
    return (lane >= j * HEAD) & (lane < (j + 1) * HEAD)


def with_ones(values):
    return jnp.concatenate([values, jnp.ones_like(values)], axis=1)


def by_head(first, second):
    return jnp.where(head_lanes(0), first, second)


def image_forward(q_ref, k_ref, v_ref, e_ref, o_ref, z_ref, m_ref):
    q = q_ref[...] * jnp.asarray(1.0 / math.sqrt(HEAD), jnp.bfloat16)
    v_aug = with_ones(v_ref[...])
    outs, tops = [], []
    for j in range(2):
        qj = jnp.where(head_lanes(j), q, jnp.zeros_like(q))
        s = dot(qj, k_ref[...], NT)
        top = jnp.max(s, axis=-1, keepdims=True)
        e = jnp.exp(s - top).astype(jnp.bfloat16)
        e_ref[j] = e
        outs.append(dot(e, v_aug))
        tops.append(top)
    o_ref[...] = by_head(outs[0][:, :LANES], outs[1][:, :LANES])
    z_ref[...] = by_head(outs[0][:, LANES:], outs[1][:, LANES:])
    m_ref[...] = by_head(tops[0], tops[1])


def text_forward(len_ref, q_ref, k_ref, v_ref, o_ref, z_ref, m_ref, att_ref, e_ref, si_ref, st_ref):
    q = q_ref[...] * jnp.asarray(1.0 / math.sqrt(HEAD), jnp.bfloat16)
    v_aug = with_ones(v_ref[...])
    kept = lax.broadcasted_iota(jnp.int32, (1, PROMPT), 1) < len_ref[0]
    outs, tops = [], []
    for j in range(2):
        qj = jnp.where(head_lanes(j), q, jnp.zeros_like(q))
        s = jnp.where(kept, dot(qj, k_ref[...], NT), -jnp.inf)
        old = m_ref[:, j * HEAD:j * HEAD + 1]
        top = jnp.maximum(old, jnp.max(s, axis=-1, keepdims=True))
        e = jnp.exp(s - top).astype(jnp.bfloat16)
        e_ref[j] = e
        outs.append(dot(e, v_aug))
        tops.append(top)
    top = by_head(tops[0], tops[1])
    alpha = jnp.exp(m_ref[...] - top)
    z = alpha * z_ref[...] + by_head(outs[0][:, LANES:], outs[1][:, LANES:])
    o = alpha * o_ref[...] + by_head(outs[0][:, :LANES], outs[1][:, :LANES])
    inv = 1.0 / z
    att_ref[...] = (o * inv).astype(jnp.bfloat16)
    si_ref[...] = alpha * inv
    st_ref[...] = inv


def backward(coef_ref, q_ref, g_ref, att_ref, ei_ref, et_ref, si_ref, st_ref, k_ref, v_ref, kt_ref, vt_ref,
             gq_ref, gk_ref, gv_ref, k_acc, v_acc):
    step = pl.program_id(0)

    @pl.when(step == 0)
    def _():
        k_acc[...] = jnp.zeros_like(k_acc)
        v_acc[...] = jnp.zeros_like(v_acc)

    coef = coef_ref[0]
    g = g_ref[...].astype(jnp.float32)
    prod = g * att_ref[...].astype(jnp.float32)
    v_aug, vt_aug = with_ones(v_ref[...]), with_ones(vt_ref[...])
    q_t = q_ref[...].T
    lane = lax.broadcasted_iota(jnp.int32, (1, LANES), 1)
    grads = []
    for j in range(2):
        mine = head_lanes(j)
        gj = jnp.where(mine, g, 0.0)
        delta = jnp.sum(jnp.where(mine, prod, 0.0), axis=-1, keepdims=True)

        def scaled(scale):
            gs = (gj * scale).astype(jnp.bfloat16)
            d = -delta * scale
            hi = d.astype(jnp.bfloat16)
            lo = (d - hi.astype(jnp.float32)).astype(jnp.bfloat16)
            extra = jnp.where(lane == 0, hi, jnp.where(lane == 1, lo, jnp.zeros_like(hi)))
            return gs, jnp.concatenate([gs, extra], axis=1)

        gi, lhs_i = scaled(si_ref[:, j * HEAD:j * HEAD + 1])
        _, lhs_t = scaled(st_ref[:, j * HEAD:j * HEAD + 1])
        ei = ei_ref[j]
        ds = (ei.astype(jnp.float32) * dot(lhs_i, v_aug, NT)).astype(jnp.bfloat16)
        ds_t = (et_ref[j].astype(jnp.float32) * dot(lhs_t, vt_aug, NT)).astype(jnp.bfloat16)
        grads.append(dot(ds, k_ref[...]) + dot(ds_t, kt_ref[...]))
        rows = slice(j * HEAD, (j + 1) * HEAD)
        k_acc[rows, :] += dot(q_t[rows, :], ds)
        v_acc[rows, :] += dot(gi.T[rows, :], ei)
    factor = coef * (1.0 / math.sqrt(HEAD))
    gq_ref[...] = (by_head(grads[0], grads[1]) * factor).T.astype(jnp.bfloat16)

    @pl.when(step == pl.num_programs(0) - 1)
    def _():
        gk_ref[...] = (k_acc[...] * factor).astype(jnp.bfloat16)
        gv_ref[...] = (v_acc[...] * coef).astype(jnp.bfloat16)


def block(shape, index_map):
    return pl.BlockSpec(shape, index_map)


def whole(*shape):
    return pl.BlockSpec(shape, lambda i: (0,) * len(shape))


def rows_of(width):
    return pl.BlockSpec((ROWS, width), lambda i: (i, 0))


def params():
    return pltpu.CompilerParams(vmem_limit_bytes=48 * 1024 * 1024)


def call_image_forward(q, k, v):
    f32 = lambda: jax.ShapeDtypeStruct((SEQ, LANES), jnp.float32)
    return pl.pallas_call(
        image_forward,
        grid=(SEQ // ROWS,),
        in_specs=[rows_of(LANES), whole(SEQ, LANES), whole(SEQ, LANES)],
        out_specs=[pl.BlockSpec((2, ROWS, SEQ), lambda i: (0, i, 0)), rows_of(LANES), rows_of(LANES), rows_of(LANES)],
        out_shape=[jax.ShapeDtypeStruct((2, SEQ, SEQ), jnp.bfloat16), f32(), f32(), f32()],
        compiler_params=params(),
        cost_estimate=pl.CostEstimate(flops=4 * 2 * SEQ * SEQ * 256, bytes_accessed=20_000_000, transcendentals=2 * SEQ * SEQ),
        name="image_forward",
    )(q, k, v)


def call_text_forward(lengths, q, k, v, o, z, m):
    f32 = lambda: jax.ShapeDtypeStruct((SEQ, LANES), jnp.float32)
    return pl.pallas_call(
        text_forward,
        grid=(SEQ // ROWS,),
        in_specs=[pl.BlockSpec(memory_space=pltpu.SMEM), rows_of(LANES), whole(PROMPT, LANES), whole(PROMPT, LANES),
                  rows_of(LANES), rows_of(LANES), rows_of(LANES)],
        out_specs=[rows_of(LANES), pl.BlockSpec((2, ROWS, PROMPT), lambda i: (0, i, 0)), rows_of(LANES), rows_of(LANES)],
        out_shape=[jax.ShapeDtypeStruct((SEQ, LANES), jnp.bfloat16), jax.ShapeDtypeStruct((2, SEQ, PROMPT), jnp.bfloat16),
                   f32(), f32()],
        compiler_params=params(),
        name="text_forward",
    )(lengths, q, k, v, o, z, m)


def call_backward(coef, q, g, att, ei, et, si, st, k, v, kt, vt):
    out = lambda: jax.ShapeDtypeStruct((LANES, SEQ), jnp.bfloat16)
    return pl.pallas_call(
        backward,
        grid=(SEQ // ROWS,),
        in_specs=[pl.BlockSpec(memory_space=pltpu.SMEM), rows_of(LANES), rows_of(LANES), rows_of(LANES),
                  pl.BlockSpec((2, ROWS, SEQ), lambda i: (0, i, 0)), pl.BlockSpec((2, ROWS, PROMPT), lambda i: (0, i, 0)),
                  rows_of(LANES), rows_of(LANES), whole(SEQ, LANES), whole(SEQ, LANES),
                  whole(PROMPT, LANES), whole(PROMPT, LANES)],
        out_specs=[pl.BlockSpec((LANES, ROWS), lambda i: (0, i)), whole(LANES, SEQ), whole(LANES, SEQ)],
        out_shape=[out(), out(), out()],
        scratch_shapes=[pltpu.VMEM((LANES, SEQ), jnp.float32), pltpu.VMEM((LANES, SEQ), jnp.float32)],
        compiler_params=params(),
        name="backward",
    )(coef, q, g, att, ei, et, si, st, k, v, kt, vt)


def to_heads(values):
    return jnp.transpose(values.reshape(2, 64, 16, LANES), (2, 0, 1, 3)).reshape(32, 64, LANES)


def exchange(values):
    return lax.all_to_all(values, "seq", split_axis=0, concat_axis=0, tiled=True)


def swap(values, pairs):
    return lax.ppermute(values, "seq", pairs)


def on_device(prompt, lengths, timesteps, ref_errors, gain_ffn, w_in_gate, w_in_up, w_in_down, gain_final, w_context,
              image_q, image_k, image_v, w_out, target):
    seat = lax.axis_index("seq")
    core = seat % 2
    pairs = [(i, i ^ 1) for i in range(32)]
    gate_full = lax.all_gather(w_in_gate, "fsdp", axis=0, tiled=True)
    up_full = lax.all_gather(w_in_up, "fsdp", axis=0, tiled=True)
    down_full = lax.all_gather(w_in_down, "fsdp", axis=1, tiled=True)
    context_full = lax.all_gather(w_context, "fsdp", axis=0, tiled=True)
    out_full = lax.all_gather(w_out, "fsdp", axis=0, tiled=True)

    sent = jnp.concatenate([to_heads(image_q[0]), to_heads(image_k[0]), to_heads(image_v[0])], axis=1)
    got = exchange(sent)
    q, k, v = (got[:, 64 * i:64 * (i + 1)].reshape(SEQ, LANES) for i in range(3))
    ei, o, z, m = call_image_forward(q, k, v)

    prompt_f32 = prompt[0].astype(jnp.float32)
    normed = rms_gain(prompt_f32, gain_ffn).astype(jnp.bfloat16)
    gate_act = dot(normed, gate_full)
    up_act = dot(normed, up_full)
    hidden = (jax.nn.gelu(gate_act, approximate=True) * up_act).astype(jnp.bfloat16)
    partial_value = dot(hidden, down_full).astype(jnp.bfloat16)
    parts = exchange(partial_value.reshape(32, 8, 4096))
    mine = lax.dynamic_slice_in_dim(prompt[0], seat * 8, 8, 0).astype(jnp.float32)
    state = mine + jnp.sum(parts.astype(jnp.float32), axis=0)
    encoded_rows = rms_gain(state, gain_final).astype(jnp.bfloat16)
    encoded = lax.all_gather(encoded_rows, "seq", axis=0, tiled=True)
    context = dot(encoded, context_full).astype(jnp.bfloat16)
    other = swap(context, pairs)
    first = jnp.where(core == 0, context, other)
    second = jnp.where(core == 0, other, context)
    kt = jnp.concatenate([first[:, :HEAD], second[:, :HEAD]], axis=1)
    vt = jnp.concatenate([first[:, HEAD:], second[:, HEAD:]], axis=1)

    att, et, si, st = call_text_forward(lengths, q, kt, vt, o, z, m)
    back = exchange(att.reshape(32, 64, LANES))
    tok = jnp.transpose(back.reshape(16, 2, 64, LANES), (1, 2, 0, 3)).reshape(LANES, SEQ)
    residual = dot(tok, out_full) - target[0].reshape(LANES, CH).astype(jnp.float32)
    err = jnp.sum((residual * residual).reshape(2, 64 * CH), axis=1)
    hi = lax.reduce_precision(err, 8, 7)
    mid = lax.reduce_precision(err - hi, 8, 7)
    low = err - hi - mid
    pieces = jnp.concatenate([hi, mid, low]).astype(jnp.bfloat16)
    grad_tok = dot(residual.astype(jnp.bfloat16), out_full, NT).astype(jnp.bfloat16)
    extra = jnp.broadcast_to(jnp.pad(pieces, (0, LANES - 6))[None, None, :], (32, 16, LANES))
    arrived = exchange(jnp.concatenate([to_heads(grad_tok), extra], axis=1))
    g = arrived[:, :64].reshape(SEQ, LANES)
    sums = jnp.sum(arrived[:, 64, :6].astype(jnp.float32).reshape(32, 3, 2), axis=(0, 1))
    mean_errors = sums / (SEQ * CH)
    error_gap = mean_errors[0] - ref_errors[0, 0] - (mean_errors[1] - ref_errors[0, 1])
    sigma_t = noise_level(timesteps[0])
    logit_value = dpo_beta * sigma_t * error_gap
    pair_loss = jax.nn.softplus(logit_value)[None]
    coefficient = sigma_t * jax.nn.sigmoid(logit_value)
    coef = jnp.where(core == 0, coefficient, -coefficient)[None]

    grads = jnp.stack(call_backward(coef, q, g, att, ei, et, si, st, k, v, kt, vt))
    halves = grads.reshape(3, 2, HEAD, SEQ)
    own = lax.dynamic_index_in_dim(halves, core, 1, keepdims=False)
    theirs = swap(lax.dynamic_index_in_dim(halves, 1 - core, 1, keepdims=False), pairs)
    outs = jnp.where(core == 0, jnp.stack([own, theirs], axis=1), jnp.stack([theirs, own], axis=1))
    outs = jnp.transpose(outs, (0, 1, 3, 2))
    return pair_loss, outs[0][None], outs[1][None], outs[2][None]


def solution(mesh):
    return jax.shard_map(
        on_device,
        mesh=mesh,
        in_specs=(
            P("fsdp", None, None),
            P("fsdp"),
            P("fsdp"),
            P("fsdp", None),
            P(),
            P("fsdp", "seq"),
            P("fsdp", "seq"),
            P("seq", "fsdp"),
            P(),
            P("fsdp", "seq"),
            P("fsdp", None, "seq", None),
            P("fsdp", None, "seq", None),
            P("fsdp", None, "seq", None),
            P("fsdp", None),
            P("fsdp", None, "seq", None),
        ),
        out_specs=(
            P("fsdp"),
            P("fsdp", None, None, "seq"),
            P("fsdp", None, None, "seq"),
            P("fsdp", None, None, "seq"),
        ),
        check_vma=False,
    )
```

time: 896 us -> 450 us (0.50); the launches traced: 884 us -> 449 us
  waiting for transfers between devices: 446 us -> 284 us
  matrix products: 150 us -> 16.5 us
  local copies, waits for them, and re-layouts: 104 us -> 9.98 us
  Pallas kernels: 0 us -> 47.1 us
  blocking collectives: 69.1 us -> 29.6 us
  other arithmetic: 44.3 us -> 9.78 us
  starting transfers between devices: 49.4 us -> 32.3 us
    psum x1 -> x0, waiting for transfers between devices: 219 us -> none  [on_device(): lax.psum(partial_value.astype(jnp.bfloat16), 'seq').astype(jnp.float32)]
    dot_general x61 -> x5, matrix products: 150 us -> 16.5 us  [dot(): return lax.dot_general(a, b, dims, preferred_element_type=jnp.float32)]
    psum x1 -> x0, blocking collectives: 69.1 us -> none  [on_device(): error_sums = lax.psum(partial_err, 'seq')]
    all_to_all x5 -> x3, waiting for transfers between devices: 64.2 us -> 113 us  [exchange(): lax.all_to_all(values, 'seq', split_axis=0, concat_axis=0, tiled=True)]
    pallas_call x0 -> x3, Pallas kernels: none -> 47.1 us  [the longest x1 21 us: call_backward(): pl.pallas_call(backward, grid=(SEQ // ROWS,), in_specs=[pl.BlockSpec(memo...]
    unnamed x43 -> x24, local copies, waits for them, and re-layouts: 41.1 us -> 3.38 us
    all_to_all x0 -> x1, blocking collectives: none -> 29.6 us  [exchange(): lax.all_to_all(values, 'seq', split_axis=0, concat_axis=0, tiled=True)]
    dynamic_slice x16 -> x1, local copies, waits for them, and re-layouts: 24.7 us -> 0.11 us  [on_device(): own = lax.dynamic_index_in_dim(halves, core, 1, keepdims=False)]
  transfers between devices with their start and end apart: 11 -> 11, of which waited for: 10 -> 9; matrix products, arithmetic and copies ran while one was open for 12% -> 3% of each run, Pallas kernels for 0% -> 6%
where the time goes in v1:
time: 450 us; the launch traced here: 449 us
  waiting for transfers between devices  284 us (63%)
  Pallas kernels  47.1 us (10%)
  starting transfers between devices  32.3 us (7%)
  blocking collectives  29.6 us (7%)
  between operations  19.7 us (4%)
  matrix products  16.5 us (4%)
  local copies, waits for them, and re-layouts  9.98 us (2%)
  other arithmetic  9.78 us (2%)
    all_to_all x3, waiting for transfers between devices, exchange(): lax.all_to_all(values, 'seq', split_axis=0, concat_axis=0, tiled=True)  113 us
    all_gather x1, waiting for transfers between devices, on_device(): up_full = lax.all_gather(w_in_up, 'fsdp', axis=0, tiled=True)  45.2 us
    all_gather x1, waiting for transfers between devices, on_device(): down_full = lax.all_gather(w_in_down, 'fsdp', axis=1, tiled=True)  42.8 us
    all_gather x1, waiting for transfers between devices, on_device(): gate_full = lax.all_gather(w_in_gate, 'fsdp', axis=0, tiled=True)  38.7 us
    all_to_all x3, starting transfers between devices, exchange(): lax.all_to_all(values, 'seq', split_axis=0, concat_axis=0, tiled=True)  30.9 us
    all_to_all x1, blocking collectives, exchange(): lax.all_to_all(values, 'seq', split_axis=0, concat_axis=0, tiled=True)  29.6 us
    all_gather x1, waiting for transfers between devices, on_device(): encoded = lax.all_gather(encoded_rows, 'seq', axis=0, tiled=True)  26 us
    pallas_call x1, Pallas kernels, call_backward(): pl.pallas_call(backward, grid=(SEQ // ROWS,), in_specs=[pl.BlockSpec(memo...  21 us
  transfers between devices with their start and end apart: 11, of which 9 were waited for; matrix products, arithmetic and copies ran while one was open for 3% of the time, Pallas kernels for 6%

profile of v1, /device:TPU:33, one launch (start us, length us, event | category | flops | bytes accessed | tf_op | source)
XLA Modules:
  0.0 448.9 jit_solution(1654853869544809633)
XLA Ops:
  7.2 0.7 all-gather.7.cloned.1.call-update
  8.0 0.7 all-gather.11.cloned.1.call-update
  8.7 0.7 all-gather.9.cloned.1.call-update
  9.4 2.1 fusion.1
  11.5 38.7 %all-gather.7.cloned.1.call-done = bf16[4096,256]{1,0:T(8,128)(2,1)} async-done(((bf16[512,256]{1,0:T(8,128)(2,1)}), bf16[4096,256]{1,0:T(8,128)(2,1)}) %all-gather.7.cloned.1.call-update) | async-done | bytes 2097168 | tf_op jit(solution)/shard_map/all_gather | solution.py:219
  50.2 2.4 fusion.20
  52.6 42.8 %all-gather.11.cloned.1.call-done = bf16[256,4096]{1,0:T(8,128)(2,1)} async-done(((bf16[256,512]{1,0:T(8,128)(2,1)}), bf16[256,4096]{1,0:T(8,128)(2,1)}) %all-gather.11.cloned.1.call-update) | async-done | bytes 2097168 | tf_op jit(solution)/shard_map/all_gather | solution.py:221
  95.4 45.2 %all-gather.9.cloned.1.call-done = bf16[4096,256]{1,0:T(8,128)(2,1)} async-done(((bf16[512,256]{1,0:T(8,128)(2,1)}), bf16[4096,256]{1,0:T(8,128)(2,1)}) %all-gather.9.cloned.1.call-update) | async-done | bytes 2097168 | tf_op jit(solution)/shard_map/all_gather | solution.py:220
  140.6 6.0 %fusion = bf16[32,8,4096]{2,1,0:T(8,128)(2,1)} fusion(bf16[256,4096]{1,0:T(8,128)(2,1)} %all-gather.11.cloned.1.call-done, f32[256,256]{1,0:T(8,128)S(1)} %fusion.20, bf16[4096,256]{1,0:T(8,128)(2,1)} %all-gather.9.cloned.1.call-done, bf16[1,256,4096]{2,1,0:T(8,128)(2,1)S(1)} %copy-done.3, f32[4096]{0:T(1024)S(1)} %copy-done.7, f32[256]{0:T(256)S(1)} %add_rsqrt_fusion), kind=kOutput, calls=%fused_computation.3 | convolution fusion | flops 1079115776 | bytes 8668160 | tf_op jit(solution)/shard_map/dot_general | solution.py:26
  146.6 15.5 %all-to-all-start.1 = ((bf16[32,8,4096]{2,1,0:T(8,128)(2,1)}), bf16[32,8,4096]{2,1,0:T(8,128)(2,1)}, u32[]{:S(2)}, u32[]{:S(2)}) async-start(bf16[32,8,4096]{2,1,0:T(8,128)(2,1)} %fusion), calls=%async_computation.1 | async-start | bytes 4194304 | tf_op jit(solution)/shard_map/all_to_all | solution.py:207
  162.1 0.0 all-gather.15.cloned.1.call-start
  162.1 0.5 all-gather.15.cloned.1.call-update
  162.7 59.7 %all-to-all-done.1 = bf16[32,8,4096]{2,1,0:T(8,128)(2,1)} async-done(((bf16[32,8,4096]{2,1,0:T(8,128)(2,1)}), bf16[32,8,4096]{2,1,0:T(8,128)(2,1)}, u32[]{:S(2)}, u32[]{:S(2)}) %all-to-all-start.1) | async-done | bytes 2097184 | tf_op jit(solution)/shard_map/all_to_all | solution.py:207
  222.4 1.9 convert_reduce_fusion
  224.3 0.2 multiply_reduce_fusion.1
  224.5 0.7 multiply_convert_fusion
  225.2 0.5 all-gather.17.cloned.1.call-update
  225.8 0.1 copy.36
  226.0 0.1 copy.29
  226.1 0.1 copy.37
  226.3 0.1 copy.30
  226.4 0.6 copy-done.6
  227.0 0.1 copy.38
  227.2 0.1 copy.31
  227.3 1.2 pad_maximum_fusion
  228.5 5.2 %all-to-all-start = ((bf16[32,192,128]{2,1,0:T(8,128)(2,1)}), bf16[32,192,128]{2,1,0:T(8,128)(2,1)S(1)}, u32[]{:S(2)}, u32[]{:S(2)}) async-start(bf16[32,192,128]{2,1,0:T(8,128)(2,1)} %pad_maximum_fusion), calls=%async_computation | async-start | bytes 3145728 | tf_op jit(solution)/shard_map/all_to_all | solution.py:207
  234.4 33.5 %all-to-all-done = bf16[32,192,128]{2,1,0:T(8,128)(2,1)S(1)} async-done(((bf16[32,192,128]{2,1,0:T(8,128)(2,1)}), bf16[32,192,128]{2,1,0:T(8,128)(2,1)S(1)}, u32[]{:S(2)}, u32[]{:S(2)}) %all-to-all-start) | async-done | bytes 1572896 | tf_op jit(solution)/shard_map/all_to_all | solution.py:207
  267.9 0.1 fusion.26
  268.1 26.0 %all-gather.13.cloned.1.call-done = bf16[256,4096]{1,0:T(8,128)(2,1)} async-done(((bf16[8,4096]{1,0:T(8,128)(2,1)}), bf16[256,4096]{1,0:T(8,128)(2,1)}) %all-gather.13.cloned.1.call-update) | async-done | bytes 2097168 | tf_op jit(solution)/shard_map/all_gather | solution.py:240
  294.1 2.5 convolution_convert_fusion.2
  296.6 0.3 collective-permute-start
  296.9 17.3 %image_forward.1 = (bf16[2,2048,2048]{2,1,0:T(8,128)(2,1)}, f32[2048,128]{1,0:T(8,128)S(1)}, f32[2048,128]{1,0:T(8,128)S(1)}, f32[2048,128]{1,0:T(8,128)S(1)}) custom-call(bf16[2048,128]{1,0:T(8,128)(2,1)S(1)} %bitcast.94, bf16[2048,128]{1,0:T(8,128)(2,1)S(1)} %bitcast.101, bf16[2048,128]{1,0:T(8,128)(2,1)S(1)} %bitcast.99), custom_call_target="tpu_custom_call" | custom-call | flops 8589934592 | bytes 20000000 | tf_op jit(solution)/shard_map/image_forward/pallas_call | solution.py:158
  314.2 0.1 fusion.27
  314.4 0.1 pad_maximum_fusion.4.v_ref.vt_ref
  314.5 0.1 pad_maximum_fusion.3.k_ref.kt_ref
  314.6 0.7 copy-done.1
  315.3 8.8 %text_forward.1 = (bf16[2048,128]{1,0:T(8,128)(2,1)S(1)}, bf16[2,2048,256]{2,1,0:T(8,128)(2,1)}, f32[2048,128]{1,0:T(8,128)S(1)}, f32[2048,128]{1,0:T(8,128)S(1)}) custom-call(s32[1]{0:T(128)S(6)} %copy.47.len_ref, bf16[2048,128]{1,0:T(8,128)(2,1)S(1)} %bitcast.95, bf16[256,128]{1,0:T(8,128)(2,1)S(1)} %pad_maximum_fusion.3.k_ref.kt_ref, ...), custom_call_target="tpu_custom_call" | custom-call | tf_op jit(solution)/shard_map/text_forward/pallas_call | solution.py:172
  324.1 1.1 copy-done
  325.2 29.6 %all_to_all.20 = bf16[32,64,128]{2,1,0:T(8,128)(2,1)S(1)} all-to-all(bf16[32,64,128]{2,1,0:T(8,128)(2,1)S(1)} %bitcast.97), channel_id=1, replica_groups=mesh['seq'=32,'fsdp'=8] {'seq'}, dimensions={0} | all-to-all | bytes 1048576 | tf_op jit(solution)/shard_map/all_to_all | solution.py:207
  354.8 1.1 copy.33
  356.0 13.4 %all-gather.17.cloned.1.call-done = bf16[2048,1280]{1,0:T(8,128)(2,1)} async-done(((bf16[256,1280]{1,0:T(8,128)(2,1)}), bf16[2048,1280]{1,0:T(8,128)(2,1)}) %all-gather.17.cloned.1.call-update) | async-done | bytes 5242896 | tf_op jit(solution)/shard_map/all_gather | solution.py:223
  369.4 3.8 multiply_reduce_fusion
  373.2 0.5 copy-done.2
  373.7 1.8 fusion.5
  375.5 0.1 copy.40
  375.7 0.9 copy.34
  376.6 0.1 reduce_sum.63
  376.7 0.1 reduce_sum.64
  376.9 0.1 select_maximum_fusion
  377.0 2.0 pad_maximum_fusion.2
  378.9 10.3 %all-to-all-start.3 = ((bf16[32,80,128]{2,1,0:T(8,128)(2,1)}), bf16[32,80,128]{2,1,0:T(8,128)(2,1)}, u32[]{:S(2)}, u32[]{:S(2)}) async-start(bf16[32,80,128]{2,1,0:T(8,128)(2,1)} %pad_maximum_fusion.2), calls=%async_computation.3 | async-start | bytes 1310720 | tf_op jit(solution)/shard_map/all_to_all | solution.py:207
  390.0 0.6 fusion.29
  390.5 19.7 %all-to-all-done.3 = bf16[32,80,128]{2,1,0:T(8,128)(2,1)} async-done(((bf16[32,80,128]{2,1,0:T(8,128)(2,1)}), bf16[32,80,128]{2,1,0:T(8,128)(2,1)}, u32[]{:S(2)}, u32[]{:S(2)}) %all-to-all-start.3) | async-done | bytes 655392 | tf_op jit(solution)/shard_map/all_to_all | solution.py:207
  410.2 0.9 fusion.23
  411.1 0.1 reduce_sum.66
  411.2 0.6 fusion.30
  414.4 1.1 slice.72
  415.5 21.0 %backward.1 = (bf16[128,2048]{1,0:T(8,128)(2,1)S(1)}, bf16[128,2048]{1,0:T(8,128)(2,1)S(1)}, bf16[128,2048]{1,0:T(8,128)(2,1)S(1)}) custom-call(f32[1]{0:T(128)} %bitcast.25.coef_ref, bf16[2048,128]{1,0:T(8,128)(2,1)S(1)} %bitcast.96, bf16[2048,128]{1,0:T(8,128)(2,1)S(1)} %bitcast.98, bf16[2048,128]{1,0:T(8,128)(2,1)S(1)} %get-tuple-element.18.att_ref, ...), custom_call_target="tpu_custom_call" | custom-call | tf_op jit(solution)/shard_map/backward/pallas_call | solution.py:187
  436.5 0.2 pad_maximum_fusion.1
  436.7 0.1 constant_dynamic-slice_fusion
  436.8 0.8 collective-permute-start.1
  437.7 1.8 collective-permute-done.1
  439.6 0.2 fusion.4
  439.8 1.2 fusion.25
  (35 shorter events, 0.5 us)
Async XLA Ops:
  7.2 43.0 %copy-start.3 = (bf16[1,256,4096]{2,1,0:T(8,128)(2,1)S(1)}, bf16[1,256,4096]{2,1,0:T(8,128)(2,1)}, u32[]{:S(2)}) copy-start(bf16[1,256,4096]{2,1,0:T(8,128)(2,1)} %param.15) | copy-start | bytes 6291460
  7.2 43.0 %copy-start.7 = (f32[4096]{0:T(1024)S(1)}, f32[4096]{0:T(1024)}, u32[]{:S(2)}) copy-start(f32[4096]{0:T(1024)} %param.19) | copy-start | bytes 49156
  7.2 43.0 %all-gather.7.cloned.1.call-start = ((), (), s32[]{:S(2)}) async-start(), calls=%async_computation.4 | async-start | bytes 2359296 | tf_op jit(solution)/shard_map/all_gather | solution.py:219
  7.9 87.5 %all-gather.11.cloned.1.call-start = ((), (), s32[]{:S(2)}) async-start(), calls=%async_computation.6 | async-start | bytes 2359296 | tf_op jit(solution)/shard_map/all_gather | solution.py:221
  8.7 131.9 %all-gather.9.cloned.1.call-start = ((), (), s32[]{:S(2)}) async-start(), calls=%async_computation.5 | async-start | bytes 2359296 | tf_op jit(solution)/shard_map/all_gather | solution.py:220
  146.6 75.8 %all-to-all-start.1 = ((bf16[32,8,4096]{2,1,0:T(8,128)(2,1)}), bf16[32,8,4096]{2,1,0:T(8,128)(2,1)}, u32[]{:S(2)}, u32[]{:S(2)}) async-start(bf16[32,8,4096]{2,1,0:T(8,128)(2,1)} %fusion), calls=%async_computation.1 | async-start | bytes 4194304 | tf_op jit(solution)/shard_map/all_to_all | solution.py:207
  162.0 62.4 %copy-start.8 = (f32[4096]{0:T(1024)S(1)}, f32[4096]{0:T(1024)}, u32[]{:S(2)}) copy-start(f32[4096]{0:T(1024)} %param.23) | copy-start | bytes 49156
  162.0 63.7 %copy-start.4 = (bf16[1,2,64,2048]{3,2,1,0:T(8,128)(2,1)S(1)}, bf16[1,2,64,2048]{3,2,1,0:T(8,128)(2,1)}, u32[]{:S(2)}) copy-start(bf16[1,2,64,2048]{3,2,1,0:T(8,128)(2,1)} %param.25) | copy-start | bytes 1572868
  162.1 106.0 %all-gather.15.cloned.1.call-start = ((), (), s32[]{:S(2)}) async-start(), calls=%async_computation.8 | async-start | bytes 1179648 | tf_op jit(solution)/shard_map/all_gather | solution.py:222
  162.6 131.4 %all-gather.13.cloned.1.call-start = ((), (), s32[]{:S(2)}) async-start(), calls=%async_computation.7 | async-start | bytes 2162688 | tf_op jit(solution)/shard_map/all_gather | solution.py:240
  224.4 1.7 copy-start.5
  225.2 144.2 %all-gather.17.cloned.1.call-start = ((), (), s32[]{:S(2)}) async-start(), calls=%async_computation.9 | async-start | bytes 5898240 | tf_op jit(solution)/shard_map/all_gather | solution.py:223
  225.9 1.0 copy-start.6
  228.5 39.4 %all-to-all-start = ((bf16[32,192,128]{2,1,0:T(8,128)(2,1)}), bf16[32,192,128]{2,1,0:T(8,128)(2,1)S(1)}, u32[]{:S(2)}, u32[]{:S(2)}) async-start(bf16[32,192,128]{2,1,0:T(8,128)(2,1)} %pad_maximum_fusion), calls=%async_computation | async-start | bytes 3145728 | tf_op jit(solution)/shard_map/all_to_all | solution.py:207
  296.6 17.6 %collective-permute-start = (bf16[256,128]{1,0:T(8,128)(2,1)S(1)}, bf16[256,128]{1,0:T(8,128)(2,1)S(1)}, u32[]{:S(2)}, u32[]{:S(2)}) collective-permute-start(bf16[256,128]{1,0:T(8,128)(2,1)S(1)} %convolution_convert_fusion.2), channel_id=1, source_target_pairs={{0,8},{8,0},{16,24},{24,16},{32,40},{40,32},{48,56},{56,48},{64,72... | collective-permute-start | bytes 196616 | tf_op jit(solution)/shard_map/ppermute | solution.py:211
  314.2 1.1 copy-start.1
  324.1 1.1 copy-start
  369.4 4.3 copy-start.2
  375.7 14.2 %copy-start.9 = (f32[1,2]{1,0:T(1,128)S(1)}, f32[1,2]{1,0:T(1,128)}, u32[]{:S(2)}) copy-start(f32[1,2]{1,0:T(1,128)} %param.18) | copy-start | bytes 28
  378.9 31.3 %all-to-all-start.3 = ((bf16[32,80,128]{2,1,0:T(8,128)(2,1)}), bf16[32,80,128]{2,1,0:T(8,128)(2,1)}, u32[]{:S(2)}, u32[]{:S(2)}) async-start(bf16[32,80,128]{2,1,0:T(8,128)(2,1)} %pad_maximum_fusion.2), calls=%async_computation.3 | async-start | bytes 1310720 | tf_op jit(solution)/shard_map/all_to_all | solution.py:207
  436.8 2.7 collective-permute-start.1
Sparse Core Ops, SparseCore 0:
  9.8 40.3 all-gather.6
  52.0 43.3 all-gather.10
  97.2 43.3 all-gather.8
  164.4 50.0 all-gather.14
  225.3 68.6 all-gather.12
  295.7 73.6 all-gather.16

commit v2 on v1

--- a/solution.py
+++ b/solution.py
@@ -26,11 +26,6 @@
     return lax.dot_general(a, b, dims, preferred_element_type=jnp.float32)
 
 
-def rms_gain(values, gain):
-    mean_sq = jnp.mean(values * values, axis=-1, keepdims=True)
-    return values * lax.rsqrt(mean_sq + norm_eps) * gain
-
-
 def noise_level(step_index):
     fraction = (step_index.astype(jnp.float32) + 1.0) / 1000.0
     return 3.0 * fraction / (1.0 + 2.0 * fraction)
@@ -49,21 +44,311 @@
     return jnp.where(head_lanes(0), first, second)
 
 
-def image_forward(q_ref, k_ref, v_ref, e_ref, o_ref, z_ref, m_ref):
-    q = q_ref[...] * jnp.asarray(1.0 / math.sqrt(HEAD), jnp.bfloat16)
-    v_aug = with_ones(v_ref[...])
+def image_rows(q, k, v_aug, e_ref):
+    q = q * jnp.asarray(1.0 / math.sqrt(HEAD), jnp.bfloat16)
     outs, tops = [], []
     for j in range(2):
         qj = jnp.where(head_lanes(j), q, jnp.zeros_like(q))
-        s = dot(qj, k_ref[...], NT)
+        s = dot(qj, k, NT)
         top = jnp.max(s, axis=-1, keepdims=True)
         e = jnp.exp(s - top).astype(jnp.bfloat16)
         e_ref[j] = e
         outs.append(dot(e, v_aug))
         tops.append(top)
-    o_ref[...] = by_head(outs[0][:, :LANES], outs[1][:, :LANES])
-    z_ref[...] = by_head(outs[0][:, LANES:], outs[1][:, LANES:])
-    m_ref[...] = by_head(tops[0], tops[1])
+    return (
+        by_head(outs[0][:, :LANES], outs[1][:, :LANES]),
+        by_head(outs[0][:, LANES:], outs[1][:, LANES:]),
+        by_head(tops[0], tops[1]),
+    )
+
+
+def place():
+    seat, pair = lax.axis_index("seq"), lax.axis_index("fsdp")
+    chip = seat // 2
+    return seat, lax.rem(seat, 2), lax.rem(chip, 4), chip // 4, pair, lax.rem(pair, 4), pair // 4
+
+
+def remote(src, dst, send_sem, recv_sem, seat, pair):
+    return pltpu.make_async_remote_copy(
+        src_ref=src, dst_ref=dst, send_sem=send_sem, recv_sem=recv_sem,
+        device_id=(seat, pair), device_id_type=pl.DeviceIdType.MESH,
+    )
+
+
+def arrived(ref, sem):
+    pltpu.make_async_copy(ref, ref, sem).wait()
+
+
+def greet_seats(barrier, seat, pair):
+    @pl.loop(1, 32)
+    def _(d):
+        pl.semaphore_signal(barrier, inc=1, device_id=(lax.rem(seat + d, 32), pair), device_id_type=pl.DeviceIdType.MESH)
+
+
+def encode_and_exchange(
+    prompt_ref, gain_in_ref, gain_out_ref, gate_in, up_in, down_in, ctx_in, q_in, k_in, v_in,
+    q_ref, k_ref, v_ref, e_ref, o_ref, z_ref, m_ref, kt_ref, vt_ref,
+    gate_buf, up_buf, down_buf, ctx_buf, normed, gate_acc, up_acc, part, sib, half, from_x, sum_x, from_z, state, ctx_pair,
+    e_tile, w_local, w_send, w_recv, qkv_local, qkv_send, qkv_recv, e_sem, stage_send, stage_recv,
+):
+    seat, core, x, zh, pair, y, zl = place()
+    other = seat + 1 - 2 * core
+    up_y, down_y = lax.rem(y + 1, 4), lax.rem(y + 3, 4)
+    far = lax.rem(y + 2, 4)
+    base, base_p = zl * 4, (1 - zl) * 4
+    partner = base_p + y
+
+    barrier = pltpu.get_barrier_semaphore()
+    greet_seats(barrier, seat, pair)
+    for peer in (partner, base + up_y, base + down_y):
+        pl.semaphore_signal(barrier, inc=1, device_id=(seat, peer), device_id_type=pl.DeviceIdType.MESH)
+    pl.semaphore_wait(barrier, 34)
+
+    weights = ((gate_in, gate_buf), (up_in, up_buf), (down_in, down_buf), (ctx_in, ctx_buf))
+
+    def send_weight(w, src, dst, sem, peer):
+        remote(src, dst, w_send.at[w], w_recv.at[w, sem], seat, peer).start()
+
+    for w, (src, buf) in enumerate(weights):
+        send_weight(w, src, buf.at[pair], 0, partner)
+        send_weight(w, src, buf.at[pair], 1, base + up_y)
+        send_weight(w, src, buf.at[pair], 2, base + down_y)
+        pltpu.make_async_copy(src, buf.at[pair], w_local.at[w]).start()
+
+    images = ((q_in, q_ref), (k_in, k_ref), (v_in, v_ref))
+    here = pl.ds(pl.multiple_of(seat * 64, 64), 64)
+    for i, (src, dst) in enumerate(images):
+
+        @pl.loop(1, 32)
+        def _(d, i=i, src=src, dst=dst):
+            to = lax.rem(seat + d, 32)
+            columns = pl.ds(pl.multiple_of((to // 2) * LANES, LANES), LANES)
+            remote(src.at[lax.rem(to, 2), :, columns], dst.at[here, :], qkv_send.at[i], qkv_recv.at[i], to, pair).start()
+
+        own = pl.ds(pl.multiple_of((seat // 2) * LANES, LANES), LANES)
+        pltpu.make_async_copy(src.at[core, :, own], dst.at[here, :], qkv_local.at[i]).start()
+
+    total = jnp.zeros((PROMPT, 1), jnp.float32)
+    for f in range(8):
+        rows = prompt_ref[:, 512 * f:512 * (f + 1)].astype(jnp.float32)
+        total = total + jnp.sum(rows * rows, axis=-1, keepdims=True)
+    inv = lax.rsqrt(total * (1.0 / 4096) + norm_eps)
+    for f in range(8):
+        cols = slice(512 * f, 512 * (f + 1))
+        normed[f] = (prompt_ref[:, cols].astype(jnp.float32) * inv * gain_in_ref[:, cols]).astype(jnp.bfloat16)
+
+    def first_half(buf, slot):
+        return buf.at[slot, pl.ds(0, buf.shape[1] // 2)]
+
+    def second_half(buf, slot):
+        return buf.at[slot, pl.ds(buf.shape[1] // 2, buf.shape[1] // 2)]
+
+    for w, (_, buf) in enumerate(weights):
+        arrived(buf.at[partner], w_recv.at[w, 0])
+        send_weight(w, buf.at[partner], buf.at[partner], 3, base + up_y)
+        send_weight(w, buf.at[partner], buf.at[partner], 4, base + down_y)
+        arrived(buf.at[base + down_y], w_recv.at[w, 1])
+        send_weight(w, first_half(buf, base + down_y), first_half(buf, base + down_y), 5, base + up_y)
+        arrived(buf.at[base + up_y], w_recv.at[w, 2])
+        send_weight(w, second_half(buf, base + up_y), second_half(buf, base + up_y), 6, base + down_y)
+    for w, (_, buf) in enumerate(weights):
+        arrived(buf.at[base_p + down_y], w_recv.at[w, 3])
+        send_weight(w, first_half(buf, base_p + down_y), first_half(buf, base_p + down_y), 7, base + up_y)
+        arrived(buf.at[base_p + up_y], w_recv.at[w, 4])
+        send_weight(w, second_half(buf, base_p + up_y), second_half(buf, base_p + up_y), 8, base + down_y)
+
+    def weight_ready(w):
+        buf = weights[w][1]
+        arrived(first_half(buf, base + far), w_recv.at[w, 5])
+        arrived(second_half(buf, base + far), w_recv.at[w, 6])
+        arrived(first_half(buf, base_p + far), w_recv.at[w, 7])
+        arrived(second_half(buf, base_p + far), w_recv.at[w, 8])
+        pltpu.make_async_copy(weights[w][0], buf.at[pair], w_local.at[w]).wait()
+
+    for i, (src, dst) in enumerate(images):
+        arrived(dst.at[pl.ds(0, 31 * 64), :], qkv_recv.at[i])
+        arrived(dst.at[pl.ds(0, 64), :], qkv_local.at[i])
+
+    blocks = SEQ // ROWS
+
+    def out_copy(b):
+        slot = lax.rem(b, 2)
+        return pltpu.make_async_copy(e_tile.at[slot], e_ref.at[:, pl.ds(pl.multiple_of(b * ROWS, ROWS), ROWS), :], e_sem.at[slot])
+
+    @pl.loop(0, blocks)
+    def _(b):
+        @pl.when(b >= 2)
+        def _():
+            out_copy(b - 2).wait()
+
+        rows = pl.ds(pl.multiple_of(b * ROWS, ROWS), ROWS)
+        o, z, m = image_rows(q_ref[rows, :], k_ref[...], with_ones(v_ref[...]), e_tile.at[lax.rem(b, 2)])
+        o_ref[rows, :], z_ref[rows, :], m_ref[rows, :] = o, z, m
+        out_copy(b).start()
+
+    weight_ready(0)
+    weight_ready(1)
+    gate_acc[...] = jnp.zeros_like(gate_acc)
+    up_acc[...] = jnp.zeros_like(up_acc)
+
+    @pl.loop(0, 8)
+    def _(f):
+        gate_acc[...] += dot(normed[f], gate_buf[f])
+        up_acc[...] += dot(normed[f], up_buf[f])
+
+    hidden = (jax.nn.gelu(gate_acc[...], approximate=True) * up_acc[...]).astype(jnp.bfloat16)
+    weight_ready(2)
+
+    def part_block(f):
+        part[f] = dot(hidden, down_buf[f]).astype(jnp.bfloat16)
+
+    @pl.loop(0, 4)
+    def _(i):
+        part_block((1 - core) * 4 + i)
+
+    to_other = remote(part.at[pl.ds((1 - core) * 4, 4)], sib, stage_send.at[0], stage_recv.at[0], other, pair)
+    to_other.start()
+
+    @pl.loop(0, 4)
+    def _(i):
+        part_block(core * 4 + i)
+
+    to_other.wait()
+    for i in range(4):
+        half[i] = (part[core * 4 + i].astype(jnp.float32) + sib[i].astype(jnp.float32)).astype(jnp.bfloat16)
+
+    def seat_of(zh_to, x_to):
+        return (zh_to * 4 + x_to) * 2 + core
+
+    def rows_x(at):
+        return pl.ds(pl.multiple_of(at * 64, 64), 64)
+
+    def rows_z(at):
+        return pl.ds(pl.multiple_of(at * 16, 16), 16)
+
+    def round_of(stage, make):
+        copies = [make(d, stage_send.at[stage + d], stage_recv.at[stage + d]) for d in (1, 2, 3)]
+        for copy in copies:
+            copy.start()
+        for copy in copies:
+            copy.wait()
+
+    round_of(0, lambda d, s, r: remote(
+        half.at[:, rows_x(lax.rem(x + d, 4)), :], from_x.at[d], s, r, seat_of(zh, lax.rem(x + d, 4)), pair))
+    for i in range(4):
+        acc = half[i, rows_x(x), :].astype(jnp.float32)
+        for d in (1, 2, 3):
+            acc = acc + from_x[d, i].astype(jnp.float32)
+        sum_x[i] = acc.astype(jnp.bfloat16)
+    round_of(3, lambda d, s, r: remote(
+        sum_x.at[:, rows_z(lax.rem(zh + d, 4)), :], from_z.at[d], s, r, seat_of(lax.rem(zh + d, 4), x), pair))
+    mine = rows_z(x * 4 + zh)
+    for i in range(4):
+        columns = pl.ds(pl.multiple_of(core * 2048 + i * 512, 512), 512)
+        acc = prompt_ref[mine, columns].astype(jnp.float32) + sum_x[i, rows_z(zh), :].astype(jnp.float32)
+        for d in (1, 2, 3):
+            acc = acc + from_z[d, i].astype(jnp.float32)
+        state[core * 4 + i, mine, :] = acc.astype(jnp.bfloat16)
+    ours = pl.ds(core * 4, 4)
+    round_of(6, lambda d, s, r: remote(
+        state.at[ours, mine, :], state.at[ours, mine, :], s, r, seat_of(lax.rem(zh + d, 4), x), pair))
+    round_of(9, lambda d, s, r: remote(
+        state.at[ours, rows_x(x), :], state.at[ours, rows_x(x), :], s, r, seat_of(zh, lax.rem(x + d, 4)), pair))
+    last = remote(state.at[ours], state.at[ours], stage_send.at[13], stage_recv.at[13], other, pair)
+    last.start()
+    weight_ready(3)
+    last.wait()
+
+    total = jnp.zeros((PROMPT, 1), jnp.float32)
+    for f in range(8):
+        rows = state[f].astype(jnp.float32)
+        total = total + jnp.sum(rows * rows, axis=-1, keepdims=True)
+    inv = lax.rsqrt(total * (1.0 / 4096) + norm_eps)
+    context = jnp.zeros((PROMPT, LANES), jnp.float32)
+    for f in range(8):
+        encoded = (state[f].astype(jnp.float32) * inv * gain_out_ref[:, 512 * f:512 * (f + 1)]).astype(jnp.bfloat16)
+        context = context + dot(encoded, ctx_buf[f])
+    ctx_pair[core] = context.astype(jnp.bfloat16)
+    give = remote(ctx_pair.at[core], ctx_pair.at[core], stage_send.at[14], stage_recv.at[14], other, pair)
+    give.start()
+    give.wait()
+    first, second = ctx_pair[0].astype(jnp.float32), ctx_pair[1].astype(jnp.float32)
+    kt_ref[...] = by_head(first, pltpu.roll(second, HEAD, 1)).astype(jnp.bfloat16)
+    vt_ref[...] = by_head(pltpu.roll(first, HEAD, 1), second).astype(jnp.bfloat16)
+
+    out_copy(blocks - 2).wait()
+    out_copy(blocks - 1).wait()
+    for w, (_, buf) in enumerate(weights):
+        arrived(buf.at[pl.ds(0, 7)], w_send.at[w])
+    for i, (_, dst) in enumerate(images):
+        arrived(dst.at[pl.ds(0, 31 * 64), :], qkv_send.at[i])
+
+
+def project_and_exchange(att_ref, w_ref, target_ref, g_ref, err_ref, tok, resid, grad, err_all,
+                         tok_local, tok_send, tok_recv, g_local, g_send, g_recv, e_send, e_recv):
+    seat, core, _, _, pair, _, _ = place()
+    barrier = pltpu.get_barrier_semaphore()
+    greet_seats(barrier, seat, pair)
+    pl.semaphore_wait(barrier, 31)
+
+    def token_rows(to):
+        return pl.ds(pl.multiple_of(to * 64, 64), 64)
+
+    def lanes_of(to):
+        return pl.ds(pl.multiple_of((to // 2) * LANES, LANES), LANES)
+
+    def stream_rows(to):
+        return pl.ds(pl.multiple_of(lax.rem(to, 2) * 64, 64), 64)
+
+    spot = tok.at[stream_rows(seat), lanes_of(seat)]
+
+    @pl.loop(1, 32)
+    def _(d):
+        to = lax.rem(seat + d, 32)
+        remote(att_ref.at[token_rows(to), :], spot, tok_send, tok_recv, to, pair).start()
+
+    keep = pltpu.make_async_copy(att_ref.at[token_rows(seat), :], spot, tok_local)
+    keep.start()
+    keep.wait()
+    arrived(att_ref.at[pl.ds(0, 31 * 64), :], tok_recv)
+
+    @pl.loop(0, CH // 256)
+    def _(n):
+        columns = pl.ds(pl.multiple_of(n * 256, 256), 256)
+        resid[:, columns] = dot(tok[...], w_ref[:, columns]) - target_ref[:, columns].astype(jnp.float32)
+
+    halves = []
+    for stream in range(2):
+        rows = resid[64 * stream:64 * (stream + 1), :]
+        halves.append(jnp.sum(jnp.sum(rows * rows, axis=1, keepdims=True), axis=0, keepdims=True))
+    row = lax.broadcasted_iota(jnp.int32, (8, LANES), 0)
+    err_all[seat] = jnp.where(row == 0, halves[0], jnp.where(row == 1, halves[1], 0.0))
+
+    @pl.loop(1, 32)
+    def _(d):
+        remote(err_all.at[seat], err_all.at[seat], e_send, e_recv, lax.rem(seat + d, 32), pair).start()
+
+    rounded = resid[...].astype(jnp.bfloat16)
+
+    @pl.loop(0, 2048 // 256)
+    def _(n):
+        columns = pl.ds(pl.multiple_of(n * 256, 256), 256)
+        grad[:, columns] = dot(rounded, w_ref[columns, :], NT).astype(jnp.bfloat16)
+
+    @pl.loop(1, 32)
+    def _(d):
+        to = lax.rem(seat + d, 32)
+        remote(grad.at[stream_rows(to), lanes_of(to)], g_ref.at[token_rows(seat), :], g_send, g_recv, to, pair).start()
+
+    keep = pltpu.make_async_copy(grad.at[stream_rows(seat), lanes_of(seat)], g_ref.at[token_rows(seat), :], g_local)
+    keep.start()
+    keep.wait()
+    arrived(err_all.at[pl.ds(0, 31)], e_recv)
+    err_ref[...] = jnp.sum(err_all[...], axis=0)
+    arrived(g_ref.at[pl.ds(0, 31 * 64), :], g_recv)
+    arrived(g_ref.at[pl.ds(0, 31 * 64), :], g_send)
+    arrived(att_ref.at[pl.ds(0, 31 * 64), :], tok_send)
+    arrived(err_all.at[pl.ds(0, 31)], e_send)
 
 
 def text_forward(len_ref, q_ref, k_ref, v_ref, o_ref, z_ref, m_ref, att_ref, e_ref, si_ref, st_ref):
@@ -153,18 +438,49 @@
     return pltpu.CompilerParams(vmem_limit_bytes=48 * 1024 * 1024)
 
 
-def call_image_forward(q, k, v):
-    f32 = lambda: jax.ShapeDtypeStruct((SEQ, LANES), jnp.float32)
+def call_encode(prompt, gain_in, gain_out, gate, up, down, ctx, q, k, v):
+    bf16, f32 = jnp.bfloat16, jnp.float32
+    anywhere, vmem = pl.BlockSpec(memory_space=pl.ANY), pl.BlockSpec(memory_space=pltpu.VMEM)
+    shape = jax.ShapeDtypeStruct
+    dma = pltpu.SemaphoreType.DMA
     return pl.pallas_call(
-        image_forward,
-        grid=(SEQ // ROWS,),
-        in_specs=[rows_of(LANES), whole(SEQ, LANES), whole(SEQ, LANES)],
-        out_specs=[pl.BlockSpec((2, ROWS, SEQ), lambda i: (0, i, 0)), rows_of(LANES), rows_of(LANES), rows_of(LANES)],
-        out_shape=[jax.ShapeDtypeStruct((2, SEQ, SEQ), jnp.bfloat16), f32(), f32(), f32()],
-        compiler_params=params(),
-        cost_estimate=pl.CostEstimate(flops=4 * 2 * SEQ * SEQ * 256, bytes_accessed=20_000_000, transcendentals=2 * SEQ * SEQ),
-        name="image_forward",
-    )(q, k, v)
+        encode_and_exchange,
+        in_specs=[vmem] * 3 + [anywhere] * 7,
+        out_specs=[vmem] * 3 + [anywhere] + [vmem] * 5,
+        out_shape=[shape((SEQ, LANES), bf16)] * 3 + [shape((2, SEQ, SEQ), bf16)] + [shape((SEQ, LANES), f32)] * 3
+        + [shape((PROMPT, LANES), bf16)] * 2,
+        scratch_shapes=[
+            pltpu.VMEM((8, 512, 256), bf16), pltpu.VMEM((8, 512, 256), bf16), pltpu.VMEM((8, 256, 512), bf16),
+            pltpu.VMEM((8, 512, 128), bf16), pltpu.VMEM((8, PROMPT, 512), bf16), pltpu.VMEM((PROMPT, 256), f32),
+            pltpu.VMEM((PROMPT, 256), f32), pltpu.VMEM((8, PROMPT, 512), bf16), pltpu.VMEM((4, PROMPT, 512), bf16),
+            pltpu.VMEM((4, PROMPT, 512), bf16), pltpu.VMEM((4, 4, 64, 512), bf16), pltpu.VMEM((4, 64, 512), bf16),
+            pltpu.VMEM((4, 4, 16, 512), bf16), pltpu.VMEM((8, PROMPT, 512), bf16), pltpu.VMEM((2, PROMPT, LANES), bf16),
+            pltpu.VMEM((2, 2, ROWS, SEQ), bf16),
+            dma((4,)), dma((4,)), dma((4, 9)), dma((3,)), dma((3,)), dma((3,)), dma((2,)), dma((15,)), dma((15,)),
+        ],
+        compiler_params=pltpu.CompilerParams(collective_id=0, has_side_effects=True, vmem_limit_bytes=56 * 1024 * 1024),
+        cost_estimate=pl.CostEstimate(flops=20_000_000_000, bytes_accessed=40_000_000, transcendentals=2 * SEQ * SEQ),
+        name="encode_and_exchange",
+    )(prompt, gain_in, gain_out, gate, up, down, ctx, q, k, v)
+
+
+def call_project(att, w_out, target):
+    bf16, f32 = jnp.bfloat16, jnp.float32
+    vmem = pl.BlockSpec(memory_space=pltpu.VMEM)
+    shape = jax.ShapeDtypeStruct
+    dma = pltpu.SemaphoreType.DMA
+    return pl.pallas_call(
+        project_and_exchange,
+        in_specs=[vmem] * 3,
+        out_specs=[vmem] * 2,
+        out_shape=[shape((SEQ, LANES), bf16), shape((8, LANES), f32)],
+        scratch_shapes=[
+            pltpu.VMEM((LANES, 2048), bf16), pltpu.VMEM((LANES, CH), f32), pltpu.VMEM((LANES, 2048), bf16),
+            pltpu.VMEM((32, 8, LANES), f32),
+        ] + [dma] * 8,
+        compiler_params=pltpu.CompilerParams(collective_id=1, has_side_effects=True, vmem_limit_bytes=40 * 1024 * 1024),
+        name="project_and_exchange",
+    )(att, w_out, target)
 
 
 def call_text_forward(lengths, q, k, v, o, z, m):
@@ -199,66 +515,20 @@
     )(coef, q, g, att, ei, et, si, st, k, v, kt, vt)
 
 
-def to_heads(values):
-    return jnp.transpose(values.reshape(2, 64, 16, LANES), (2, 0, 1, 3)).reshape(32, 64, LANES)
-
-
-def exchange(values):
-    return lax.all_to_all(values, "seq", split_axis=0, concat_axis=0, tiled=True)
-
-
 def swap(values, pairs):
     return lax.ppermute(values, "seq", pairs)
 
 
 def on_device(prompt, lengths, timesteps, ref_errors, gain_ffn, w_in_gate, w_in_up, w_in_down, gain_final, w_context,
               image_q, image_k, image_v, w_out, target):
-    seat = lax.axis_index("seq")
-    core = seat % 2
+    core = lax.axis_index("seq") % 2
     pairs = [(i, i ^ 1) for i in range(32)]
-    gate_full = lax.all_gather(w_in_gate, "fsdp", axis=0, tiled=True)
-    up_full = lax.all_gather(w_in_up, "fsdp", axis=0, tiled=True)
-    down_full = lax.all_gather(w_in_down, "fsdp", axis=1, tiled=True)
-    context_full = lax.all_gather(w_context, "fsdp", axis=0, tiled=True)
     out_full = lax.all_gather(w_out, "fsdp", axis=0, tiled=True)
-
-    sent = jnp.concatenate([to_heads(image_q[0]), to_heads(image_k[0]), to_heads(image_v[0])], axis=1)
-    got = exchange(sent)
-    q, k, v = (got[:, 64 * i:64 * (i + 1)].reshape(SEQ, LANES) for i in range(3))
-    ei, o, z, m = call_image_forward(q, k, v)
-
-    prompt_f32 = prompt[0].astype(jnp.float32)
-    normed = rms_gain(prompt_f32, gain_ffn).astype(jnp.bfloat16)
-    gate_act = dot(normed, gate_full)
-    up_act = dot(normed, up_full)
-    hidden = (jax.nn.gelu(gate_act, approximate=True) * up_act).astype(jnp.bfloat16)
-    partial_value = dot(hidden, down_full).astype(jnp.bfloat16)
-    parts = exchange(partial_value.reshape(32, 8, 4096))
-    mine = lax.dynamic_slice_in_dim(prompt[0], seat * 8, 8, 0).astype(jnp.float32)
-    state = mine + jnp.sum(parts.astype(jnp.float32), axis=0)
-    encoded_rows = rms_gain(state, gain_final).astype(jnp.bfloat16)
-    encoded = lax.all_gather(encoded_rows, "seq", axis=0, tiled=True)
-    context = dot(encoded, context_full).astype(jnp.bfloat16)
-    other = swap(context, pairs)
-    first = jnp.where(core == 0, context, other)
-    second = jnp.where(core == 0, other, context)
-    kt = jnp.concatenate([first[:, :HEAD], second[:, :HEAD]], axis=1)
-    vt = jnp.concatenate([first[:, HEAD:], second[:, HEAD:]], axis=1)
-
+    q, k, v, ei, o, z, m, kt, vt = call_encode(
+        prompt[0], gain_ffn[None], gain_final[None], w_in_gate, w_in_up, w_in_down, w_context, image_q[0], image_k[0], image_v[0])
     att, et, si, st = call_text_forward(lengths, q, kt, vt, o, z, m)
-    back = exchange(att.reshape(32, 64, LANES))
-    tok = jnp.transpose(back.reshape(16, 2, 64, LANES), (1, 2, 0, 3)).reshape(LANES, SEQ)
-    residual = dot(tok, out_full) - target[0].reshape(LANES, CH).astype(jnp.float32)
-    err = jnp.sum((residual * residual).reshape(2, 64 * CH), axis=1)
-    hi = lax.reduce_precision(err, 8, 7)
-    mid = lax.reduce_precision(err - hi, 8, 7)
-    low = err - hi - mid
-    pieces = jnp.concatenate([hi, mid, low]).astype(jnp.bfloat16)
-    grad_tok = dot(residual.astype(jnp.bfloat16), out_full, NT).astype(jnp.bfloat16)
-    extra = jnp.broadcast_to(jnp.pad(pieces, (0, LANES - 6))[None, None, :], (32, 16, LANES))
-    arrived = exchange(jnp.concatenate([to_heads(grad_tok), extra], axis=1))
-    g = arrived[:, :64].reshape(SEQ, LANES)
-    sums = jnp.sum(arrived[:, 64, :6].astype(jnp.float32).reshape(32, 3, 2), axis=(0, 1))
+    g, err = call_project(att, out_full, target[0].reshape(LANES, CH))
+    sums = err[:2, 0]
     mean_errors = sums / (SEQ * CH)
     error_gap = mean_errors[0] - ref_errors[0, 0] - (mean_errors[1] - ref_errors[0, 1])
     sigma_t = noise_level(timesteps[0])

time: 450 us -> 287 us (0.64)
  waiting for transfers between devices: 284 us -> 2.65 us
  Pallas kernels: 47.1 us -> 247 us
  starting transfers between devices: 32.3 us -> 0.34 us
  blocking collectives: 29.6 us -> 0 us
  matrix products: 16.5 us -> 0 us
  other arithmetic: 9.78 us -> 0.4 us
    pallas_call x1 -> x2, Pallas kernels: 17.3 us -> 217 us  [the longest x1 181 us: call_encode(): pl.pallas_call(encode_and_exchange, in_specs=[vmem] * 3 + [anywhere] * 7,...]
    all_gather x5 -> x0, waiting for transfers between devices: 153 us -> none  [the longest x1 45.2 us: on_device(): up_full = lax.all_gather(w_in_up, 'fsdp', axis=0, tiled=True)]
    all_to_all x3 -> x0, waiting for transfers between devices: 113 us -> none  [exchange(): lax.all_to_all(values, 'seq', split_axis=0, concat_axis=0, tiled=True)]
    all_to_all x3 -> x0, starting transfers between devices: 30.9 us -> none  [exchange(): lax.all_to_all(values, 'seq', split_axis=0, concat_axis=0, tiled=True)]
    all_to_all x1 -> x0, blocking collectives: 29.6 us -> none  [exchange(): lax.all_to_all(values, 'seq', split_axis=0, concat_axis=0, tiled=True)]
    dot_general x5 -> x0, matrix products: 16.5 us -> none  [dot(): return lax.dot_general(a, b, dims, preferred_element_type=jnp.float32)]
    all_gather x1, waiting for transfers between devices: 13.4 us -> 0.01 us  [on_device(): out_full = lax.all_gather(w_out, 'fsdp', axis=0, tiled=True)]
    unnamed x24 -> x32, local copies, waits for them, and re-layouts: 3.38 us -> 11.4 us
  transfers between devices with their start and end apart: 11 -> 2, of which waited for: 9 -> 1; matrix products, arithmetic and copies ran while one was open for 3% -> 0% of each run, Pallas kernels for 6% -> 67%
where the time goes in v2:
time: 287 us; the launch traced here: 283 us
  Pallas kernels  247 us (86%)
  between operations  19.5 us (7%)
  local copies, waits for them, and re-layouts  13.4 us (5%)
    pallas_call x1, Pallas kernels, call_encode(): pl.pallas_call(encode_and_exchange, in_specs=[vmem] * 3 + [anywhere] * 7,...  181 us
    pallas_call x1, Pallas kernels, call_project(): pl.pallas_call(project_and_exchange, in_specs=[vmem] * 3, out_specs=[vmem...  36.7 us
    pallas_call x1, Pallas kernels, call_backward(): pl.pallas_call(backward, grid=(SEQ // ROWS,), in_specs=[pl.BlockSpec(memo...  21 us
    unnamed x32, local copies, waits for them, and re-layouts  11.4 us
    pallas_call x1, Pallas kernels, call_text_forward(): pl.pallas_call(text_forward, grid=(SEQ // ROWS,), in_specs=[pl.BlockSpec(...  8.89 us
  transfers between devices with their start and end apart: 2, of which 1 were waited for; matrix products, arithmetic and copies ran while one was open for 0% of the time, Pallas kernels for 67%

profile of v2, /device:TPU:33, one launch (start us, length us, event | category | flops | bytes accessed | tf_op | source)
XLA Modules:
  0.0 283.3 jit_solution(16481249904036667609)
XLA Ops:
  7.2 0.0 all-gather.2.cloned.1.call-start
  7.2 0.7 all-gather.2.cloned.1.call-update
  9.3 180.5 %encode_and_exchange.1 = (bf16[2048,128]{1,0:T(8,128)(2,1)}, bf16[2048,128]{1,0:T(8,128)(2,1)}, bf16[2048,128]{1,0:T(8,128)(2,1)}, bf16[2,2048,2048]{2,1,0:T(8,1...) custom-call(bf16[256,4096]{1,0:T(8,128)(2,1)} %bitcast.24, ...), custom_call_target="tpu_custom_call" | custom-call | flops 20000000000 | bytes 40000000 | tf_op jit(solution)/shard_map/encode_and_exchange/pallas_call | solution.py:446
  189.8 0.0 copy-start.1
  189.8 1.0 copy-done.1
  190.8 0.0 copy-start.4
  190.8 1.2 copy-done.4
  192.0 0.0 copy-start.5
  192.0 1.2 copy-done.5
  193.3 0.0 copy-start.11
  193.3 0.8 copy-done.11
  194.1 0.0 copy-start.13
  194.1 0.8 copy-done.13
  195.0 0.0 copy-start.10
  195.0 8.9 %text_forward.1 = (bf16[2048,128]{1,0:T(8,128)(2,1)S(1)}, bf16[2,2048,256]{2,1,0:T(8,128)(2,1)}, f32[2048,128]{1,0:T(8,128)S(1)}, f32[2048,128]{1,0:T(8,128)S(1)}) custom-call(s32[1]{0:T(128)S(6)} %copy.19.len_ref, bf16[2048,128]{1,0:T(8,128)(2,1)S(1)} %copy-done.1, bf16[256,128]{1,0:T(8,128)(2,1)S(1)} %copy-done.11, bf16[256,128]{1,0:T(8,128)(2,1)S(1)} %copy-done.13, ...), custom_call_target="tpu_custom_call" | custom-call | tf_op jit(solution)/shard_map/text_forward/pallas_call | solution.py:488
  203.8 0.0 copy-start.3
  203.8 1.1 copy-done.3
  204.9 0.0 all-gather.2.cloned.1.call-done.w_ref
  204.9 0.0 copy-done.10
  204.9 0.0 copy-start
  204.9 2.5 copy-done
  207.4 0.0 copy-start.15
  207.4 0.0 copy-start.2
  207.4 0.0 copy-start.6
  207.4 0.0 copy-start.7
  207.4 0.0 copy-start.12
  207.4 36.7 %project_and_exchange.1 = (bf16[2048,128]{1,0:T(8,128)(2,1)S(1)}, f32[8,128]{1,0:T(8,128)S(1)}) custom-call(bf16[2048,128]{1,0:T(8,128)(2,1)S(1)} %get-tuple-element.28.att_ref, bf16[2048,1280]{1,0:T(8,128)(2,1)S(1)} %copy-done, bf16[128,1280]{1,0:T(8,128)(2,1)S(1)} %bitcast.22), custom_call_target="tpu_custom_call" | custom-call | tf_op jit(solution)/shard_map/project_and_exchange/pallas_call | solution.py:472
  244.1 0.0 copy-start.8
  244.1 0.8 copy-done.8
  244.9 0.0 copy-done.15
  244.9 0.7 fusion.2
  248.3 0.0 copy-done.2
  248.3 0.0 copy-done.6
  248.4 0.0 copy-done.7
  248.4 0.0 copy-done.12
  248.4 0.0 copy-start.9
  248.4 1.0 copy-done.9
  249.4 0.0 copy-start.14
  249.4 0.8 copy-done.14
  250.3 21.0 %backward.1 = (bf16[128,2048]{1,0:T(8,128)(2,1)S(1)}, bf16[128,2048]{1,0:T(8,128)(2,1)S(1)}, bf16[128,2048]{1,0:T(8,128)(2,1)S(1)}) custom-call(f32[1]{0:T(128)} %bitcast.10.coef_ref, bf16[2048,128]{1,0:T(8,128)(2,1)S(1)} %copy-done.2, bf16[2048,128]{1,0:T(8,128)(2,1)S(1)} %copy-done.9, bf16[2048,128]{1,0:T(8,128)(2,1)S(1)} %get-tuple-element.28.att_ref, ...), custom_call_target="tpu_custom_call" | custom-call | tf_op jit(solution)/shard_map/backward/pallas_call | solution.py:503
  271.3 0.2 pad_maximum_fusion
  271.5 0.1 constant_dynamic-slice_fusion
  271.6 0.3 collective-permute-start
  272.0 2.0 collective-permute-done
  274.0 0.2 fusion
  274.2 1.2 fusion.1
  (1 shorter events, 0.0 us)
Async XLA Ops:
  7.2 197.8 %all-gather.2.cloned.1.call-start = ((), (), s32[]{:S(2)}) async-start(), calls=%async_computation | async-start | bytes 5898240 | tf_op jit(solution)/shard_map/all_gather | solution.py:526
  189.8 1.0 copy-start.1
  190.8 1.2 copy-start.4
  192.0 1.2 copy-start.5
  193.3 0.8 copy-start.11
  194.1 0.8 copy-start.13
  195.0 10.0 %copy-start.10 = (bf16[1,2,64,1280]{3,2,1,0:T(8,128)(2,1)S(1)}, bf16[1,2,64,1280]{3,2,1,0:T(8,128)(2,1)}, u32[]{:S(2)}) copy-start(bf16[1,2,64,1280]{3,2,1,0:T(8,128)(2,1)} %param.29) | copy-start | bytes 983044
  203.8 1.1 copy-start.3
  204.9 2.5 copy-start
  207.4 37.5 %copy-start.15 = (f32[1,2]{1,0:T(1,128)S(1)}, f32[1,2]{1,0:T(1,128)}, u32[]{:S(2)}) copy-start(f32[1,2]{1,0:T(1,128)} %param.18) | copy-start | bytes 28
  207.4 40.9 %copy-start.2 = (bf16[2048,128]{1,0:T(8,128)(2,1)S(1)}, bf16[2048,128]{1,0:T(8,128)(2,1)}, u32[]{:S(2)}) copy-start(bf16[2048,128]{1,0:T(8,128)(2,1)} %get-tuple-element.22.q_ref) | copy-start | bytes 1572868
  207.4 40.9 %copy-start.6 = (bf16[2048,128]{1,0:T(8,128)(2,1)S(1)}, bf16[2048,128]{1,0:T(8,128)(2,1)}, u32[]{:S(2)}) copy-start(bf16[2048,128]{1,0:T(8,128)(2,1)} %get-tuple-element.35.k_ref) | copy-start | bytes 1572868
  207.4 40.9 %copy-start.7 = (bf16[2048,128]{1,0:T(8,128)(2,1)S(1)}, bf16[2048,128]{1,0:T(8,128)(2,1)}, u32[]{:S(2)}) copy-start(bf16[2048,128]{1,0:T(8,128)(2,1)} %get-tuple-element.36.v_ref) | copy-start | bytes 1572868
  207.4 40.9 %copy-start.12 = (bf16[256,128]{1,0:T(8,128)(2,1)S(1)}, bf16[256,128]{1,0:T(8,128)(2,1)}, u32[]{:S(2)}) copy-start(bf16[256,128]{1,0:T(8,128)(2,1)} %get-tuple-element.23.k_ref.kt_ref) | copy-start | bytes 196612
  244.1 0.8 copy-start.8
  248.4 1.0 copy-start.9
  249.4 0.8 copy-start.14
  271.6 2.4 collective-permute-start
Sparse Core Ops, SparseCore 0:
  9.8 119.2 all-gather.1

commit v3 on v2

v3 whole, which is shorter than its diff:
```python
import math

import jax
import jax.numpy as jnp
from jax import lax
from jax.experimental import pallas as pl
from jax.experimental.pallas import tpu as pltpu
from jax.sharding import PartitionSpec as P

PROMPT = 256
HEAD = 64
CH = 1280
SEQ = 2048
LANES = 128
ROWS = 256

dpo_beta = 20.0
norm_eps = 1e-06

NT = (((1,), (1,)), ((), ()))
NN = (((1,), (0,)), ((), ()))


def dot(a, b, dims=NN):
    return lax.dot_general(a, b, dims, preferred_element_type=jnp.float32)


def noise_level(step_index):
    fraction = (step_index.astype(jnp.float32) + 1.0) / 1000.0
    return 3.0 * fraction / (1.0 + 2.0 * fraction)


def head_lanes(j):
    lane = lax.broadcasted_iota(jnp.int32, (1, LANES), 1)
    return (lane >= j * HEAD) & (lane < (j + 1) * HEAD)


def with_ones(values):
    return jnp.concatenate([values, jnp.ones_like(values)], axis=1)


def by_head(first, second):
    return jnp.where(head_lanes(0), first, second)


def image_rows(q, k, v_aug, e_ref):
    q = q * jnp.asarray(1.0 / math.sqrt(HEAD), jnp.bfloat16)
    outs, tops = [], []
    for j in range(2):
        qj = jnp.where(head_lanes(j), q, jnp.zeros_like(q))
        s = dot(qj, k, NT)
        top = jnp.max(s, axis=-1, keepdims=True)
        e = jnp.exp(s - top).astype(jnp.bfloat16)
        e_ref[j] = e
        outs.append(dot(e, v_aug))
        tops.append(top)
    return (
        by_head(outs[0][:, :LANES], outs[1][:, :LANES]),
        by_head(outs[0][:, LANES:], outs[1][:, LANES:]),
        by_head(tops[0], tops[1]),
    )


def place():
    seat, pair = lax.axis_index("seq"), lax.axis_index("fsdp")
    chip = seat // 2
    return seat, lax.rem(seat, 2), lax.rem(chip, 4), chip // 4, pair, lax.rem(pair, 4), pair // 4


def remote(src, dst, send_sem, recv_sem, seat, pair):
    return pltpu.make_async_remote_copy(
        src_ref=src, dst_ref=dst, send_sem=send_sem, recv_sem=recv_sem,
        device_id=(seat, pair), device_id_type=pl.DeviceIdType.MESH,
    )


def arrived(ref, sem):
    pltpu.make_async_copy(ref, ref, sem).wait()


ALTERNATE = (1, 3, 2, 0)


def forward(
    len_ref, prompt_ref, gain_in_ref, gain_out_ref, target_ref, gate_in, up_in, down_in, ctx_in, out_in, q_in, k_in, v_in,
    q_ref, k_ref, v_ref, kt_ref, vt_ref, ei_ref, et_ref, si_ref, st_ref, att_ref, g_ref, err_ref,
    gate_buf, up_buf, down_buf, ctx_buf, out_buf, normed, gate_acc, up_acc, part, sib, half, from_x, sum_x, from_z, state,
    ctx_pair, e_tile, o_all, z_all, m_all, tok, resid, grad, err_all,
    w_local, w_send, w_recv, qkv_local, qkv_send, qkv_recv, e_sem, stage_send, stage_recv,
    tok_local, tok_send, tok_recv, g_local, g_send, g_recv, err_send, err_recv,
):
    seat, core, x, zh, pair, y, zl = place()
    other = seat + 1 - 2 * core
    low = lax.rem(seat, 8)
    up_y, down_y = lax.rem(y + 1, 4), lax.rem(y + 3, 4)
    far = lax.rem(y + 2, 4)
    base, base_p = zl * 4, (1 - zl) * 4
    partner = base_p + y

    barrier = pltpu.get_barrier_semaphore()

    @pl.loop(1, 32)
    def _(d):
        pl.semaphore_signal(barrier, inc=1, device_id=(lax.rem(seat + d, 32), pair), device_id_type=pl.DeviceIdType.MESH)

    for peer in (partner, base + up_y, base + down_y):
        pl.semaphore_signal(barrier, inc=1, device_id=(seat, peer), device_id_type=pl.DeviceIdType.MESH)
    pl.semaphore_wait(barrier, 34)

    def plain(buf):
        return lambda slot, rows=None: buf.at[slot] if rows is None else buf.at[slot, rows]

    def own_half(slot, rows=None):
        return out_buf.at[slot, core] if rows is None else out_buf.at[slot, core, rows]

    weights = (
        (gate_in, plain(gate_buf), 512), (up_in, plain(up_buf), 512), (down_in, plain(down_buf), 256),
        (ctx_in, plain(ctx_buf), 512), (out_in.at[core], own_half, 128),
    )
    early, late = (0, 1, 2), (3, 4)

    def send_weight(w, src, dst, sem, peer):
        remote(src, dst, w_send.at[w], w_recv.at[w, sem], seat, peer).start()

    def upper(w, slot):
        return weights[w][1](slot, pl.ds(0, weights[w][2] // 2))

    def lower(w, slot):
        return weights[w][1](slot, pl.ds(weights[w][2] // 2, weights[w][2] // 2))

    def send_own(w):
        src, at, _ = weights[w]
        send_weight(w, src, at(pair), 0, partner)
        send_weight(w, src, at(pair), 1, base + up_y)
        send_weight(w, src, at(pair), 2, base + down_y)
        pltpu.make_async_copy(src, at(pair), w_local.at[w]).start()

    def forward_near(w):
        at = weights[w][1]
        arrived(at(partner), w_recv.at[w, 0])
        send_weight(w, at(partner), at(partner), 3, base + up_y)
        send_weight(w, at(partner), at(partner), 4, base + down_y)
        arrived(at(base + down_y), w_recv.at[w, 1])
        send_weight(w, upper(w, base + down_y), upper(w, base + down_y), 5, base + up_y)
        arrived(at(base + up_y), w_recv.at[w, 2])
        send_weight(w, lower(w, base + up_y), lower(w, base + up_y), 6, base + down_y)

    def forward_partner(w):
        at = weights[w][1]
        arrived(at(base_p + down_y), w_recv.at[w, 3])
        send_weight(w, upper(w, base_p + down_y), upper(w, base_p + down_y), 7, base + up_y)
        arrived(at(base_p + up_y), w_recv.at[w, 4])
        send_weight(w, lower(w, base_p + up_y), lower(w, base_p + up_y), 8, base + down_y)

    def weight_ready(w):
        arrived(upper(w, base + far), w_recv.at[w, 5])
        arrived(lower(w, base + far), w_recv.at[w, 6])
        arrived(upper(w, base_p + far), w_recv.at[w, 7])
        arrived(lower(w, base_p + far), w_recv.at[w, 8])
        pltpu.make_async_copy(weights[w][0], weights[w][1](pair), w_local.at[w]).wait()

    for w in early:
        send_own(w)

    def token_rows(to):
        return pl.ds(pl.multiple_of(to * 64, 64), 64)

    def lanes_of(to):
        return pl.ds(pl.multiple_of((to // 2) * LANES, LANES), LANES)

    def stream_rows(to):
        return pl.ds(pl.multiple_of(lax.rem(to, 2) * 64, 64), 64)

    images = ((q_in, q_ref), (k_in, k_ref), (v_in, v_ref))
    for i, (src, dst) in enumerate(images):

        @pl.loop(0, 8)
        def _(j, i=i, src=src, dst=dst):
            for dz in ALTERNATE:
                to = lax.rem(zh + dz, 4) * 8 + lax.rem(low + j, 8)

                def start(to=to):
                    remote(src.at[lax.rem(to, 2), :, lanes_of(to)], dst.at[token_rows(seat), :],
                           qkv_send.at[i], qkv_recv.at[i], to, pair).start()

                if dz:
                    start()
                else:
                    pl.when(j > 0)(start)

        pltpu.make_async_copy(src.at[core, :, lanes_of(seat)], dst.at[token_rows(seat), :], qkv_local.at[i]).start()

    total = jnp.zeros((PROMPT, 1), jnp.float32)
    for f in range(8):
        rows = prompt_ref[:, 512 * f:512 * (f + 1)].astype(jnp.float32)
        total = total + jnp.sum(rows * rows, axis=-1, keepdims=True)
    inv = lax.rsqrt(total * (1.0 / 4096) + norm_eps)
    for f in range(8):
        cols = slice(512 * f, 512 * (f + 1))
        normed[f] = (prompt_ref[:, cols].astype(jnp.float32) * inv * gain_in_ref[:, cols]).astype(jnp.bfloat16)

    for w in early:
        forward_near(w)
    forward_partner(0)
    forward_partner(1)

    for i, (src, dst) in enumerate(images):
        arrived(dst.at[pl.ds(0, 31 * 64), :], qkv_recv.at[i])
        arrived(dst.at[pl.ds(0, 64), :], qkv_local.at[i])

    blocks = SEQ // ROWS

    def out_copy(b):
        slot = lax.rem(b, 2)
        return pltpu.make_async_copy(e_tile.at[slot], ei_ref.at[:, pl.ds(pl.multiple_of(b * ROWS, ROWS), ROWS), :], e_sem.at[slot])

    def image_blocks(start, stop):
        @pl.loop(start, stop)
        def _(b):
            @pl.when(b >= 2)
            def _():
                out_copy(b - 2).wait()

            rows = pl.ds(pl.multiple_of(b * ROWS, ROWS), ROWS)
            o, z, m = image_rows(q_ref[rows, :], k_ref[...], with_ones(v_ref[...]), e_tile.at[lax.rem(b, 2)])
            o_all[rows, :], z_all[rows, :], m_all[rows, :] = o, z, m
            out_copy(b).start()

    image_blocks(0, 4)
    forward_partner(2)
    for w in late:
        send_own(w)
    image_blocks(4, 8)

    weight_ready(0)
    weight_ready(1)
    gate_acc[...] = jnp.zeros_like(gate_acc)
    up_acc[...] = jnp.zeros_like(up_acc)

    @pl.loop(0, 8)
    def _(f):
        gate_acc[...] += dot(normed[f], gate_buf[f])
        up_acc[...] += dot(normed[f], up_buf[f])

    hidden = (jax.nn.gelu(gate_acc[...], approximate=True) * up_acc[...]).astype(jnp.bfloat16)
    weight_ready(2)

    def part_block(f):
        part[f] = dot(hidden, down_buf[f]).astype(jnp.bfloat16)

    @pl.loop(0, 4)
    def _(i):
        part_block((1 - core) * 4 + i)

    to_other = remote(part.at[pl.ds((1 - core) * 4, 4)], sib, stage_send.at[0], stage_recv.at[0], other, pair)
    to_other.start()

    @pl.loop(0, 4)
    def _(i):
        part_block(core * 4 + i)

    for w in late:
        forward_near(w)
    to_other.wait()
    for i in range(4):
        half[i] = (part[core * 4 + i].astype(jnp.float32) + sib[i].astype(jnp.float32)).astype(jnp.bfloat16)

    def seat_of(zh_to, x_to):
        return (zh_to * 4 + x_to) * 2 + core

    def rows_x(at):
        return pl.ds(pl.multiple_of(at * 64, 64), 64)

    def rows_z(at):
        return pl.ds(pl.multiple_of(at * 16, 16), 16)

    def round_of(stage, make, between=lambda: None):
        copies = [make(d, stage_send.at[stage + d], stage_recv.at[stage + d]) for d in (1, 3, 2)]
        for copy in copies:
            copy.start()
        between()
        for copy in copies:
            copy.wait()

    round_of(0, lambda d, s, r: remote(
        half.at[:, rows_x(lax.rem(x + d, 4)), :], from_x.at[d], s, r, seat_of(zh, lax.rem(x + d, 4)), pair))
    for i in range(4):
        acc = half[i, rows_x(x), :].astype(jnp.float32)
        for d in (1, 2, 3):
            acc = acc + from_x[d, i].astype(jnp.float32)
        sum_x[i] = acc.astype(jnp.bfloat16)
    round_of(3, lambda d, s, r: remote(
        sum_x.at[:, rows_z(lax.rem(zh + d, 4)), :], from_z.at[d], s, r, seat_of(lax.rem(zh + d, 4), x), pair))
    mine = rows_z(x * 4 + zh)
    for i in range(4):
        columns = pl.ds(pl.multiple_of(core * 2048 + i * 512, 512), 512)
        acc = prompt_ref[mine, columns].astype(jnp.float32) + sum_x[i, rows_z(zh), :].astype(jnp.float32)
        for d in (1, 2, 3):
            acc = acc + from_z[d, i].astype(jnp.float32)
        state[core * 4 + i, mine, :] = acc.astype(jnp.bfloat16)
    ours = pl.ds(core * 4, 4)
    round_of(6, lambda d, s, r: remote(
        state.at[ours, mine, :], state.at[ours, mine, :], s, r, seat_of(lax.rem(zh + d, 4), x), pair))

    def forward_late():
        for w in late:
            forward_partner(w)

    round_of(9, lambda d, s, r: remote(
        state.at[ours, rows_x(x), :], state.at[ours, rows_x(x), :], s, r, seat_of(zh, lax.rem(x + d, 4)), pair), forward_late)
    last = remote(state.at[ours], state.at[ours], stage_send.at[13], stage_recv.at[13], other, pair)
    last.start()
    weight_ready(3)
    last.wait()

    total = jnp.zeros((PROMPT, 1), jnp.float32)
    for f in range(8):
        rows = state[f].astype(jnp.float32)
        total = total + jnp.sum(rows * rows, axis=-1, keepdims=True)
    inv = lax.rsqrt(total * (1.0 / 4096) + norm_eps)
    context = jnp.zeros((PROMPT, LANES), jnp.float32)
    for f in range(8):
        encoded = (state[f].astype(jnp.float32) * inv * gain_out_ref[:, 512 * f:512 * (f + 1)]).astype(jnp.bfloat16)
        context = context + dot(encoded, ctx_buf[f])
    ctx_pair[core] = context.astype(jnp.bfloat16)
    give = remote(ctx_pair.at[core], ctx_pair.at[core], stage_send.at[14], stage_recv.at[14], other, pair)
    give.start()
    weight_ready(4)
    share = remote(out_buf.at[:, core], out_buf.at[:, core], stage_send.at[15], stage_recv.at[15], other, pair)
    share.start()
    give.wait()
    first, second = ctx_pair[0].astype(jnp.float32), ctx_pair[1].astype(jnp.float32)
    kt_ref[...] = by_head(first, pltpu.roll(second, HEAD, 1)).astype(jnp.bfloat16)
    vt_ref[...] = by_head(pltpu.roll(first, HEAD, 1), second).astype(jnp.bfloat16)

    spot = tok.at[stream_rows(seat), lanes_of(seat)]
    kept = lax.broadcasted_iota(jnp.int32, (1, PROMPT), 1) < len_ref[...]

    @pl.loop(0, 2)
    def _(part_of):
        for dz in ALTERNATE:
            b = lax.rem(zh + dz, 4) * 2 + part_of
            rows = pl.ds(pl.multiple_of(b * ROWS, ROWS), ROWS)
            att, scale_i, scale_t = text_rows(
                q_ref[rows, :], kt_ref[...], with_ones(vt_ref[...]), kept, o_all[rows, :], z_all[rows, :], m_all[rows, :],
                et_ref.at[:, rows, :])
            att_ref[rows, :], si_ref[rows, :], st_ref[rows, :] = att, scale_i, scale_t
            for t in range(4):
                to = b * 4 + t

                def start(to=to):
                    remote(att_ref.at[token_rows(to), :], spot, tok_send, tok_recv, to, pair).start()

                def keep(to=to):
                    pltpu.make_async_copy(att_ref.at[token_rows(to), :], spot, tok_local).start()

                if dz:
                    start()
                else:
                    pl.when(to != seat)(start)
                    pl.when(to == seat)(keep)

    share.wait()
    arrived(spot, tok_local)
    arrived(att_ref.at[pl.ds(0, 31 * 64), :], tok_recv)

    acc = -target_ref[...].astype(jnp.float32)
    resid[...] = acc

    @pl.loop(0, 8)
    def _(f):
        columns = pl.ds(pl.multiple_of(f * 256, 256), 256)
        resid[...] += dot(tok[:, columns], out_buf[f].reshape(256, CH))

    halves = []
    for stream in range(2):
        rows = resid[64 * stream:64 * (stream + 1), :]
        halves.append(jnp.sum(jnp.sum(rows * rows, axis=1, keepdims=True), axis=0, keepdims=True))
    row = lax.broadcasted_iota(jnp.int32, (8, LANES), 0)
    err_all[seat] = jnp.where(row == 0, halves[0], jnp.where(row == 1, halves[1], 0.0))
    rounded = resid[...].astype(jnp.bfloat16)

    @pl.loop(0, 2)
    def _(part_of):
        for dz in ALTERNATE:
            n = lax.rem(zh + dz, 4) * 2 + part_of
            columns = pl.ds(pl.multiple_of(n * 256, 256), 256)
            grad[:, columns] = dot(rounded, out_buf[n].reshape(256, CH), NT).astype(jnp.bfloat16)
            for t in range(4):
                to = n * 4 + t

                def start(to=to):
                    remote(grad.at[stream_rows(to), lanes_of(to)], g_ref.at[token_rows(seat), :], g_send, g_recv, to, pair).start()
                    remote(err_all.at[seat], err_all.at[seat], err_send, err_recv, to, pair).start()

                def keep(to=to):
                    pltpu.make_async_copy(grad.at[stream_rows(to), lanes_of(to)], g_ref.at[token_rows(seat), :], g_local).start()

                if dz:
                    start()
                else:
                    pl.when(to != seat)(start)
                    pl.when(to == seat)(keep)

    arrived(err_all.at[pl.ds(0, 31)], err_recv)
    err_ref[...] = jnp.sum(err_all[...], axis=0)
    arrived(g_ref.at[pl.ds(0, 64), :], g_local)
    arrived(g_ref.at[pl.ds(0, 31 * 64), :], g_recv)

    out_copy(blocks - 2).wait()
    out_copy(blocks - 1).wait()
    for w, buf in enumerate((gate_buf, up_buf, down_buf, ctx_buf)):
        arrived(buf.at[pl.ds(0, 7)], w_send.at[w])
    arrived(out_buf.at[pl.ds(0, 7), 0], w_send.at[4])
    for i, (_, dst) in enumerate(images):
        arrived(dst.at[pl.ds(0, 31 * 64), :], qkv_send.at[i])
    arrived(g_ref.at[pl.ds(0, 31 * 64), :], g_send)
    arrived(att_ref.at[pl.ds(0, 31 * 64), :], tok_send)
    arrived(err_all.at[pl.ds(0, 31)], err_send)


def text_rows(q, k, v_aug, kept, o, z, m, e_ref):
    q = q * jnp.asarray(1.0 / math.sqrt(HEAD), jnp.bfloat16)
    outs, tops = [], []
    for j in range(2):
        qj = jnp.where(head_lanes(j), q, jnp.zeros_like(q))
        s = jnp.where(kept, dot(qj, k, NT), -jnp.inf)
        top = jnp.maximum(m[:, j * HEAD:j * HEAD + 1], jnp.max(s, axis=-1, keepdims=True))
        e = jnp.exp(s - top).astype(jnp.bfloat16)
        e_ref[j] = e
        outs.append(dot(e, v_aug))
        tops.append(top)
    alpha = jnp.exp(m - by_head(tops[0], tops[1]))
    inv = 1.0 / (alpha * z + by_head(outs[0][:, LANES:], outs[1][:, LANES:]))
    o = alpha * o + by_head(outs[0][:, :LANES], outs[1][:, :LANES])
    return (o * inv).astype(jnp.bfloat16), alpha * inv, inv


def backward(coef_ref, q_ref, g_ref, att_ref, ei_ref, et_ref, si_ref, st_ref, k_ref, v_ref, kt_ref, vt_ref,
             gq_ref, gk_ref, gv_ref, k_acc, v_acc):
    step = pl.program_id(0)

    @pl.when(step == 0)
    def _():
        k_acc[...] = jnp.zeros_like(k_acc)
        v_acc[...] = jnp.zeros_like(v_acc)

    coef = coef_ref[0]
    g = g_ref[...].astype(jnp.float32)
    prod = g * att_ref[...].astype(jnp.float32)
    v_aug, vt_aug = with_ones(v_ref[...]), with_ones(vt_ref[...])
    q_t = q_ref[...].T
    lane = lax.broadcasted_iota(jnp.int32, (1, LANES), 1)
    grads = []
    for j in range(2):
        mine = head_lanes(j)
        gj = jnp.where(mine, g, 0.0)
        delta = jnp.sum(jnp.where(mine, prod, 0.0), axis=-1, keepdims=True)

        def scaled(scale):
            gs = (gj * scale).astype(jnp.bfloat16)
            d = -delta * scale
            hi = d.astype(jnp.bfloat16)
            lo = (d - hi.astype(jnp.float32)).astype(jnp.bfloat16)
            extra = jnp.where(lane == 0, hi, jnp.where(lane == 1, lo, jnp.zeros_like(hi)))
            return gs, jnp.concatenate([gs, extra], axis=1)

        gi, lhs_i = scaled(si_ref[:, j * HEAD:j * HEAD + 1])
        _, lhs_t = scaled(st_ref[:, j * HEAD:j * HEAD + 1])
        ei = ei_ref[j]
        ds = (ei.astype(jnp.float32) * dot(lhs_i, v_aug, NT)).astype(jnp.bfloat16)
        ds_t = (et_ref[j].astype(jnp.float32) * dot(lhs_t, vt_aug, NT)).astype(jnp.bfloat16)
        grads.append(dot(ds, k_ref[...]) + dot(ds_t, kt_ref[...]))
        rows = slice(j * HEAD, (j + 1) * HEAD)
        k_acc[rows, :] += dot(q_t[rows, :], ds)
        v_acc[rows, :] += dot(gi.T[rows, :], ei)
    factor = coef * (1.0 / math.sqrt(HEAD))
    gq_ref[...] = (by_head(grads[0], grads[1]) * factor).T.astype(jnp.bfloat16)

    @pl.when(step == pl.num_programs(0) - 1)
    def _():
        gk_ref[...] = (k_acc[...] * factor).astype(jnp.bfloat16)
        gv_ref[...] = (v_acc[...] * coef).astype(jnp.bfloat16)


def block(shape, index_map):
    return pl.BlockSpec(shape, index_map)


def whole(*shape):
    return pl.BlockSpec(shape, lambda i: (0,) * len(shape))


def rows_of(width):
    return pl.BlockSpec((ROWS, width), lambda i: (i, 0))


def params():
    return pltpu.CompilerParams(vmem_limit_bytes=48 * 1024 * 1024)


def call_forward(lengths, prompt, gain_in, gain_out, target, gate, up, down, ctx, out, q, k, v):
    bf16, f32 = jnp.bfloat16, jnp.float32
    anywhere, vmem = pl.BlockSpec(memory_space=pl.ANY), pl.BlockSpec(memory_space=pltpu.VMEM)
    shape = jax.ShapeDtypeStruct
    dma, buf = pltpu.SemaphoreType.DMA, pltpu.VMEM
    rows_bf16, rows_f32 = shape((SEQ, LANES), bf16), shape((SEQ, LANES), f32)
    text = shape((PROMPT, LANES), bf16)
    return pl.pallas_call(
        forward,
        in_specs=[vmem] * 5 + [anywhere] * 8,
        out_specs=[vmem] * 5 + [anywhere] + [vmem] * 6,
        out_shape=[rows_bf16] * 3 + [text] * 2 + [shape((2, SEQ, SEQ), bf16), shape((2, SEQ, PROMPT), bf16)]
        + [rows_f32] * 2 + [rows_bf16] * 2 + [shape((8, LANES), f32)],
        scratch_shapes=[
            buf((8, 512, 256), bf16), buf((8, 512, 256), bf16), buf((8, 256, 512), bf16), buf((8, 512, 128), bf16),
            buf((8, 2, 128, CH), bf16),
            buf((8, PROMPT, 512), bf16), buf((PROMPT, 256), f32), buf((PROMPT, 256), f32),
            buf((8, PROMPT, 512), bf16), buf((4, PROMPT, 512), bf16), buf((4, PROMPT, 512), bf16),
            buf((4, 4, 64, 512), bf16), buf((4, 64, 512), bf16), buf((4, 4, 16, 512), bf16),
            buf((8, PROMPT, 512), bf16), buf((2, PROMPT, LANES), bf16), buf((2, 2, ROWS, SEQ), bf16),
            buf((SEQ, LANES), f32), buf((SEQ, LANES), f32), buf((SEQ, LANES), f32),
            buf((LANES, 2048), bf16), buf((LANES, CH), f32), buf((LANES, 2048), bf16), buf((32, 8, LANES), f32),
            dma((5,)), dma((5,)), dma((5, 9)), dma((3,)), dma((3,)), dma((3,)), dma((2,)), dma((16,)), dma((16,)),
        ] + [dma] * 8,
        compiler_params=pltpu.CompilerParams(collective_id=0, has_side_effects=True, vmem_limit_bytes=60 * 1024 * 1024),
        name="forward",
    )(lengths, prompt, gain_in, gain_out, target, gate, up, down, ctx, out, q, k, v)


def call_backward(coef, q, g, att, ei, et, si, st, k, v, kt, vt):
    out = lambda: jax.ShapeDtypeStruct((LANES, SEQ), jnp.bfloat16)
    return pl.pallas_call(
        backward,
        grid=(SEQ // ROWS,),
        in_specs=[pl.BlockSpec(memory_space=pltpu.SMEM), rows_of(LANES), rows_of(LANES), rows_of(LANES),
                  pl.BlockSpec((2, ROWS, SEQ), lambda i: (0, i, 0)), pl.BlockSpec((2, ROWS, PROMPT), lambda i: (0, i, 0)),
                  rows_of(LANES), rows_of(LANES), whole(SEQ, LANES), whole(SEQ, LANES),
                  whole(PROMPT, LANES), whole(PROMPT, LANES)],
        out_specs=[pl.BlockSpec((LANES, ROWS), lambda i: (0, i)), whole(LANES, SEQ), whole(LANES, SEQ)],
        out_shape=[out(), out(), out()],
        scratch_shapes=[pltpu.VMEM((LANES, SEQ), jnp.float32), pltpu.VMEM((LANES, SEQ), jnp.float32)],
        compiler_params=params(),
        name="backward",
    )(coef, q, g, att, ei, et, si, st, k, v, kt, vt)


def swap(values, pairs):
    return lax.ppermute(values, "seq", pairs)


def on_device(prompt, lengths, timesteps, ref_errors, gain_ffn, w_in_gate, w_in_up, w_in_down, gain_final, w_context,
              image_q, image_k, image_v, w_out, target):
    core = lax.axis_index("seq") % 2
    pairs = [(i, i ^ 1) for i in range(32)]
    q, k, v, kt, vt, ei, et, si, st, att, g, err = call_forward(
        jnp.broadcast_to(lengths[:, None], (1, PROMPT)), prompt[0], gain_ffn[None], gain_final[None],
        target[0].reshape(LANES, CH), w_in_gate, w_in_up, w_in_down, w_context, w_out.reshape(2, 128, CH),
        image_q[0], image_k[0], image_v[0])
    sums = err[:2, 0]
    mean_errors = sums / (SEQ * CH)
    error_gap = mean_errors[0] - ref_errors[0, 0] - (mean_errors[1] - ref_errors[0, 1])
    sigma_t = noise_level(timesteps[0])
    logit_value = dpo_beta * sigma_t * error_gap
    pair_loss = jax.nn.softplus(logit_value)[None]
    coefficient = sigma_t * jax.nn.sigmoid(logit_value)
    coef = jnp.where(core == 0, coefficient, -coefficient)[None]

    grads = jnp.stack(call_backward(coef, q, g, att, ei, et, si, st, k, v, kt, vt))
    halves = grads.reshape(3, 2, HEAD, SEQ)
    own = lax.dynamic_index_in_dim(halves, core, 1, keepdims=False)
    theirs = swap(lax.dynamic_index_in_dim(halves, 1 - core, 1, keepdims=False), pairs)
    outs = jnp.where(core == 0, jnp.stack([own, theirs], axis=1), jnp.stack([theirs, own], axis=1))
    outs = jnp.transpose(outs, (0, 1, 3, 2))
    return pair_loss, outs[0][None], outs[1][None], outs[2][None]


def solution(mesh):
    return jax.shard_map(
        on_device,
        mesh=mesh,
        in_specs=(
            P("fsdp", None, None),
            P("fsdp"),
            P("fsdp"),
            P("fsdp", None),
            P(),
            P("fsdp", "seq"),
            P("fsdp", "seq"),
            P("seq", "fsdp"),
            P(),
            P("fsdp", "seq"),
            P("fsdp", None, "seq", None),
            P("fsdp", None, "seq", None),
            P("fsdp", None, "seq", None),
            P("fsdp", None),
            P("fsdp", None, "seq", None),
        ),
        out_specs=(
            P("fsdp"),
            P("fsdp", None, None, "seq"),
            P("fsdp", None, None, "seq"),
            P("fsdp", None, None, "seq"),
        ),
        check_vma=False,
    )
```

time: 287 us -> 219 us (0.76)
  Pallas kernels: 247 us -> 195 us
  between operations: 19.5 us -> 5.98 us
    pallas_call x3 -> x1, Pallas kernels: 226 us -> 174 us  [call_forward(): pl.pallas_call(forward, in_specs=[vmem] * 5 + [anywhere] * 8, out_specs=[...]
    unnamed x32 -> x18, local copies, waits for them, and re-layouts: 11.4 us -> 8.1 us
  transfers between devices with their start and end apart: 2 -> 1, of which waited for: 1 -> 1; matrix products, arithmetic and copies ran while one was open for 0% -> 0% of each run, Pallas kernels for 67% -> 0%
where the time goes in v3:
time: 219 us; the launch traced here: 215 us
  Pallas kernels  195 us (89%)
  local copies, waits for them, and re-layouts  10.6 us (5%)
  between operations  5.98 us (3%)
    pallas_call x1, Pallas kernels, call_forward(): pl.pallas_call(forward, in_specs=[vmem] * 5 + [anywhere] * 8, out_specs=[...  174 us
    pallas_call x1, Pallas kernels, call_backward(): pl.pallas_call(backward, grid=(SEQ // ROWS,), in_specs=[pl.BlockSpec(memo...  21 us
    unnamed x18, local copies, waits for them, and re-layouts  8.1 us
  transfers between devices with their start and end apart: 1, of which 1 were waited for; matrix products, arithmetic and copies ran while one was open for 0% of the time, Pallas kernels for 0%

profile of v3, /device:TPU:33, one launch (start us, length us, event | category | flops | bytes accessed | tf_op | source)
XLA Modules:
  0.0 215.1 jit_solution(6842205315173579569)
XLA Ops:
  1.3 0.6 broadcast_in_dim.21.len_ref
  1.9 0.0 copy-start.8
  1.9 174.2 %forward.1 = (bf16[2048,128]{1,0:T(8,128)(2,1)}, bf16[2048,128]{1,0:T(8,128)(2,1)}, bf16[2048,128]{1,0:T(8,128)(2,1)}, bf16[256,128]{1,0:T(8,128)(2,1)}, bf16[25...) custom-call(s32[1,256]{1,0:T(1,128)} %broadcast_in_dim.21.len_ref, ...), custom_call_target="tpu_custom_call" | custom-call | tf_op jit(solution)/shard_map/forward/pallas_call | solution.py:509
  176.0 0.7 slice_multiply_fusion
  177.4 0.0 copy-done.8
  177.4 0.6 fusion.2
  180.7 0.0 copy-start
  180.7 1.2 copy-done
  181.9 0.0 copy-start.1
  181.9 1.0 copy-done.1
  183.0 0.0 copy-start.2
  183.0 1.0 copy-done.2
  184.0 0.0 copy-start.3
  184.0 1.0 copy-done.3
  185.0 0.0 copy-start.4
  185.0 1.0 copy-done.4
  186.1 0.0 copy-start.5
  186.1 1.0 copy-done.5
  187.1 0.0 copy-start.6
  187.1 0.8 copy-done.6
  188.0 0.0 copy-start.7
  188.0 0.8 copy-done.7
  188.8 21.0 %backward.1 = (bf16[128,2048]{1,0:T(8,128)(2,1)S(1)}, bf16[128,2048]{1,0:T(8,128)(2,1)S(1)}, bf16[128,2048]{1,0:T(8,128)(2,1)S(1)}) custom-call(f32[1]{0:T(128)} %bitcast.12.coef_ref, bf16[2048,128]{1,0:T(8,128)(2,1)S(1)} %copy-done.1, bf16[2048,128]{1,0:T(8,128)(2,1)S(1)} %copy-done.5, bf16[2048,128]{1,0:T(8,128)(2,1)S(1)} %copy-done.4, ...), custom_call_target="tpu_custom_call" | custom-call | tf_op jit(solution)/shard_map/backward/pallas_call | solution.py:533
  209.8 0.2 pad_maximum_fusion
  210.0 0.2 constant_dynamic-slice_fusion
  210.1 0.3 collective-permute-start
  210.6 1.9 collective-permute-done
  212.5 0.2 fusion
  212.7 1.2 fusion.1
Async XLA Ops:
  1.9 175.5 %copy-start.8 = (f32[1,2]{1,0:T(1,128)S(1)}, f32[1,2]{1,0:T(1,128)}, u32[]{:S(2)}) copy-start(f32[1,2]{1,0:T(1,128)} %param.18) | copy-start | bytes 28
  180.7 1.2 copy-start
  181.9 1.0 copy-start.1
  183.0 1.0 copy-start.2
  184.0 1.0 copy-start.3
  185.0 1.0 copy-start.4
  186.1 1.0 copy-start.5
  187.1 0.8 copy-start.6
  188.0 0.8 copy-start.7
  210.1 2.4 %collective-permute-start = (bf16[3,64,2048]{2,1,0:T(8,128)(2,1)S(1)}, bf16[3,64,2048]{2,1,0:T(8,128)(2,1)S(1)}, u32[]{:S(2)}, u32[]{:S(2)}) collective-permute-start(bf16[3,64,2048]{2,1,0:T(8,128)(2,1)S(1)} %get-tuple-element.38), channel_id=1, source_target_pairs={{0,8},{8,0},{16,24},{24,16},{32,40},{40,32},{48,56},{56,48},{64,72... | collective-permute-start | bytes 2359304 | tf_op jit(solution)/shard_map/ppermute | solution.py:549

commit v4 on v3

--- a/solution.py
+++ b/solution.py
@@ -81,13 +81,14 @@
 ALTERNATE = (1, 3, 2, 0)
 
 
-def forward(
-    len_ref, prompt_ref, gain_in_ref, gain_out_ref, target_ref, gate_in, up_in, down_in, ctx_in, out_in, q_in, k_in, v_in,
-    q_ref, k_ref, v_ref, kt_ref, vt_ref, ei_ref, et_ref, si_ref, st_ref, att_ref, g_ref, err_ref,
+def window(
+    len_ref, scalar_ref, prompt_ref, gain_in_ref, gain_out_ref, target_ref, gate_in, up_in, down_in, ctx_in, out_in, q_in, k_in, v_in,
+    loss_ref, gq_ref, gk_ref, gv_ref, ei_ref,
     gate_buf, up_buf, down_buf, ctx_buf, out_buf, normed, gate_acc, up_acc, part, sib, half, from_x, sum_x, from_z, state,
     ctx_pair, e_tile, o_all, z_all, m_all, tok, resid, grad, err_all,
-    w_local, w_send, w_recv, qkv_local, qkv_send, qkv_recv, e_sem, stage_send, stage_recv,
-    tok_local, tok_send, tok_recv, g_local, g_send, g_recv, err_send, err_recv,
+    q_ref, k_ref, v_ref, kt_ref, vt_ref, et_ref, si_ref, st_ref, att_ref, g_ref, k_acc, v_acc, give_q, give_k, give_v,
+    w_local, w_send, w_recv, qkv_local, qkv_send, qkv_recv, e_sem, stage_send, stage_recv, swap_send, swap_recv, g_recv,
+    tok_local, tok_send, tok_recv, g_local, g_send, err_send, err_recv,
 ):
     seat, core, x, zh, pair, y, zl = place()
     other = seat + 1 - 2 * core
@@ -323,12 +324,12 @@
         encoded = (state[f].astype(jnp.float32) * inv * gain_out_ref[:, 512 * f:512 * (f + 1)]).astype(jnp.bfloat16)
         context = context + dot(encoded, ctx_buf[f])
     ctx_pair[core] = context.astype(jnp.bfloat16)
-    give = remote(ctx_pair.at[core], ctx_pair.at[core], stage_send.at[14], stage_recv.at[14], other, pair)
-    give.start()
+    text_swap = remote(ctx_pair.at[core], ctx_pair.at[core], stage_send.at[14], stage_recv.at[14], other, pair)
+    text_swap.start()
     weight_ready(4)
     share = remote(out_buf.at[:, core], out_buf.at[:, core], stage_send.at[15], stage_recv.at[15], other, pair)
     share.start()
-    give.wait()
+    text_swap.wait()
     first, second = ctx_pair[0].astype(jnp.float32), ctx_pair[1].astype(jnp.float32)
     kt_ref[...] = by_head(first, pltpu.roll(second, HEAD, 1)).astype(jnp.bfloat16)
     vt_ref[...] = by_head(pltpu.roll(first, HEAD, 1), second).astype(jnp.bfloat16)
@@ -383,14 +384,14 @@
     @pl.loop(0, 2)
     def _(part_of):
         for dz in ALTERNATE:
-            n = lax.rem(zh + dz, 4) * 2 + part_of
+            n = lax.rem(zh + dz, 4) * 2 + lax.rem(low // 4 + part_of, 2)
             columns = pl.ds(pl.multiple_of(n * 256, 256), 256)
             grad[:, columns] = dot(rounded, out_buf[n].reshape(256, CH), NT).astype(jnp.bfloat16)
             for t in range(4):
                 to = n * 4 + t
 
                 def start(to=to):
-                    remote(grad.at[stream_rows(to), lanes_of(to)], g_ref.at[token_rows(seat), :], g_send, g_recv, to, pair).start()
+                    remote(grad.at[stream_rows(to), lanes_of(to)], g_ref.at[token_rows(seat), :], g_send, g_recv.at[seat // 4], to, pair).start()
                     remote(err_all.at[seat], err_all.at[seat], err_send, err_recv, to, pair).start()
 
                 def keep(to=to):
@@ -402,13 +403,70 @@
                     pl.when(to != seat)(start)
                     pl.when(to == seat)(keep)
 
-    arrived(err_all.at[pl.ds(0, 31)], err_recv)
-    err_ref[...] = jnp.sum(err_all[...], axis=0)
-    arrived(g_ref.at[pl.ds(0, 64), :], g_local)
-    arrived(g_ref.at[pl.ds(0, 31 * 64), :], g_recv)
+    def order(i):
+        r = lax.rem(i, 4)
+        return lax.rem(zh + lax.rem(1 + 2 * r + r // 2, 4), 4) * 2 + lax.rem(low // 4 + i // 4, 2)
+
+    def in_copy(i):
+        slot = lax.rem(i, 2)
+        rows = pl.ds(pl.multiple_of(order(i) * ROWS, ROWS), ROWS)
+        return pltpu.make_async_copy(ei_ref.at[:, rows, :], e_tile.at[slot], e_sem.at[slot])
 
     out_copy(blocks - 2).wait()
     out_copy(blocks - 1).wait()
+    in_copy(0).start()
+    in_copy(1).start()
+    k_acc[...] = jnp.zeros_like(k_acc)
+    v_acc[...] = jnp.zeros_like(v_acc)
+
+    arrived(err_all.at[pl.ds(0, 31)], err_recv)
+    mean_errors = jnp.sum(err_all[...], axis=0) * (1.0 / (SEQ * CH))
+    error_gap = (mean_errors[0:1] - scalar_ref[1:2]) - (mean_errors[1:2] - scalar_ref[2:3])
+    logit = dpo_beta * scalar_ref[0:1] * error_gap
+    loss_ref[...] = jnp.maximum(logit, 0.0) + jnp.log1p(jnp.exp(-jnp.abs(logit)))
+    coef = scalar_ref[0:1] / (1.0 + jnp.exp(-logit)) * (1 - 2 * core).astype(jnp.float32)
+    factor = coef * (1.0 / math.sqrt(HEAD))
+    head_rows = pl.ds(pl.multiple_of(core * HEAD, HEAD), HEAD)
+    other_rows = pl.ds(pl.multiple_of((1 - core) * HEAD, HEAD), HEAD)
+    arrived(g_ref.at[pl.ds(0, 64), :], g_local)
+
+    def give(i, staged, out, cols):
+        return remote(staged.at[other_rows, cols], out.at[core, :, cols], swap_send.at[i], swap_recv.at[i], other, pair)
+
+    every = pl.ds(0, SEQ)
+
+    @pl.loop(0, blocks)
+    def _(i):
+        b = order(i)
+        rows = pl.ds(pl.multiple_of(b * ROWS, ROWS), ROWS)
+
+        @pl.when(b == seat // 4)
+        def _():
+            arrived(g_ref.at[pl.ds(0, 192), :], g_recv.at[b])
+
+        @pl.when(b != seat // 4)
+        def _():
+            arrived(g_ref.at[pl.ds(0, 256), :], g_recv.at[b])
+
+        in_copy(i).wait()
+        grad_q = backward_rows(
+            q_ref[rows, :], g_ref[rows, :], att_ref[rows, :], e_tile.at[lax.rem(i, 2)], et_ref.at[:, rows, :],
+            si_ref[rows, :], st_ref[rows, :], k_ref[...], with_ones(v_ref[...]), kt_ref[...], with_ones(vt_ref[...]), k_acc, v_acc)
+
+        @pl.when(i + 2 < blocks)
+        def _():
+            in_copy(i + 2).start()
+
+        give_q[:, rows] = (grad_q * factor).T.astype(jnp.bfloat16)
+        gq_ref[core, :, rows] = give_q[head_rows, rows]
+        give(0, give_q, gq_ref, rows).start()
+
+    give_k[...] = (k_acc[...] * factor[:, :1]).astype(jnp.bfloat16)
+    give(1, give_k, gk_ref, every).start()
+    give_v[...] = (v_acc[...] * coef[:, :1]).astype(jnp.bfloat16)
+    give(2, give_v, gv_ref, every).start()
+    gk_ref[core] = give_k[head_rows, :]
+    gv_ref[core] = give_v[head_rows, :]
     for w, buf in enumerate((gate_buf, up_buf, down_buf, ctx_buf)):
         arrived(buf.at[pl.ds(0, 7)], w_send.at[w])
     arrived(out_buf.at[pl.ds(0, 7), 0], w_send.at[4])
@@ -417,6 +475,8 @@
     arrived(g_ref.at[pl.ds(0, 31 * 64), :], g_send)
     arrived(att_ref.at[pl.ds(0, 31 * 64), :], tok_send)
     arrived(err_all.at[pl.ds(0, 31)], err_send)
+    for i, (staged, out) in enumerate(((give_q, gq_ref), (give_k, gk_ref), (give_v, gv_ref))):
+        give(i, staged, out, every).wait()
 
 
 def text_rows(q, k, v_aug, kept, o, z, m, e_ref):
@@ -436,20 +496,10 @@
     return (o * inv).astype(jnp.bfloat16), alpha * inv, inv
 
 
-def backward(coef_ref, q_ref, g_ref, att_ref, ei_ref, et_ref, si_ref, st_ref, k_ref, v_ref, kt_ref, vt_ref,
-             gq_ref, gk_ref, gv_ref, k_acc, v_acc):
-    step = pl.program_id(0)
-
-    @pl.when(step == 0)
-    def _():
-        k_acc[...] = jnp.zeros_like(k_acc)
-        v_acc[...] = jnp.zeros_like(v_acc)
-
-    coef = coef_ref[0]
-    g = g_ref[...].astype(jnp.float32)
-    prod = g * att_ref[...].astype(jnp.float32)
-    v_aug, vt_aug = with_ones(v_ref[...]), with_ones(vt_ref[...])
-    q_t = q_ref[...].T
+def backward_rows(q, g, att, ei_ref, et_ref, si, st, k, v_aug, kt, vt_aug, k_acc, v_acc):
+    g = g.astype(jnp.float32)
+    prod = g * att.astype(jnp.float32)
+    q_t = q.T
     lane = lax.broadcasted_iota(jnp.int32, (1, LANES), 1)
     grads = []
     for j in range(2):
@@ -461,57 +511,33 @@
             gs = (gj * scale).astype(jnp.bfloat16)
             d = -delta * scale
             hi = d.astype(jnp.bfloat16)
-            lo = (d - hi.astype(jnp.float32)).astype(jnp.bfloat16)
-            extra = jnp.where(lane == 0, hi, jnp.where(lane == 1, lo, jnp.zeros_like(hi)))
+            low = (d - hi.astype(jnp.float32)).astype(jnp.bfloat16)
+            extra = jnp.where(lane == 0, hi, jnp.where(lane == 1, low, jnp.zeros_like(hi)))
             return gs, jnp.concatenate([gs, extra], axis=1)
 
-        gi, lhs_i = scaled(si_ref[:, j * HEAD:j * HEAD + 1])
-        _, lhs_t = scaled(st_ref[:, j * HEAD:j * HEAD + 1])
+        gi, lhs_i = scaled(si[:, j * HEAD:j * HEAD + 1])
+        _, lhs_t = scaled(st[:, j * HEAD:j * HEAD + 1])
         ei = ei_ref[j]
         ds = (ei.astype(jnp.float32) * dot(lhs_i, v_aug, NT)).astype(jnp.bfloat16)
         ds_t = (et_ref[j].astype(jnp.float32) * dot(lhs_t, vt_aug, NT)).astype(jnp.bfloat16)
-        grads.append(dot(ds, k_ref[...]) + dot(ds_t, kt_ref[...]))
+        grads.append(dot(ds, k) + dot(ds_t, kt))
         rows = slice(j * HEAD, (j + 1) * HEAD)
         k_acc[rows, :] += dot(q_t[rows, :], ds)
         v_acc[rows, :] += dot(gi.T[rows, :], ei)
-    factor = coef * (1.0 / math.sqrt(HEAD))
-    gq_ref[...] = (by_head(grads[0], grads[1]) * factor).T.astype(jnp.bfloat16)
-
-    @pl.when(step == pl.num_programs(0) - 1)
-    def _():
-        gk_ref[...] = (k_acc[...] * factor).astype(jnp.bfloat16)
-        gv_ref[...] = (v_acc[...] * coef).astype(jnp.bfloat16)
-
-
-def block(shape, index_map):
-    return pl.BlockSpec(shape, index_map)
-
-
-def whole(*shape):
-    return pl.BlockSpec(shape, lambda i: (0,) * len(shape))
-
-
-def rows_of(width):
-    return pl.BlockSpec((ROWS, width), lambda i: (i, 0))
-
-
-def params():
-    return pltpu.CompilerParams(vmem_limit_bytes=48 * 1024 * 1024)
-
-
-def call_forward(lengths, prompt, gain_in, gain_out, target, gate, up, down, ctx, out, q, k, v):
+    return by_head(grads[0], grads[1])
+
+
+def call_window(lengths, scalars, prompt, gain_in, gain_out, target, gate, up, down, ctx, out, q, k, v):
     bf16, f32 = jnp.bfloat16, jnp.float32
     anywhere, vmem = pl.BlockSpec(memory_space=pl.ANY), pl.BlockSpec(memory_space=pltpu.VMEM)
     shape = jax.ShapeDtypeStruct
     dma, buf = pltpu.SemaphoreType.DMA, pltpu.VMEM
-    rows_bf16, rows_f32 = shape((SEQ, LANES), bf16), shape((SEQ, LANES), f32)
-    text = shape((PROMPT, LANES), bf16)
+    grads = shape((2, HEAD, SEQ), bf16)
     return pl.pallas_call(
-        forward,
-        in_specs=[vmem] * 5 + [anywhere] * 8,
-        out_specs=[vmem] * 5 + [anywhere] + [vmem] * 6,
-        out_shape=[rows_bf16] * 3 + [text] * 2 + [shape((2, SEQ, SEQ), bf16), shape((2, SEQ, PROMPT), bf16)]
-        + [rows_f32] * 2 + [rows_bf16] * 2 + [shape((8, LANES), f32)],
+        window,
+        in_specs=[vmem] * 6 + [anywhere] * 8,
+        out_specs=[vmem] * 4 + [anywhere],
+        out_shape=[shape((1, LANES), f32)] + [grads] * 3 + [shape((2, SEQ, SEQ), bf16)],
         scratch_shapes=[
             buf((8, 512, 256), bf16), buf((8, 512, 256), bf16), buf((8, 256, 512), bf16), buf((8, 512, 128), bf16),
             buf((8, 2, 128, CH), bf16),
@@ -521,58 +547,26 @@
             buf((8, PROMPT, 512), bf16), buf((2, PROMPT, LANES), bf16), buf((2, 2, ROWS, SEQ), bf16),
             buf((SEQ, LANES), f32), buf((SEQ, LANES), f32), buf((SEQ, LANES), f32),
             buf((LANES, 2048), bf16), buf((LANES, CH), f32), buf((LANES, 2048), bf16), buf((32, 8, LANES), f32),
+            buf((SEQ, LANES), bf16), buf((SEQ, LANES), bf16), buf((SEQ, LANES), bf16), buf((PROMPT, LANES), bf16),
+            buf((PROMPT, LANES), bf16), buf((2, SEQ, PROMPT), bf16), buf((SEQ, LANES), f32), buf((SEQ, LANES), f32),
+            buf((SEQ, LANES), bf16), buf((SEQ, LANES), bf16), buf((LANES, SEQ), f32), buf((LANES, SEQ), f32),
+            buf((LANES, SEQ), bf16), buf((LANES, SEQ), bf16), buf((LANES, SEQ), bf16),
             dma((5,)), dma((5,)), dma((5, 9)), dma((3,)), dma((3,)), dma((3,)), dma((2,)), dma((16,)), dma((16,)),
-        ] + [dma] * 8,
+            dma((3,)), dma((3,)), dma((8,)),
+        ] + [dma] * 7,
         compiler_params=pltpu.CompilerParams(collective_id=0, has_side_effects=True, vmem_limit_bytes=60 * 1024 * 1024),
-        name="forward",
-    )(lengths, prompt, gain_in, gain_out, target, gate, up, down, ctx, out, q, k, v)
-
-
-def call_backward(coef, q, g, att, ei, et, si, st, k, v, kt, vt):
-    out = lambda: jax.ShapeDtypeStruct((LANES, SEQ), jnp.bfloat16)
-    return pl.pallas_call(
-        backward,
-        grid=(SEQ // ROWS,),
-        in_specs=[pl.BlockSpec(memory_space=pltpu.SMEM), rows_of(LANES), rows_of(LANES), rows_of(LANES),
-                  pl.BlockSpec((2, ROWS, SEQ), lambda i: (0, i, 0)), pl.BlockSpec((2, ROWS, PROMPT), lambda i: (0, i, 0)),
-                  rows_of(LANES), rows_of(LANES), whole(SEQ, LANES), whole(SEQ, LANES),
-                  whole(PROMPT, LANES), whole(PROMPT, LANES)],
-        out_specs=[pl.BlockSpec((LANES, ROWS), lambda i: (0, i)), whole(LANES, SEQ), whole(LANES, SEQ)],
-        out_shape=[out(), out(), out()],
-        scratch_shapes=[pltpu.VMEM((LANES, SEQ), jnp.float32), pltpu.VMEM((LANES, SEQ), jnp.float32)],
-        compiler_params=params(),
-        name="backward",
-    )(coef, q, g, att, ei, et, si, st, k, v, kt, vt)
-
-
-def swap(values, pairs):
-    return lax.ppermute(values, "seq", pairs)
+        name="window",
+    )(lengths, scalars, prompt, gain_in, gain_out, target, gate, up, down, ctx, out, q, k, v)
 
 
 def on_device(prompt, lengths, timesteps, ref_errors, gain_ffn, w_in_gate, w_in_up, w_in_down, gain_final, w_context,
               image_q, image_k, image_v, w_out, target):
-    core = lax.axis_index("seq") % 2
-    pairs = [(i, i ^ 1) for i in range(32)]
-    q, k, v, kt, vt, ei, et, si, st, att, g, err = call_forward(
-        jnp.broadcast_to(lengths[:, None], (1, PROMPT)), prompt[0], gain_ffn[None], gain_final[None],
-        target[0].reshape(LANES, CH), w_in_gate, w_in_up, w_in_down, w_context, w_out.reshape(2, 128, CH),
-        image_q[0], image_k[0], image_v[0])
-    sums = err[:2, 0]
-    mean_errors = sums / (SEQ * CH)
-    error_gap = mean_errors[0] - ref_errors[0, 0] - (mean_errors[1] - ref_errors[0, 1])
-    sigma_t = noise_level(timesteps[0])
-    logit_value = dpo_beta * sigma_t * error_gap
-    pair_loss = jax.nn.softplus(logit_value)[None]
-    coefficient = sigma_t * jax.nn.sigmoid(logit_value)
-    coef = jnp.where(core == 0, coefficient, -coefficient)[None]
-
-    grads = jnp.stack(call_backward(coef, q, g, att, ei, et, si, st, k, v, kt, vt))
-    halves = grads.reshape(3, 2, HEAD, SEQ)
-    own = lax.dynamic_index_in_dim(halves, core, 1, keepdims=False)
-    theirs = swap(lax.dynamic_index_in_dim(halves, 1 - core, 1, keepdims=False), pairs)
-    outs = jnp.where(core == 0, jnp.stack([own, theirs], axis=1), jnp.stack([theirs, own], axis=1))
-    outs = jnp.transpose(outs, (0, 1, 3, 2))
-    return pair_loss, outs[0][None], outs[1][None], outs[2][None]
+    scalars = jnp.stack([noise_level(timesteps[0]), ref_errors[0, 0], ref_errors[0, 1]])
+    loss, grad_q, grad_k, grad_v, _ = call_window(
+        jnp.broadcast_to(lengths[:, None], (1, PROMPT)), jnp.broadcast_to(scalars[:, None], (3, LANES)),
+        prompt[0], gain_ffn[None], gain_final[None], target[0].reshape(LANES, CH),
+        w_in_gate, w_in_up, w_in_down, w_context, w_out.reshape(2, 128, CH), image_q[0], image_k[0], image_v[0])
+    return (loss[0, :1],) + tuple(jnp.transpose(grads, (0, 2, 1))[None] for grads in (grad_q, grad_k, grad_v))
 
 
 def solution(mesh):

time: 219 us -> 210 us (0.959); the launches traced: 215 us -> 209 us
  local copies, waits for them, and re-layouts: 10.6 us -> 8.17 us
  between operations: 5.98 us -> 3.73 us
    unnamed x18 -> x3, local copies, waits for them, and re-layouts: 8.1 us -> 5.64 us
    pallas_call x2 -> x1, Pallas kernels: 195 us -> 196 us  [call_window(): pl.pallas_call(window, in_specs=[vmem] * 6 + [anywhere] * 8, out_specs=[v...]
  transfers between devices with their start and end apart: 1 -> 0, of which waited for: 1 -> 0; matrix products, arithmetic and copies ran while one was open for 0% -> 0% of each run, Pallas kernels for 0% -> 0%
where the time goes in v4:
time: 210 us; the launch traced here: 209 us
  Pallas kernels  196 us (93%)
  local copies, waits for them, and re-layouts  8.17 us (4%)
  between operations  3.73 us (2%)
    pallas_call x1, Pallas kernels, call_window(): pl.pallas_call(window, in_specs=[vmem] * 6 + [anywhere] * 8, out_specs=[v...  196 us
    unnamed x3, local copies, waits for them, and re-layouts  5.64 us

profile of v4, /device:TPU:33, one launch (start us, length us, event | category | flops | bytes accessed | tf_op | source)
XLA Modules:
  0.0 209.5 jit_solution(3112351873800019895)
XLA Ops:
  2.0 0.6 broadcast_in_dim.30.len_ref
  2.5 1.3 fusion
  3.8 1.4 pad_maximum_fusion
  5.2 0.7 broadcast_in_dim.31.scalar_ref
  5.9 196.2 %window.1 = (f32[1,128]{1,0:T(1,128)}, bf16[2,64,2048]{2,1,0:T(8,128)(2,1)}, bf16[2,64,2048]{2,1,0:T(8,128)(2,1)}, bf16[2,64,2048]{2,1,0:T(8,128)(2,1)}, bf16[2,2048,2048]{2,1,0:T(8,128)(2,1)}) custom-call(s32[1,256]{1,0:T(1,128)} %broadcast_in_dim.30.len_ref, f32[3,128]{1,0:T(4,128)} %broadcast_in_dim.31.scalar_ref, bf16[256,4096]{1,0:T(8,128)(2,1)} %bitcast.23, ...), custom_call_target="tpu_custom_call" | custom-call | tf_op jit(solution)/shard_map/window/pallas_call | solution.py:536
  202.7 1.9 copy.26
  204.6 1.9 copy.27
  206.5 1.9 copy.28

commit v5 on v4

--- a/solution.py
+++ b/solution.py
@@ -82,7 +82,7 @@
 
 
 def window(
-    len_ref, scalar_ref, prompt_ref, gain_in_ref, gain_out_ref, target_ref, gate_in, up_in, down_in, ctx_in, out_in, q_in, k_in, v_in,
+    len_ref, step_ref, error_ref, prompt_ref, gain_in_ref, gain_out_ref, target_ref, gate_in, up_in, down_in, ctx_in, out_in, q_in, k_in, v_in,
     loss_ref, gq_ref, gk_ref, gv_ref, ei_ref,
     gate_buf, up_buf, down_buf, ctx_buf, out_buf, normed, gate_acc, up_acc, part, sib, half, from_x, sum_x, from_z, state,
     ctx_pair, e_tile, o_all, z_all, m_all, tok, resid, grad, err_all,
@@ -173,10 +173,12 @@
         return pl.ds(pl.multiple_of(lax.rem(to, 2) * 64, 64), 64)
 
     images = ((q_in, q_ref), (k_in, k_ref), (v_in, v_ref))
-    for i, (src, dst) in enumerate(images):
+
+    def send_image(i):
+        src, dst = images[i]
 
         @pl.loop(0, 8)
-        def _(j, i=i, src=src, dst=dst):
+        def _(j):
             for dz in ALTERNATE:
                 to = lax.rem(zh + dz, 4) * 8 + lax.rem(low + j, 8)
 
@@ -202,12 +204,14 @@
 
     for w in early:
         forward_near(w)
-    forward_partner(0)
-    forward_partner(1)
-
-    for i, (src, dst) in enumerate(images):
-        arrived(dst.at[pl.ds(0, 31 * 64), :], qkv_recv.at[i])
-        arrived(dst.at[pl.ds(0, 64), :], qkv_local.at[i])
+    for i in range(3):
+        send_image(i)
+        forward_partner(i)
+
+    def images_ready():
+        for i, (_, dst) in enumerate(images):
+            arrived(dst.at[pl.ds(0, 31 * 64), :], qkv_recv.at[i])
+            arrived(dst.at[pl.ds(0, 64), :], qkv_local.at[i])
 
     blocks = SEQ // ROWS
 
@@ -227,12 +231,6 @@
             o_all[rows, :], z_all[rows, :], m_all[rows, :] = o, z, m
             out_copy(b).start()
 
-    image_blocks(0, 4)
-    forward_partner(2)
-    for w in late:
-        send_own(w)
-    image_blocks(4, 8)
-
     weight_ready(0)
     weight_ready(1)
     gate_acc[...] = jnp.zeros_like(gate_acc)
@@ -255,13 +253,13 @@
 
     to_other = remote(part.at[pl.ds((1 - core) * 4, 4)], sib, stage_send.at[0], stage_recv.at[0], other, pair)
     to_other.start()
+    for w in late:
+        send_own(w)
 
     @pl.loop(0, 4)
     def _(i):
         part_block(core * 4 + i)
 
-    for w in late:
-        forward_near(w)
     to_other.wait()
     for i in range(4):
         half[i] = (part[core * 4 + i].astype(jnp.float32) + sib[i].astype(jnp.float32)).astype(jnp.bfloat16)
@@ -283,15 +281,23 @@
         for copy in copies:
             copy.wait()
 
+    def during_x():
+        images_ready()
+        image_blocks(0, 2)
+        for w in late:
+            forward_near(w)
+        image_blocks(2, 4)
+
     round_of(0, lambda d, s, r: remote(
-        half.at[:, rows_x(lax.rem(x + d, 4)), :], from_x.at[d], s, r, seat_of(zh, lax.rem(x + d, 4)), pair))
+        half.at[:, rows_x(lax.rem(x + d, 4)), :], from_x.at[d], s, r, seat_of(zh, lax.rem(x + d, 4)), pair), during_x)
     for i in range(4):
         acc = half[i, rows_x(x), :].astype(jnp.float32)
         for d in (1, 2, 3):
             acc = acc + from_x[d, i].astype(jnp.float32)
         sum_x[i] = acc.astype(jnp.bfloat16)
     round_of(3, lambda d, s, r: remote(
-        sum_x.at[:, rows_z(lax.rem(zh + d, 4)), :], from_z.at[d], s, r, seat_of(lax.rem(zh + d, 4), x), pair))
+        sum_x.at[:, rows_z(lax.rem(zh + d, 4)), :], from_z.at[d], s, r, seat_of(lax.rem(zh + d, 4), x), pair),
+        lambda: image_blocks(4, 5))
     mine = rows_z(x * 4 + zh)
     for i in range(4):
         columns = pl.ds(pl.multiple_of(core * 2048 + i * 512, 512), 512)
@@ -301,11 +307,13 @@
         state[core * 4 + i, mine, :] = acc.astype(jnp.bfloat16)
     ours = pl.ds(core * 4, 4)
     round_of(6, lambda d, s, r: remote(
-        state.at[ours, mine, :], state.at[ours, mine, :], s, r, seat_of(lax.rem(zh + d, 4), x), pair))
+        state.at[ours, mine, :], state.at[ours, mine, :], s, r, seat_of(lax.rem(zh + d, 4), x), pair),
+        lambda: image_blocks(5, 6))
 
     def forward_late():
         for w in late:
             forward_partner(w)
+        image_blocks(6, 8)
 
     round_of(9, lambda d, s, r: remote(
         state.at[ours, rows_x(x), :], state.at[ours, rows_x(x), :], s, r, seat_of(zh, lax.rem(x + d, 4)), pair), forward_late)
@@ -335,7 +343,7 @@
     vt_ref[...] = by_head(pltpu.roll(first, HEAD, 1), second).astype(jnp.bfloat16)
 
     spot = tok.at[stream_rows(seat), lanes_of(seat)]
-    kept = lax.broadcasted_iota(jnp.int32, (1, PROMPT), 1) < len_ref[...]
+    kept = lax.broadcasted_iota(jnp.int32, (1, PROMPT), 1) < len_ref[0]
 
     @pl.loop(0, 2)
     def _(part_of):
@@ -421,10 +429,11 @@
 
     arrived(err_all.at[pl.ds(0, 31)], err_recv)
     mean_errors = jnp.sum(err_all[...], axis=0) * (1.0 / (SEQ * CH))
-    error_gap = (mean_errors[0:1] - scalar_ref[1:2]) - (mean_errors[1:2] - scalar_ref[2:3])
-    logit = dpo_beta * scalar_ref[0:1] * error_gap
+    error_gap = (mean_errors[0:1] - error_ref[:, 0:1]) - (mean_errors[1:2] - error_ref[:, 1:2])
+    sigma = noise_level(jnp.full((1, LANES), step_ref[0], jnp.int32))
+    logit = dpo_beta * sigma * error_gap
     loss_ref[...] = jnp.maximum(logit, 0.0) + jnp.log1p(jnp.exp(-jnp.abs(logit)))
-    coef = scalar_ref[0:1] / (1.0 + jnp.exp(-logit)) * (1 - 2 * core).astype(jnp.float32)
+    coef = sigma / (1.0 + jnp.exp(-logit)) * (1 - 2 * core).astype(jnp.float32)
     factor = coef * (1.0 / math.sqrt(HEAD))
     head_rows = pl.ds(pl.multiple_of(core * HEAD, HEAD), HEAD)
     other_rows = pl.ds(pl.multiple_of((1 - core) * HEAD, HEAD), HEAD)
@@ -527,7 +536,7 @@
     return by_head(grads[0], grads[1])
 
 
-def call_window(lengths, scalars, prompt, gain_in, gain_out, target, gate, up, down, ctx, out, q, k, v):
+def call_window(lengths, timesteps, ref_errors, prompt, gain_in, gain_out, target, gate, up, down, ctx, out, q, k, v):
     bf16, f32 = jnp.bfloat16, jnp.float32
     anywhere, vmem = pl.BlockSpec(memory_space=pl.ANY), pl.BlockSpec(memory_space=pltpu.VMEM)
     shape = jax.ShapeDtypeStruct
@@ -535,7 +544,7 @@
     grads = shape((2, HEAD, SEQ), bf16)
     return pl.pallas_call(
         window,
-        in_specs=[vmem] * 6 + [anywhere] * 8,
+        in_specs=[pl.BlockSpec(memory_space=pltpu.SMEM)] * 2 + [vmem] * 5 + [anywhere] * 8,
         out_specs=[vmem] * 4 + [anywhere],
         out_shape=[shape((1, LANES), f32)] + [grads] * 3 + [shape((2, SEQ, SEQ), bf16)],
         scratch_shapes=[
@@ -554,17 +563,15 @@
             dma((5,)), dma((5,)), dma((5, 9)), dma((3,)), dma((3,)), dma((3,)), dma((2,)), dma((16,)), dma((16,)),
             dma((3,)), dma((3,)), dma((8,)),
         ] + [dma] * 7,
-        compiler_params=pltpu.CompilerParams(collective_id=0, has_side_effects=True, vmem_limit_bytes=60 * 1024 * 1024),
+        compiler_params=pltpu.CompilerParams(collective_id=0, has_side_effects=True, vmem_limit_bytes=54 * 1024 * 1024),
         name="window",
-    )(lengths, scalars, prompt, gain_in, gain_out, target, gate, up, down, ctx, out, q, k, v)
+    )(lengths, timesteps, ref_errors, prompt, gain_in, gain_out, target, gate, up, down, ctx, out, q, k, v)
 
 
 def on_device(prompt, lengths, timesteps, ref_errors, gain_ffn, w_in_gate, w_in_up, w_in_down, gain_final, w_context,
               image_q, image_k, image_v, w_out, target):
-    scalars = jnp.stack([noise_level(timesteps[0]), ref_errors[0, 0], ref_errors[0, 1]])
     loss, grad_q, grad_k, grad_v, _ = call_window(
-        jnp.broadcast_to(lengths[:, None], (1, PROMPT)), jnp.broadcast_to(scalars[:, None], (3, LANES)),
-        prompt[0], gain_ffn[None], gain_final[None], target[0].reshape(LANES, CH),
+        lengths, timesteps, ref_errors, prompt[0], gain_ffn[None], gain_final[None], target[0].reshape(LANES, CH),
         w_in_gate, w_in_up, w_in_down, w_context, w_out.reshape(2, 128, CH), image_q[0], image_k[0], image_v[0])
     return (loss[0, :1],) + tuple(jnp.transpose(grads, (0, 2, 1))[None] for grads in (grad_q, grad_k, grad_v))
 

time: 210 us -> 188 us (0.90)
  Pallas kernels: 196 us -> 179 us
  local copies, waits for them, and re-layouts: 8.17 us -> 5.64 us
    pallas_call x1, Pallas kernels: 196 us -> 179 us  [call_window(): pl.pallas_call(window, in_specs=[pl.BlockSpec(memory_space=pltpu.SMEM)] *...]
where the time goes in v5:
time: 188 us
  Pallas kernels  179 us (95%)
  local copies, waits for them, and re-layouts  5.64 us (3%)
  between operations  3.67 us (2%)
    pallas_call x1, Pallas kernels, call_window(): pl.pallas_call(window, in_specs=[pl.BlockSpec(memory_space=pltpu.SMEM)] *...  179 us
    unnamed x3, local copies, waits for them, and re-layouts  5.64 us

profile of v5, /device:TPU:33, one launch (start us, length us, event | category | flops | bytes accessed | tf_op | source)
XLA Modules:
  0.0 188.1 jit_solution(139586759216144411)
XLA Ops:
  1.9 178.8 %window.1 = (f32[1,128]{1,0:T(1,128)}, bf16[2,64,2048]{2,1,0:T(8,128)(2,1)}, bf16[2,64,2048]{2,1,0:T(8,128)(2,1)}, bf16[2,64,2048]{2,1,0:T(8,128)(2,1)}, bf16[2,2048,2048]{2,1,0:T(8,128)(2,1)}) custom-call(s32[1]{0:T(128)S(6)} %copy.23.len_ref, s32[1]{0:T(128)S(6)} %copy.24.step_ref, f32[1,2]{1,0:T(1,128)} %error_ref.1, bf16[256,4096]{1,0:T(8,128)(2,1)} %bitcast.19, ...), custom_call_target="tpu_custom_call" | custom-call | tf_op jit(solution)/shard_map/window/pallas_call | solution.py:545
  181.3 1.9 %copy.26 = bf16[1,2,2048,64]{2,3,1,0:T(8,128)(2,1)} copy(bf16[1,2,2048,64]{2,3,1,0:T(8,128)(2,1)} %bitcast.26) | data formatting | bytes 1048576
  183.2 1.9 copy.27
  185.1 1.9 copy.28

commit v6 on v5

--- a/solution.py
+++ b/solution.py
@@ -247,12 +247,18 @@
     def part_block(f):
         part[f] = dot(hidden, down_buf[f]).astype(jnp.bfloat16)
 
-    @pl.loop(0, 4)
-    def _(i):
-        part_block((1 - core) * 4 + i)
-
-    to_other = remote(part.at[pl.ds((1 - core) * 4, 4)], sib, stage_send.at[0], stage_recv.at[0], other, pair)
-    to_other.start()
+    def two(c, start=0):
+        return pl.ds(start + 2 * c, 2)
+
+    def sems(c, stage):
+        return stage_send.at[16 * c + stage], stage_recv.at[16 * c + stage]
+
+    to_other = []
+    for c in range(2):
+        for i in range(2):
+            part_block((1 - core) * 4 + 2 * c + i)
+        to_other.append(remote(part.at[two(c, (1 - core) * 4)], sib.at[two(c)], *sems(c, 0), other, pair))
+        to_other[c].start()
     for w in late:
         send_own(w)
 
@@ -260,10 +266,6 @@
     def _(i):
         part_block(core * 4 + i)
 
-    to_other.wait()
-    for i in range(4):
-        half[i] = (part[core * 4 + i].astype(jnp.float32) + sib[i].astype(jnp.float32)).astype(jnp.bfloat16)
-
     def seat_of(zh_to, x_to):
         return (zh_to * 4 + x_to) * 2 + core
 
@@ -273,54 +275,81 @@
     def rows_z(at):
         return pl.ds(pl.multiple_of(at * 16, 16), 16)
 
-    def round_of(stage, make, between=lambda: None):
-        copies = [make(d, stage_send.at[stage + d], stage_recv.at[stage + d]) for d in (1, 3, 2)]
+    def begin(make):
+        copies = [make(d) for d in (1, 3, 2)]
         for copy in copies:
             copy.start()
-        between()
+        return copies
+
+    def finish(copies):
         for copy in copies:
             copy.wait()
 
-    def during_x():
-        images_ready()
-        image_blocks(0, 2)
-        for w in late:
-            forward_near(w)
-        image_blocks(2, 4)
-
-    round_of(0, lambda d, s, r: remote(
-        half.at[:, rows_x(lax.rem(x + d, 4)), :], from_x.at[d], s, r, seat_of(zh, lax.rem(x + d, 4)), pair), during_x)
-    for i in range(4):
-        acc = half[i, rows_x(x), :].astype(jnp.float32)
-        for d in (1, 2, 3):
-            acc = acc + from_x[d, i].astype(jnp.float32)
-        sum_x[i] = acc.astype(jnp.bfloat16)
-    round_of(3, lambda d, s, r: remote(
-        sum_x.at[:, rows_z(lax.rem(zh + d, 4)), :], from_z.at[d], s, r, seat_of(lax.rem(zh + d, 4), x), pair),
-        lambda: image_blocks(4, 5))
     mine = rows_z(x * 4 + zh)
-    for i in range(4):
-        columns = pl.ds(pl.multiple_of(core * 2048 + i * 512, 512), 512)
-        acc = prompt_ref[mine, columns].astype(jnp.float32) + sum_x[i, rows_z(zh), :].astype(jnp.float32)
-        for d in (1, 2, 3):
-            acc = acc + from_z[d, i].astype(jnp.float32)
-        state[core * 4 + i, mine, :] = acc.astype(jnp.bfloat16)
-    ours = pl.ds(core * 4, 4)
-    round_of(6, lambda d, s, r: remote(
-        state.at[ours, mine, :], state.at[ours, mine, :], s, r, seat_of(lax.rem(zh + d, 4), x), pair),
-        lambda: image_blocks(5, 6))
-
-    def forward_late():
-        for w in late:
-            forward_partner(w)
-        image_blocks(6, 8)
-
-    round_of(9, lambda d, s, r: remote(
-        state.at[ours, rows_x(x), :], state.at[ours, rows_x(x), :], s, r, seat_of(zh, lax.rem(x + d, 4)), pair), forward_late)
-    last = remote(state.at[ours], state.at[ours], stage_send.at[13], stage_recv.at[13], other, pair)
-    last.start()
+
+    def reduce_x(c):
+        to_other[c].wait()
+        for i in (2 * c, 2 * c + 1):
+            half[i] = (part[core * 4 + i].astype(jnp.float32) + sib[i].astype(jnp.float32)).astype(jnp.bfloat16)
+        return begin(lambda d: remote(
+            half.at[two(c), rows_x(lax.rem(x + d, 4)), :], from_x.at[d, two(c)], *sems(c, d), seat_of(zh, lax.rem(x + d, 4)), pair))
+
+    def reduce_z(c, copies):
+        finish(copies)
+        for i in (2 * c, 2 * c + 1):
+            acc = half[i, rows_x(x), :].astype(jnp.float32)
+            for d in (1, 2, 3):
+                acc = acc + from_x[d, i].astype(jnp.float32)
+            sum_x[i] = acc.astype(jnp.bfloat16)
+        return begin(lambda d: remote(
+            sum_x.at[two(c), rows_z(lax.rem(zh + d, 4)), :], from_z.at[d, two(c)], *sems(c, 3 + d),
+            seat_of(lax.rem(zh + d, 4), x), pair))
+
+    def gather_z(c, copies):
+        finish(copies)
+        for i in (2 * c, 2 * c + 1):
+            columns = pl.ds(pl.multiple_of(core * 2048 + i * 512, 512), 512)
+            acc = prompt_ref[mine, columns].astype(jnp.float32) + sum_x[i, rows_z(zh), :].astype(jnp.float32)
+            for d in (1, 2, 3):
+                acc = acc + from_z[d, i].astype(jnp.float32)
+            state[core * 4 + i, mine, :] = acc.astype(jnp.bfloat16)
+        spot = state.at[two(c, core * 4), mine, :]
+        return begin(lambda d: remote(spot, spot, *sems(c, 6 + d), seat_of(lax.rem(zh + d, 4), x), pair))
+
+    def gather_x(c, copies):
+        finish(copies)
+        spot = state.at[two(c, core * 4), rows_x(x), :]
+        return begin(lambda d: remote(spot, spot, *sems(c, 9 + d), seat_of(zh, lax.rem(x + d, 4)), pair))
+
+    def gather_core(c, copies):
+        finish(copies)
+        spot = state.at[two(c, core * 4)]
+        copy = remote(spot, spot, *sems(c, 13), other, pair)
+        copy.start()
+        return copy
+
+    first = reduce_x(0)
+    second = reduce_x(1)
+    first = reduce_z(0, first)
+    images_ready()
+    image_blocks(0, 2)
+    second = reduce_z(1, second)
+    first = gather_z(0, first)
+    for w in late:
+        forward_near(w)
+    image_blocks(2, 4)
+    second = gather_z(1, second)
+    first = gather_x(0, first)
+    image_blocks(4, 5)
+    second = gather_x(1, second)
+    for w in late:
+        forward_partner(w)
+    image_blocks(5, 8)
+    first = gather_core(0, first)
+    second = gather_core(1, second)
     weight_ready(3)
-    last.wait()
+    first.wait()
+    second.wait()
 
     total = jnp.zeros((PROMPT, 1), jnp.float32)
     for f in range(8):
@@ -534,6 +563,30 @@
         k_acc[rows, :] += dot(q_t[rows, :], ds)
         v_acc[rows, :] += dot(gi.T[rows, :], ei)
     return by_head(grads[0], grads[1])
+
+
+def copy_out(q_in, k_in, v_in, q_ref, k_ref, v_ref, sem):
+    copies = [
+        pltpu.make_async_copy(src.at[stream], dst.at[stream], sem.at[2 * i + stream])
+        for i, (src, dst) in enumerate(((q_in, q_ref), (k_in, k_ref), (v_in, v_ref)))
+        for stream in range(2)
+    ]
+    for copy in copies:
+        copy.start()
+    for copy in copies:
+        copy.wait()
+
+
+def call_copy_out(*grads):
+    anywhere = pl.BlockSpec(memory_space=pl.ANY)
+    return pl.pallas_call(
+        copy_out,
+        in_specs=[anywhere] * 3,
+        out_specs=[anywhere] * 3,
+        out_shape=[jax.ShapeDtypeStruct((2, HEAD, SEQ), jnp.bfloat16)] * 3,
+        scratch_shapes=[pltpu.SemaphoreType.DMA((6,))],
+        name="copy_out",
+    )(*grads)
 
 
 def call_window(lengths, timesteps, ref_errors, prompt, gain_in, gain_out, target, gate, up, down, ctx, out, q, k, v):
@@ -560,7 +613,7 @@
             buf((PROMPT, LANES), bf16), buf((2, SEQ, PROMPT), bf16), buf((SEQ, LANES), f32), buf((SEQ, LANES), f32),
             buf((SEQ, LANES), bf16), buf((SEQ, LANES), bf16), buf((LANES, SEQ), f32), buf((LANES, SEQ), f32),
             buf((LANES, SEQ), bf16), buf((LANES, SEQ), bf16), buf((LANES, SEQ), bf16),
-            dma((5,)), dma((5,)), dma((5, 9)), dma((3,)), dma((3,)), dma((3,)), dma((2,)), dma((16,)), dma((16,)),
+            dma((5,)), dma((5,)), dma((5, 9)), dma((3,)), dma((3,)), dma((3,)), dma((2,)), dma((32,)), dma((32,)),
             dma((3,)), dma((3,)), dma((8,)),
         ] + [dma] * 7,
         compiler_params=pltpu.CompilerParams(collective_id=0, has_side_effects=True, vmem_limit_bytes=54 * 1024 * 1024),
@@ -573,7 +626,7 @@
     loss, grad_q, grad_k, grad_v, _ = call_window(
         lengths, timesteps, ref_errors, prompt[0], gain_ffn[None], gain_final[None], target[0].reshape(LANES, CH),
         w_in_gate, w_in_up, w_in_down, w_context, w_out.reshape(2, 128, CH), image_q[0], image_k[0], image_v[0])
-    return (loss[0, :1],) + tuple(jnp.transpose(grads, (0, 2, 1))[None] for grads in (grad_q, grad_k, grad_v))
+    return (loss[0, :1],) + tuple(jnp.transpose(grads, (0, 2, 1))[None] for grads in call_copy_out(grad_q, grad_k, grad_v))
 
 
 def solution(mesh):

time: 188 us -> 222 us (1.18)
  Pallas kernels: 179 us -> 219 us
  local copies, waits for them, and re-layouts: 5.64 us -> 0 us
    pallas_call x0 -> x1, Pallas kernels: none -> 48.8 us  [call_copy_out(): pl.pallas_call(copy_out, in_specs=[anywhere] * 3, out_specs=[anywhere] *...]
    pallas_call x1, Pallas kernels: 179 us -> 170 us  [call_window(): pl.pallas_call(window, in_specs=[pl.BlockSpec(memory_space=pltpu.SMEM)] *...]
    unnamed x3 -> x0, local copies, waits for them, and re-layouts: 5.64 us -> none
where the time goes in v6:
time: 222 us
  Pallas kernels  219 us (99%)
  between operations  3.69 us (2%)
    pallas_call x1, Pallas kernels, call_window(): pl.pallas_call(window, in_specs=[pl.BlockSpec(memory_space=pltpu.SMEM)] *...  170 us
    pallas_call x1, Pallas kernels, call_copy_out(): pl.pallas_call(copy_out, in_specs=[anywhere] * 3, out_specs=[anywhere] *...  48.8 us

profile of v6, /device:TPU:33, one launch (start us, length us, event | category | flops | bytes accessed | tf_op | source)
XLA Modules:
  0.0 222.3 jit_solution(11507498539811461712)
XLA Ops:
  1.9 169.8 %window.1 = (f32[1,128]{1,0:T(1,128)}, bf16[2,64,2048]{2,1,0:T(8,128)(2,1)}, bf16[2,64,2048]{2,1,0:T(8,128)(2,1)}, bf16[2,64,2048]{2,1,0:T(8,128)(2,1)}, bf16[2,2048,2048]{2,1,0:T(8,128)(2,1)}) custom-call(s32[1]{0:T(128)S(6)} %copy.20.len_ref, s32[1]{0:T(128)S(6)} %copy.21.step_ref, f32[1,2]{1,0:T(1,128)} %error_ref.1, bf16[256,4096]{1,0:T(8,128)(2,1)} %bitcast.19, ...), custom_call_target="tpu_custom_call" | custom-call | tf_op jit(solution)/shard_map/window/pallas_call | solution.py:598
  171.8 48.8 %copy_out.1 = (bf16[2,64,2048]{2,1,0:T(8,128)(2,1)}, bf16[2,64,2048]{2,1,0:T(8,128)(2,1)}, bf16[2,64,2048]{2,1,0:T(8,128)(2,1)}) custom-call(bf16[2,64,2048]{2,1,0:T(8,128)(2,1)} %get-tuple-element.12.q_in, bf16[2,64,2048]{2,1,0:T(8,128)(2,1)} %get-tuple-element.13.k_in, bf16[2,64,2048]{2,1,0:T(8,128)(2,1)} %get-tuple-element.14.v_in), custom_call_target="tpu_custom_call" | custom-call | tf_op jit(solution)/shard_map/copy_out/pallas_call | solution.py:582

commit v7 on v6

--- a/solution.py
+++ b/solution.py
@@ -565,26 +565,17 @@
     return by_head(grads[0], grads[1])
 
 
-def copy_out(q_in, k_in, v_in, q_ref, k_ref, v_ref, sem):
-    copies = [
-        pltpu.make_async_copy(src.at[stream], dst.at[stream], sem.at[2 * i + stream])
-        for i, (src, dst) in enumerate(((q_in, q_ref), (k_in, k_ref), (v_in, v_ref)))
-        for stream in range(2)
-    ]
-    for copy in copies:
-        copy.start()
-    for copy in copies:
-        copy.wait()
+def copy_out(q_in, k_in, v_in, q_ref, k_ref, v_ref):
+    q_ref[...], k_ref[...], v_ref[...] = q_in[...], k_in[...], v_in[...]
 
 
 def call_copy_out(*grads):
-    anywhere = pl.BlockSpec(memory_space=pl.ANY)
+    vmem = pl.BlockSpec(memory_space=pltpu.VMEM)
     return pl.pallas_call(
         copy_out,
-        in_specs=[anywhere] * 3,
-        out_specs=[anywhere] * 3,
+        in_specs=[vmem] * 3,
+        out_specs=[vmem] * 3,
         out_shape=[jax.ShapeDtypeStruct((2, HEAD, SEQ), jnp.bfloat16)] * 3,
-        scratch_shapes=[pltpu.SemaphoreType.DMA((6,))],
         name="copy_out",
     )(*grads)
 

time: 222 us -> 176 us (0.79)
  Pallas kernels: 219 us -> 172 us
    pallas_call x1, Pallas kernels: 48.8 us -> 2.53 us  [call_copy_out(): pl.pallas_call(copy_out, in_specs=[vmem] * 3, out_specs=[vmem] * 3, out_s...]
where the time goes in v7:
time: 176 us
  Pallas kernels  172 us (98%)
  between operations  3.69 us (2%)
    pallas_call x1, Pallas kernels, call_window(): pl.pallas_call(window, in_specs=[pl.BlockSpec(memory_space=pltpu.SMEM)] *...  170 us

profile of v7, /device:TPU:33, one launch (start us, length us, event | category | flops | bytes accessed | tf_op | source)
XLA Modules:
  0.0 176.1 jit_solution(11500825569232949382)
XLA Ops:
  1.9 169.8 %window.1 = (f32[1,128]{1,0:T(1,128)}, bf16[2,64,2048]{2,1,0:T(8,128)(2,1)}, bf16[2,64,2048]{2,1,0:T(8,128)(2,1)}, bf16[2,64,2048]{2,1,0:T(8,128)(2,1)}, bf16[2,2048,2048]{2,1,0:T(8,128)(2,1)}) custom-call(s32[1]{0:T(128)S(6)} %copy.20.len_ref, s32[1]{0:T(128)S(6)} %copy.21.step_ref, f32[1,2]{1,0:T(1,128)} %error_ref.1, bf16[256,4096]{1,0:T(8,128)(2,1)} %bitcast.19, ...), custom_call_target="tpu_custom_call" | custom-call | tf_op jit(solution)/shard_map/window/pallas_call | solution.py:589
  171.8 2.5 %copy_out.1 = (bf16[2,64,2048]{2,1,0:T(8,128)(2,1)}, bf16[2,64,2048]{2,1,0:T(8,128)(2,1)}, bf16[2,64,2048]{2,1,0:T(8,128)(2,1)}) custom-call(bf16[2,64,2048]{2,1,0:T(8,128)(2,1)} %get-tuple-element.12.q_in, bf16[2,64,2048]{2,1,0:T(8,128)(2,1)} %get-tuple-element.13.k_in, bf16[2,64,2048]{2,1,0:T(8,128)(2,1)} %get-tuple-element.14.v_in), custom_call_target="tpu_custom_call" | custom-call | tf_op jit(solution)/shard_map/copy_out/pallas_call | solution.py:574

commit v8 on v7

--- a/solution.py
+++ b/solution.py
@@ -84,9 +84,9 @@
 def window(
     len_ref, step_ref, error_ref, prompt_ref, gain_in_ref, gain_out_ref, target_ref, gate_in, up_in, down_in, ctx_in, out_in, q_in, k_in, v_in,
     loss_ref, gq_ref, gk_ref, gv_ref, ei_ref,
-    gate_buf, up_buf, down_buf, ctx_buf, out_buf, normed, gate_acc, up_acc, part, sib, half, from_x, sum_x, from_z, state,
+    gate_buf, up_buf, down_buf, ctx_buf, out_buf, normed, gate_acc, up_acc, part, sib, from_x, sum_x, from_z, state,
     ctx_pair, e_tile, o_all, z_all, m_all, tok, resid, grad, err_all,
-    q_ref, k_ref, v_ref, kt_ref, vt_ref, et_ref, si_ref, st_ref, att_ref, g_ref, k_acc, v_acc, give_q, give_k, give_v,
+    q_ref, k_ref, v_aug, kt_ref, vt_ref, et_ref, si_ref, st_ref, att_ref, g_ref, k_acc, v_acc, give_q, give_k, give_v,
     w_local, w_send, w_recv, qkv_local, qkv_send, qkv_recv, e_sem, stage_send, stage_recv, swap_send, swap_recv, g_recv,
     tok_local, tok_send, tok_recv, g_local, g_send, err_send, err_recv,
 ):
@@ -98,6 +98,8 @@
     base, base_p = zl * 4, (1 - zl) * 4
     partner = base_p + y
 
+    v_aug[:, LANES:] = jnp.ones((SEQ, LANES), jnp.bfloat16)
+    v_ref = v_aug.at[:, pl.ds(0, LANES)]
     barrier = pltpu.get_barrier_semaphore()
 
     @pl.loop(1, 32)
@@ -227,7 +229,7 @@
                 out_copy(b - 2).wait()
 
             rows = pl.ds(pl.multiple_of(b * ROWS, ROWS), ROWS)
-            o, z, m = image_rows(q_ref[rows, :], k_ref[...], with_ones(v_ref[...]), e_tile.at[lax.rem(b, 2)])
+            o, z, m = image_rows(q_ref[rows, :], k_ref[...], v_aug[...], e_tile.at[lax.rem(b, 2)])
             o_all[rows, :], z_all[rows, :], m_all[rows, :] = o, z, m
             out_copy(b).start()
 
@@ -290,14 +292,14 @@
     def reduce_x(c):
         to_other[c].wait()
         for i in (2 * c, 2 * c + 1):
-            half[i] = (part[core * 4 + i].astype(jnp.float32) + sib[i].astype(jnp.float32)).astype(jnp.bfloat16)
+            sib[i] = (part[core * 4 + i].astype(jnp.float32) + sib[i].astype(jnp.float32)).astype(jnp.bfloat16)
         return begin(lambda d: remote(
-            half.at[two(c), rows_x(lax.rem(x + d, 4)), :], from_x.at[d, two(c)], *sems(c, d), seat_of(zh, lax.rem(x + d, 4)), pair))
+            sib.at[two(c), rows_x(lax.rem(x + d, 4)), :], from_x.at[d, two(c)], *sems(c, d), seat_of(zh, lax.rem(x + d, 4)), pair))
 
     def reduce_z(c, copies):
         finish(copies)
         for i in (2 * c, 2 * c + 1):
-            acc = half[i, rows_x(x), :].astype(jnp.float32)
+            acc = sib[i, rows_x(x), :].astype(jnp.float32)
             for d in (1, 2, 3):
                 acc = acc + from_x[d, i].astype(jnp.float32)
             sum_x[i] = acc.astype(jnp.bfloat16)
@@ -371,13 +373,17 @@
     kt_ref[...] = by_head(first, pltpu.roll(second, HEAD, 1)).astype(jnp.bfloat16)
     vt_ref[...] = by_head(pltpu.roll(first, HEAD, 1), second).astype(jnp.bfloat16)
 
+    def order(i):
+        r = lax.rem(i, 4)
+        return lax.rem(zh + lax.rem(1 + 2 * r + r // 2, 4), 4) * 2 + lax.rem(low // 4 + i // 4, 2)
+
     spot = tok.at[stream_rows(seat), lanes_of(seat)]
     kept = lax.broadcasted_iota(jnp.int32, (1, PROMPT), 1) < len_ref[0]
 
     @pl.loop(0, 2)
     def _(part_of):
         for dz in ALTERNATE:
-            b = lax.rem(zh + dz, 4) * 2 + part_of
+            b = lax.rem(zh + dz, 4) * 2 + lax.rem(low // 4 + part_of, 2)
             rows = pl.ds(pl.multiple_of(b * ROWS, ROWS), ROWS)
             att, scale_i, scale_t = text_rows(
                 q_ref[rows, :], kt_ref[...], with_ones(vt_ref[...]), kept, o_all[rows, :], z_all[rows, :], m_all[rows, :],
@@ -387,7 +393,7 @@
                 to = b * 4 + t
 
                 def start(to=to):
-                    remote(att_ref.at[token_rows(to), :], spot, tok_send, tok_recv, to, pair).start()
+                    remote(att_ref.at[token_rows(to), :], spot, tok_send, tok_recv.at[seat // 4], to, pair).start()
 
                 def keep(to=to):
                     pltpu.make_async_copy(att_ref.at[token_rows(to), :], spot, tok_local).start()
@@ -398,17 +404,24 @@
                     pl.when(to != seat)(start)
                     pl.when(to == seat)(keep)
 
+    def block_arrived(ref, sem, b):
+        @pl.when(b == seat // 4)
+        def _():
+            arrived(ref.at[pl.ds(0, 192), :], sem.at[b])
+
+        @pl.when(b != seat // 4)
+        def _():
+            arrived(ref.at[pl.ds(0, 256), :], sem.at[b])
+
+    resid[...] = -target_ref[...].astype(jnp.float32)
     share.wait()
     arrived(spot, tok_local)
-    arrived(att_ref.at[pl.ds(0, 31 * 64), :], tok_recv)
-
-    acc = -target_ref[...].astype(jnp.float32)
-    resid[...] = acc
 
     @pl.loop(0, 8)
-    def _(f):
-        columns = pl.ds(pl.multiple_of(f * 256, 256), 256)
-        resid[...] += dot(tok[:, columns], out_buf[f].reshape(256, CH))
+    def _(i):
+        b = order(i)
+        block_arrived(att_ref, tok_recv, b)
+        resid[...] += dot(tok[:, pl.ds(pl.multiple_of(b * 256, 256), 256)], out_buf[b].reshape(256, CH))
 
     halves = []
     for stream in range(2):
@@ -439,10 +452,6 @@
                 else:
                     pl.when(to != seat)(start)
                     pl.when(to == seat)(keep)
-
-    def order(i):
-        r = lax.rem(i, 4)
-        return lax.rem(zh + lax.rem(1 + 2 * r + r // 2, 4), 4) * 2 + lax.rem(low // 4 + i // 4, 2)
 
     def in_copy(i):
         slot = lax.rem(i, 2)
@@ -478,18 +487,11 @@
         b = order(i)
         rows = pl.ds(pl.multiple_of(b * ROWS, ROWS), ROWS)
 
-        @pl.when(b == seat // 4)
-        def _():
-            arrived(g_ref.at[pl.ds(0, 192), :], g_recv.at[b])
-
-        @pl.when(b != seat // 4)
-        def _():
-            arrived(g_ref.at[pl.ds(0, 256), :], g_recv.at[b])
-
+        block_arrived(g_ref, g_recv, b)
         in_copy(i).wait()
         grad_q = backward_rows(
             q_ref[rows, :], g_ref[rows, :], att_ref[rows, :], e_tile.at[lax.rem(i, 2)], et_ref.at[:, rows, :],
-            si_ref[rows, :], st_ref[rows, :], k_ref[...], with_ones(v_ref[...]), kt_ref[...], with_ones(vt_ref[...]), k_acc, v_acc)
+            si_ref[rows, :], st_ref[rows, :], k_ref[...], v_aug[...], kt_ref[...], with_ones(vt_ref[...]), k_acc, v_acc)
 
         @pl.when(i + 2 < blocks)
         def _():
@@ -556,8 +558,8 @@
         gi, lhs_i = scaled(si[:, j * HEAD:j * HEAD + 1])
         _, lhs_t = scaled(st[:, j * HEAD:j * HEAD + 1])
         ei = ei_ref[j]
-        ds = (ei.astype(jnp.float32) * dot(lhs_i, v_aug, NT)).astype(jnp.bfloat16)
-        ds_t = (et_ref[j].astype(jnp.float32) * dot(lhs_t, vt_aug, NT)).astype(jnp.bfloat16)
+        ds = ei * dot(lhs_i, v_aug, NT).astype(jnp.bfloat16)
+        ds_t = et_ref[j] * dot(lhs_t, vt_aug, NT).astype(jnp.bfloat16)
         grads.append(dot(ds, k) + dot(ds_t, kt))
         rows = slice(j * HEAD, (j + 1) * HEAD)
         k_acc[rows, :] += dot(q_t[rows, :], ds)
@@ -595,19 +597,19 @@
             buf((8, 512, 256), bf16), buf((8, 512, 256), bf16), buf((8, 256, 512), bf16), buf((8, 512, 128), bf16),
             buf((8, 2, 128, CH), bf16),
             buf((8, PROMPT, 512), bf16), buf((PROMPT, 256), f32), buf((PROMPT, 256), f32),
-            buf((8, PROMPT, 512), bf16), buf((4, PROMPT, 512), bf16), buf((4, PROMPT, 512), bf16),
+            buf((8, PROMPT, 512), bf16), buf((4, PROMPT, 512), bf16),
             buf((4, 4, 64, 512), bf16), buf((4, 64, 512), bf16), buf((4, 4, 16, 512), bf16),
             buf((8, PROMPT, 512), bf16), buf((2, PROMPT, LANES), bf16), buf((2, 2, ROWS, SEQ), bf16),
             buf((SEQ, LANES), f32), buf((SEQ, LANES), f32), buf((SEQ, LANES), f32),
             buf((LANES, 2048), bf16), buf((LANES, CH), f32), buf((LANES, 2048), bf16), buf((32, 8, LANES), f32),
-            buf((SEQ, LANES), bf16), buf((SEQ, LANES), bf16), buf((SEQ, LANES), bf16), buf((PROMPT, LANES), bf16),
+            buf((SEQ, LANES), bf16), buf((SEQ, LANES), bf16), buf((SEQ, 2 * LANES), bf16), buf((PROMPT, LANES), bf16),
             buf((PROMPT, LANES), bf16), buf((2, SEQ, PROMPT), bf16), buf((SEQ, LANES), f32), buf((SEQ, LANES), f32),
             buf((SEQ, LANES), bf16), buf((SEQ, LANES), bf16), buf((LANES, SEQ), f32), buf((LANES, SEQ), f32),
             buf((LANES, SEQ), bf16), buf((LANES, SEQ), bf16), buf((LANES, SEQ), bf16),
             dma((5,)), dma((5,)), dma((5, 9)), dma((3,)), dma((3,)), dma((3,)), dma((2,)), dma((32,)), dma((32,)),
-            dma((3,)), dma((3,)), dma((8,)),
-        ] + [dma] * 7,
-        compiler_params=pltpu.CompilerParams(collective_id=0, has_side_effects=True, vmem_limit_bytes=54 * 1024 * 1024),
+            dma((3,)), dma((3,)), dma((8,)), dma, dma, dma((8,)),
+        ] + [dma] * 4,
+        compiler_params=pltpu.CompilerParams(collective_id=0, has_side_effects=True, vmem_limit_bytes=61 * 1024 * 1024),
         name="window",
     )(lengths, timesteps, ref_errors, prompt, gain_in, gain_out, target, gate, up, down, ctx, out, q, k, v)
 

time: 176 us -> 175 us (level)
  no operation moved by 1% of the time
where the time goes in v8:
time: 175 us
  Pallas kernels  171 us (98%)
  between operations  3.69 us (2%)
    pallas_call x1, Pallas kernels, call_window(): pl.pallas_call(window, in_specs=[pl.BlockSpec(memory_space=pltpu.SMEM)] *...  169 us

profile of v8, /device:TPU:33, one launch (start us, length us, event | category | flops | bytes accessed | tf_op | source)
XLA Modules:
  0.0 174.9 jit_solution(10443096108402965534)
XLA Ops:
  1.9 168.7 %window.1 = (f32[1,128]{1,0:T(1,128)}, bf16[2,64,2048]{2,1,0:T(8,128)(2,1)}, bf16[2,64,2048]{2,1,0:T(8,128)(2,1)}, bf16[2,64,2048]{2,1,0:T(8,128)(2,1)}, bf16[2,2048,2048]{2,1,0:T(8,128)(2,1)}) custom-call(s32[1]{0:T(128)S(6)} %copy.20.len_ref, s32[1]{0:T(128)S(6)} %copy.21.step_ref, f32[1,2]{1,0:T(1,128)} %error_ref.1, bf16[256,4096]{1,0:T(8,128)(2,1)} %bitcast.19, ...), custom_call_target="tpu_custom_call" | custom-call | tf_op jit(solution)/shard_map/window/pallas_call | solution.py:591
  170.6 2.5 %copy_out.1 = (bf16[2,64,2048]{2,1,0:T(8,128)(2,1)}, bf16[2,64,2048]{2,1,0:T(8,128)(2,1)}, bf16[2,64,2048]{2,1,0:T(8,128)(2,1)}) custom-call(bf16[2,64,2048]{2,1,0:T(8,128)(2,1)} %get-tuple-element.12.q_in, bf16[2,64,2048]{2,1,0:T(8,128)(2,1)} %get-tuple-element.13.k_in, bf16[2,64,2048]{2,1,0:T(8,128)(2,1)} %get-tuple-element.14.v_in), custom_call_target="tpu_custom_call" | custom-call | tf_op jit(solution)/shard_map/copy_out/pallas_call | solution.py:576
